TPU v7x, 32 devices: a whole 2x2x4 slice. The times are simulated.
32 devices in a mesh: dp: 8 (over z, y), mp: 4 (over x, core).
Axes of the slice: x: 2, y: 2, z: 4, core: 2. Of those that a mesh axis runs over, the one named last changes fastest.
Arguments:
- tokens: bfloat16 [16384, 768], P('dp'), may hold values from -6 to 6
- ln1_gain: float32 [768], replicated, may hold values from 0.1 to 1.9
- ln1_bias: float32 [768], replicated, may hold values from -3 to 3
- w_qkv: bfloat16 [3, 768, 768], P(None, None, 'mp'), may hold values from -0.21875 to 0.21875
- qv_bias: float32 [2, 768], P(None, 'mp'), may hold values from -3 to 3
- w_out: bfloat16 [768, 768], P('mp'), may hold values from -0.875 to 0.875
- out_bias: float32 [768], replicated, may hold values from -3 to 3
- ln2_gain: float32 [768], replicated, may hold values from 0.1 to 1.9
- ln2_bias: float32 [768], replicated, may hold values from -3 to 3
- w_up: bfloat16 [768, 3072], P(None, 'mp'), may hold values from -0.21875 to 0.21875
- up_bias: float32 [3072], P('mp'), may hold values from -3 to 3
- w_down: bfloat16 [3072, 768], P('mp'), may hold values from -0.15625 to 0.15625
- down_bias: float32 [768], replicated, may hold values from -3 to 3
- images: bfloat16 [2048, 768], P('dp'), may hold values from -6 to 6
- image_group: int32 [2048], P('dp'), may hold values from 0 to 1
- pair_shard: int32 [1024, 1], P('dp'), may hold values from 0 to 7; in each aligned block of 128 rows (0 to 127, 128 to 255, ...) at most 32 rows name the same one
- pair_row: int32 [1024], P('dp'), may hold values from 0 to 255
Outputs:
- text_out: bfloat16 [16384, 768], P('dp')
- input_grad: bfloat16 [16384, 768], P('dp')
- caption_loss: float32 [1024], P('dp')
- ln1_gain_grad: float32 [768], replicated
- ln1_bias_grad: float32 [768], replicated
- w_qkv_grad: float32 [3, 768, 768], P(None, None, 'mp')
- qv_bias_grad: float32 [2, 768], P(None, 'mp')
- w_out_grad: float32 [768, 768], P('mp')
- out_bias_grad: float32 [768], replicated
- ln2_gain_grad: float32 [768], replicated
- ln2_bias_grad: float32 [768], replicated
- w_up_grad: float32 [768, 3072], P(None, 'mp')
- up_bias_grad: float32 [3072], P('mp')
- w_down_grad: float32 [3072, 768], P('mp')
- down_bias_grad: float32 [768], replicated
Inputs may be any that keep to these rules, and one draw needn't show every extreme that they name: `pair_shard`: among the 128 captions of one index of dp at most 32 name the same image shard.
All inputs are finite; a program needn't handle non-finite values.
Results may differ from a plain program's by a relative error of at most 0.023.
Values may be sent and summed in bfloat16 or wider, within the bound.
A program may use at most 192 MiB of HBM per device.

v0:
```python
import jax
import jax.numpy as jnp
from jax import lax
from jax.sharding import PartitionSpec as P

D = 768
HEAD_DIM = 64
SEQ = 16


def layer_norm(values, gain_vec, shift_vec):
    mean_val = jnp.mean(values, axis=-1, keepdims=True)
    centred = values - mean_val
    scaled = centred * lax.rsqrt(jnp.mean(centred * centred, axis=-1, keepdims=True) + 1e-05)
    return scaled * gain_vec + shift_vec


def unit_rows(values):
    return values * lax.rsqrt(jnp.sum(values * values, axis=-1, keepdims=True) + 1e-06)


def exact_gelu(values):
    return jax.nn.gelu(values, approximate=False)


def heads_attn(values):
    return lax.psum(values.astype(jnp.bfloat16), "mp").astype(jnp.float32)


def heads_mlp(values):
    return lax.psum(values.astype(jnp.bfloat16), "mp").astype(jnp.float32)


def heads_mlp_back(values):
    return lax.psum(values.astype(jnp.bfloat16), "mp").astype(jnp.float32)


def heads_attn_back(values):
    return lax.psum(values.astype(jnp.bfloat16), "mp").astype(jnp.float32)


def text_forward(inputs, params, reduce_attn, reduce_mlp):
    (
        ln1_gain,
        ln1_bias,
        w_qkv,
        qv_bias,
        w_out,
        out_bias,
        ln2_gain,
        ln2_bias,
        w_up,
        up_bias,
        w_down,
        down_bias,
    ) = params
    row_count = inputs.shape[0]
    captions = row_count // SEQ
    local_width = w_qkv.shape[2]
    local_heads = local_width // HEAD_DIM
    factor = HEAD_DIM ** (-0.5)
    norm_one, ln1_back = jax.vjp(layer_norm, inputs, ln1_gain, ln1_bias)
    norm_one_low = norm_one.astype(jnp.bfloat16)
    projected = jnp.einsum("rd,kde->kre", norm_one_low, w_qkv, preferred_element_type=jnp.float32)
    queries = (
        (projected[0] + qv_bias[0])
        .astype(jnp.bfloat16)
        .reshape(captions, SEQ, local_heads, HEAD_DIM)
    )
    keys_all = projected[1].astype(jnp.bfloat16).reshape(captions, SEQ, local_heads, HEAD_DIM)
    values_all = (
        (projected[2] + qv_bias[1])
        .astype(jnp.bfloat16)
        .reshape(captions, SEQ, local_heads, HEAD_DIM)
    )
    scores = (
        jnp.einsum("cshe,cthe->chst", queries, keys_all, preferred_element_type=jnp.float32)
        * factor
    )
    score_top = jnp.max(scores, axis=-1, keepdims=True)
    score_lse = score_top + jnp.log(jnp.sum(jnp.exp(scores - score_top), axis=-1, keepdims=True))
    probs_low = jnp.exp(scores - score_lse).astype(jnp.bfloat16)
    mixed = jnp.einsum("chst,cthe->cshe", probs_low, values_all, preferred_element_type=jnp.float32)
    mixed = mixed.reshape(row_count, local_width).astype(jnp.bfloat16)
    attn_full = reduce_attn(jnp.dot(mixed, w_out, preferred_element_type=jnp.float32))
    hidden = inputs + attn_full + out_bias
    norm_two, ln2_back = jax.vjp(layer_norm, hidden, ln2_gain, ln2_bias)
    norm_two_low = norm_two.astype(jnp.bfloat16)
    upper = jnp.dot(norm_two_low, w_up, preferred_element_type=jnp.float32) + up_bias
    activity, gelu_back = jax.vjp(exact_gelu, upper)
    activity_low = activity.astype(jnp.bfloat16)
    mlp_full = reduce_mlp(jnp.dot(activity_low, w_down, preferred_element_type=jnp.float32))
    result = hidden + mlp_full + down_bias
    saved = (
        ln1_back,
        norm_one_low,
        queries,
        keys_all,
        values_all,
        score_lse,
        probs_low,
        mixed,
        ln2_back,
        norm_two_low,
        gelu_back,
        activity_low,
    )
    return (result, saved)


def text_backward(saved, result_grad, params, reduce_mlp_back, reduce_attn_back):
    (
        ln1_back,
        norm_one_low,
        queries,
        keys_all,
        values_all,
        score_lse,
        probs_low,
        mixed,
        ln2_back,
        norm_two_low,
        gelu_back,
        activity_low,
    ) = saved
    w_qkv = params[2]
    w_out = params[4]
    w_up = params[8]
    w_down = params[10]
    row_count = result_grad.shape[0]
    captions = row_count // SEQ
    local_width = w_qkv.shape[2]
    local_heads = local_width // HEAD_DIM
    factor = HEAD_DIM ** (-0.5)
    down_bias_grad = jnp.sum(result_grad, axis=0)
    result_low = result_grad.astype(jnp.bfloat16)
    w_down_grad = jnp.einsum(
        "rf,rd->fd", activity_low, result_low, preferred_element_type=jnp.float32
    )
    activity_grad = jnp.einsum("rd,fd->rf", result_low, w_down, preferred_element_type=jnp.float32)
    (upper_grad,) = gelu_back(activity_grad)
    upper_low = upper_grad.astype(jnp.bfloat16)
    up_bias_grad = jnp.sum(upper_low.astype(jnp.float32), axis=0)
    w_up_grad = jnp.einsum("rd,rf->df", norm_two_low, upper_low, preferred_element_type=jnp.float32)
    norm_two_grad = reduce_mlp_back(
        jnp.einsum("rf,df->rd", upper_low, w_up, preferred_element_type=jnp.float32)
    )
    hidden_part, ln2_gain_grad, ln2_bias_grad = ln2_back(norm_two_grad)
    hidden_grad = result_grad + hidden_part
    out_bias_grad = jnp.sum(hidden_grad, axis=0)
    hidden_low = hidden_grad.astype(jnp.bfloat16)
    w_out_grad = jnp.einsum("re,rd->ed", mixed, hidden_low, preferred_element_type=jnp.float32)
    mixed_grad = jnp.einsum("rd,ed->re", hidden_low, w_out, preferred_element_type=jnp.float32)
    mixed_grad = mixed_grad.astype(jnp.bfloat16).reshape(captions, SEQ, local_heads, HEAD_DIM)
    scores_again = (
        jnp.einsum("cshe,cthe->chst", queries, keys_all, preferred_element_type=jnp.float32)
        * factor
    )
    probs_again = jnp.exp(scores_again - score_lse)
    value_grad = jnp.einsum(
        "chst,cshe->cthe", probs_low, mixed_grad, preferred_element_type=jnp.float32
    )
    probs_grad = jnp.einsum(
        "cshe,cthe->chst", mixed_grad, values_all, preferred_element_type=jnp.float32
    )
    score_grad = probs_again * (
        probs_grad - jnp.sum(probs_again * probs_grad, axis=-1, keepdims=True)
    )
    score_low = score_grad.astype(jnp.bfloat16)
    query_grad = (
        jnp.einsum("chst,cthe->cshe", score_low, keys_all, preferred_element_type=jnp.float32)
        * factor
    )
    key_grad = (
        jnp.einsum("chst,cshe->cthe", score_low, queries, preferred_element_type=jnp.float32)
        * factor
    )
    proj_grad = (
        jnp.stack([query_grad, key_grad, value_grad])
        .reshape(3, row_count, local_width)
        .astype(jnp.bfloat16)
    )
    bias_sums = jnp.sum(proj_grad.astype(jnp.float32), axis=1)
    qv_bias_grad = jnp.stack([bias_sums[0], bias_sums[2]])
    w_qkv_grad = jnp.einsum(
        "rd,kre->kde", norm_one_low, proj_grad, preferred_element_type=jnp.float32
    )
    norm_one_grad = reduce_attn_back(
        jnp.einsum("kre,kde->rd", proj_grad, w_qkv, preferred_element_type=jnp.float32)
    )
    input_part, ln1_gain_grad, ln1_bias_grad = ln1_back(norm_one_grad)
    input_grad = hidden_grad + input_part
    grads = (
        ln1_gain_grad,
        ln1_bias_grad,
        w_qkv_grad,
        qv_bias_grad,
        w_out_grad,
        out_bias_grad,
        ln2_gain_grad,
        ln2_bias_grad,
        w_up_grad,
        up_bias_grad,
        w_down_grad,
        down_bias_grad,
    )
    return (input_grad, grads)


def body(
    tokens,
    ln1_gain,
    ln1_bias,
    w_qkv,
    qv_bias,
    w_out,
    out_bias,
    ln2_gain,
    ln2_bias,
    w_up,
    up_bias,
    w_down,
    down_bias,
    images,
    image_group,
    pair_shard,
    pair_row,
):
    row_count = tokens.shape[0]
    captions = row_count // SEQ
    inputs_all = tokens.astype(jnp.float32)
    params = (
        ln1_gain,
        ln1_bias,
        w_qkv,
        qv_bias,
        w_out,
        out_bias,
        ln2_gain,
        ln2_bias,
        w_up,
        up_bias,
        w_down,
        down_bias,
    )
    result, saved = text_forward(inputs_all, params, heads_attn, heads_mlp)
    own_caps = result.shape[0] // SEQ
    pooled = jnp.mean(result.reshape(own_caps, SEQ, D), axis=1)
    text_unit, unit_back = jax.vjp(unit_rows, pooled)
    text_part = text_unit.astype(jnp.bfloat16)
    shards = lax.axis_size("dp")
    slot_size = max(2, 2 * captions // shards)
    source = pair_shard[:, 0]
    order = jnp.arange(captions, dtype=jnp.int32)
    earlier = (source[:, None] == source[None, :]) & (order[None, :] < order[:, None])
    rank_in = jnp.sum(earlier.astype(jnp.int32), axis=1)
    slot_id = source * slot_size + rank_in
    table = slot_id[:, None] == jnp.arange(shards * slot_size, dtype=jnp.int32)[None, :]
    request = jnp.sum(jnp.where(table, pair_row[:, None], 0), axis=0)
    asked = lax.all_to_all(
        request.reshape(shards, slot_size), "dp", split_axis=0, concat_axis=0, tiled=True
    )
    temps_local = jnp.where(image_group == 1, 64.0, 40.0).astype(jnp.bfloat16)
    sent_rows = images[asked]
    sent_temps = temps_local[asked]
    got_rows, got_temps = (
        lax.all_to_all(sent_rows, "dp", split_axis=0, concat_axis=0, tiled=True),
        lax.all_to_all(sent_temps, "dp", split_axis=0, concat_axis=0, tiled=True),
    )
    picker = table.astype(jnp.bfloat16)
    raw_image = jnp.dot(
        picker, got_rows.reshape(shards * slot_size, D), preferred_element_type=jnp.float32
    )
    temp_own = jnp.dot(
        picker, got_temps.reshape(shards * slot_size), preferred_element_type=jnp.float32
    )
    image_low = unit_rows(raw_image).astype(jnp.bfloat16)
    image_all, temp_gathered = (
        lax.all_gather(image_low, "dp", axis=0, tiled=True),
        lax.all_gather(temp_own.astype(jnp.bfloat16), "dp", axis=0, tiled=True),
    )
    temp_all = temp_gathered.astype(jnp.float32)
    total = image_all.shape[0]
    base = lax.axis_index("dp") * captions
    every = jnp.arange(total, dtype=jnp.int32)
    eye_row = (every[None, :] == (base + order)[:, None]).astype(jnp.float32)
    row_logits = (
        jnp.einsum("cd,jd->cj", text_part, image_all, preferred_element_type=jnp.float32)
        * temp_all[None, :]
    )
    row_top = jnp.max(row_logits, axis=1, keepdims=True)
    row_lse = row_top + jnp.log(jnp.sum(jnp.exp(row_logits - row_top), axis=1, keepdims=True))
    row_prob = jnp.exp(row_logits - row_lse)
    row_loss = row_lse[:, 0] - jnp.sum(row_logits * eye_row, axis=1)
    row_grad = ((row_prob - eye_row) * temp_all[None, :]).astype(jnp.bfloat16)
    text_grad = jnp.dot(row_grad, image_all, preferred_element_type=jnp.float32)
    text_all = lax.all_gather(text_part, "dp", axis=0, tiled=True)
    col_logits = (
        jnp.einsum("id,jd->ij", text_all, image_low, preferred_element_type=jnp.float32)
        * temp_own[None, :]
    )
    col_top = jnp.max(col_logits, axis=0, keepdims=True)
    col_lse = col_top + jnp.log(jnp.sum(jnp.exp(col_logits - col_top), axis=0, keepdims=True))
    eye_col = (every[:, None] == (base + order)[None, :]).astype(jnp.float32)
    col_prob = jnp.exp(col_logits - col_lse)
    col_loss = col_lse[0] - jnp.sum(col_logits * eye_col, axis=0)
    col_grad = ((col_prob - eye_col) * temp_own[None, :]).astype(jnp.bfloat16)
    spread_terms = jnp.dot(col_grad, image_low, preferred_element_type=jnp.float32)
    text_grad = text_grad + lax.psum_scatter(spread_terms, "dp", scatter_dimension=0, tiled=True)
    caption_loss = row_loss + col_loss
    (pooled_grad,) = unit_back(text_grad)
    result_grad = jnp.broadcast_to((pooled_grad / SEQ)[:, None, :], (own_caps, SEQ, D)).reshape(
        own_caps * SEQ, D
    )
    input_grad, grads = text_backward(saved, result_grad, params, heads_mlp_back, heads_attn_back)
    text_out = result.astype(jnp.bfloat16)
    input_grad_low = input_grad.astype(jnp.bfloat16)
    summed = lax.psum(
        (
            grads[0],
            grads[1],
            grads[2],
            grads[3],
            grads[4],
            grads[5],
            grads[6],
            grads[7],
            grads[8],
            grads[9],
            grads[10],
            grads[11],
        ),
        "dp",
    )
    return (
        text_out,
        input_grad_low,
        caption_loss,
        summed[0],
        summed[1],
        summed[2],
        summed[3],
        summed[4],
        summed[5],
        summed[6],
        summed[7],
        summed[8],
        summed[9],
        summed[10],
        summed[11],
    )


def solution(mesh):
    in_specs = (
        P("dp", None),
        P(),
        P(),
        P(None, None, "mp"),
        P(None, "mp"),
        P("mp", None),
        P(),
        P(),
        P(),
        P(None, "mp"),
        P("mp"),
        P("mp", None),
        P(),
        P("dp", None),
        P("dp"),
        P("dp", None),
        P("dp"),
    )
    out_specs = (
        P("dp", None),
        P("dp", None),
        P("dp"),
        P(),
        P(),
        P(None, None, "mp"),
        P(None, "mp"),
        P("mp", None),
        P(),
        P(),
        P(),
        P(None, "mp"),
        P("mp"),
        P("mp", None),
        P(),
    )
    return jax.shard_map(body, mesh=mesh, in_specs=in_specs, out_specs=out_specs, check_vma=False)
```

profile of v0, /device:TPU:0, one launch (start us, length us, event | category | flops | bytes accessed | tf_op | source)
XLA Modules:
  0.0 850.7 jit_solution(13457039335615946435)
XLA Ops:
  8.1 2.5 convert_reduce_fusion.2
  20.1 3.0 squeeze.5
  23.1 3.6 copy.108
  31.5 5.0 convert_element_type.124
  36.4 2.6 multiply_reduce_fusion.2
  43.9 3.0 squeeze.4
  46.9 3.5 copy.106
  53.7 2.7 fusion.34
  56.4 2.5 copy.114
  58.9 4.9 convert_element_type.128
  63.9 3.9 convolution_convert_fusion.2
  68.8 7.3 all-to-all-start
  76.2 62.9 %all-reduce.8.cloned.1.call-done = bf16[2048,768]{1,0:T(8,128)(2,1)} async-done(((bf16[2048,768]{1,0:T(8,128)(2,1)}), bf16[2048,768]{1,0:T(8,128)(2,1)}) %all-reduce.8.cloned.1.call-update) | async-done | bytes 3145744 | tf_op jit(solution)/shard_map/psum | solution.py:27
  139.1 4.1 fusion.23
  146.1 18.7 %multiply_convert_fusion = (bf16[2048,768]{1,0:T(8,128)(2,1)S(1)}, f32[2048,768]{1,0:T(8,128)}, f32[2048,768]{1,0:T(8,128)}) fusion(f32[768]{0:T(1024)S(1)} %copy-done.59, bf16[768,768]{1,0:T(8,128)(2,1)S(1)} %copy-done, f32[768]{0:T(1024)S(1)} %copy-done.60, f32[768]{0:T(1024)S(1)} %copy-done.48, f32[2048]{0:T(1024)S(1)} %fusion.59, ...), kind=kOutput, calls=%fused_computation.39 | convolution fusion | flops 2533883904 | bytes 23228416 | tf_op jit(solution)/shard_map/dot_general | solution.py:89
  166.5 3.9 convolution_convert_fusion.1
  172.6 17.3 %all_to_all.27 = bf16[8,32,768]{2,1,0:T(8,128)(2,1)S(1)} all-to-all(bf16[8,32,768]{2,1,0:T(8,128)(2,1)S(1)} %bitcast.86), channel_id=1, replica_groups=mesh['dp'=8,'mp'=4] {'dp'}, dimensions={0} | all-to-all | bytes 786432 | tf_op jit(solution)/shard_map/all_to_all | solution.py:267
  191.8 47.4 %all-reduce.10.cloned.1.call-done = bf16[2048,768]{1,0:T(8,128)(2,1)} async-done(((bf16[2048,768]{1,0:T(8,128)(2,1)}), bf16[2048,768]{1,0:T(8,128)(2,1)}) %all-reduce.10.cloned.1.call-update) | async-done | bytes 3145744 | tf_op jit(solution)/shard_map/psum | solution.py:31
  239.2 6.2 bitcast_reduce_fusion
  249.4 5.5 all-to-all-start.2
  255.0 6.3 all-to-all-done.2
  261.6 16.8 %all-gather = bf16[8,1,128]{2,1,0:T(2,128)(2,1)S(1)} all-gather(bf16[1,1,128]{2,1,0:T(2,128)(2,1)S(1)} %convert_bitcast_fusion), channel_id=1, replica_groups=mesh['dp'=8,'mp'=4] {'dp'}, dimensions={0}, use_global_device_ids=true | all-gather | bytes 2304 | tf_op jit(solution)/shard_map/all_gather | solution.py:280
  281.8 9.5 %all-gather.6.cloned.1.call-done = bf16[1024,768]{1,0:T(8,128)(2,1)} async-done(((bf16[128,768]{1,0:T(8,128)(2,1)}), bf16[1024,768]{1,0:T(8,128)(2,1)}) %all-gather.6.cloned.1.call-update) | async-done | bytes 1572880 | tf_op jit(solution)/shard_map/all_gather | solution.py:297
  296.4 72.4 %reduce-scatter.2.cloned.1.call-done = f32[128,768]{1,0:T(8,128)} async-done(((f32[1024,768]{1,0:T(8,128)}), f32[128,768]{1,0:T(8,128)}) %reduce-scatter.2.cloned.1.call-update) | async-done | bytes 393232 | tf_op jit(solution)/shard_map/reduce_scatter | solution.py:309
  371.5 8.4 convert_reduce_fusion.3
  381.6 4.0 convolution_convert_fusion
  385.7 8.5 %fusion.64 = f32[768,768]{1,0:T(8,128)} fusion(bf16[2048,768]{1,0:T(8,128)(2,1)} %copy-done.67, f32[768]{0:T(1024)S(1)} %copy-done.61, f32[768]{0:T(1024)S(1)} %copy-done.49, f32[2048]{0:T(1024)S(1)} %copy-done.45, bf16[2048,768]{1,0:T(8,128)(2,1)} %all-reduce.8.cloned.1.call-done, bf16[2048,768]{1,0:T(8,128)(2,1)} %param.17, ...), kind=kOutput, calls=%fused_computation.159 | convolution fusion | flops 2430074880 | bytes 11822080 | tf_op jit(solution)/shard_map/rd,rf->df/dot_general | solution.py:144
  394.2 59.0 %all-reduce.12.cloned.1.call-done = bf16[2048,768]{1,0:T(8,128)(2,1)} async-done(((bf16[2048,768]{1,0:T(8,128)(2,1)}), bf16[2048,768]{1,0:T(8,128)(2,1)}) %all-reduce.12.cloned.1.call-update) | async-done | bytes 3145744 | tf_op jit(solution)/shard_map/psum | solution.py:35
  453.2 6.7 fusion.15
  460.1 6.6 fusion.71
  475.2 5.0 reshape.241
  480.2 4.1 multiply_reduce_fusion.1
  489.8 2.5 copy.121
  492.3 4.9 stack.15
  499.6 3.9 copy.123
  503.6 4.9 stack.16
  510.7 2.5 copy.125
  513.2 4.1 stack.17
  518.6 6.0 bitcast_convert_fusion.1
  524.7 7.1 fusion.78
  534.3 3.6 fusion.31
  540.6 52.7 %all-reduce.14.cloned.1.call-done = bf16[2048,768]{1,0:T(8,128)(2,1)} async-done(((bf16[2048,768]{1,0:T(8,128)(2,1)}), bf16[2048,768]{1,0:T(8,128)(2,1)}) %all-reduce.14.cloned.1.call-update) | async-done | bytes 3145744 | tf_op jit(solution)/shard_map/psum | solution.py:39
  593.3 4.6 convert_reduce_fusion
  598.1 3.7 fusion.16
  601.8 6.8 add_convert_fusion
  608.5 40.2 %all-reduce = (f32[768]{0:T(1024)}, f32[768]{0:T(1024)}, f32[2,192]{1,0:T(2,128)}, f32[768]{0:T(1024)}, f32[768]{0:T(1024)}, /*index=5*/f32[768]{0:T(1024)}, f32[768]{0:T(1024)}, f32[768]{0:T(1024)}) all-reduce(f32[768]{0:T(1024)S(1)} %get-tuple-element.17, f32[768]{0:T(1024)S(1)} %get-tuple-element.20, ...), channel_id=1, replica_groups=mesh['dp'=8,'mp'=4] {'dp'}, use_global_device_ids=true, to_apply=%region_29.30 | all-reduce | flops 5760 | bytes 46080 | tf_op jit(solution)/shard_map/psum | solution.py:318
  648.7 186.6 %all-reduce.16.cloned.1.call-done = (f32[3,768,192]{1,2,0:T(8,128)}, f32[192,768]{1,0:T(8,128)}, f32[768,768]{1,0:T(8,128)}, f32[768,768]{1,0:T(8,128)}) async-done(((f32[3,768,192]{1,2,0:T(8,128)}, f32[192,768]{1,0:T(8,128)}, f32[768,768]{1,0:T(8,128)}, f32[768,768]{1,0:T(8,128)}), (f32[3,768,192]{1,2,0:T(8,128)}, f32[192,768]{1,0:T(8,128)}, f32[768,768]{1,0:T(8,128)}, ...) | async-done | bytes 7077904 | tf_op jit(solution)/shard_map/psum | solution.py:318
  835.3 2.9 copy.151
  (230 shorter events, 78.8 us)
Async XLA Ops:
  8.0 138.1 %copy-start = (bf16[768,768]{1,0:T(8,128)(2,1)S(1)}, bf16[768,768]{1,0:T(8,128)(2,1)}, u32[]{:S(2)}) copy-start(bf16[768,768]{1,0:T(8,128)(2,1)} %param.26) | copy-start | bytes 3538948
  8.0 4.7 copy-start.46
  8.0 4.7 copy-start.62
  8.1 131.1 %all-reduce.8.cloned.1.call-start = ((), (), s32[]{:S(2)}) async-start(), calls=%async_computation.4 | async-start | bytes 6291456 | tf_op jit(solution)/shard_map/psum | solution.py:27
  8.1 4.6 copy-start.58
  20.1 6.6 copy-start.53
  23.1 6.9 copy-start.23
  30.0 9.1 %copy-start.13 = (bf16[128,16,3,64]{3,1,2,0:T(8,128)(2,1)}, bf16[128,16,3,64]{3,1,2,0:T(8,128)(2,1)S(1)}, u32[]{:S(2)}) copy-start(bf16[128,16,3,64]{3,1,2,0:T(8,128)(2,1)S(1)} %copy.110) | copy-start | bytes 2359300
  42.0 11.7 %copy-start.19 = (f32[128,3,16]{2,1,0:T(4,128)}, f32[128,3,16]{2,1,0:T(4,128)S(1)}, u32[]{:S(2)}) copy-start(f32[128,3,16]{2,1,0:T(4,128)S(1)} %log_add_fusion) | copy-start | bytes 73732
  56.4 7.5 copy-start.33
  63.9 4.1 copy-start.55
  63.9 75.2 %copy-start.37 = (f32[768]{0:T(1024)S(1)}, f32[768]{0:T(1024)}, u32[]{:S(2)}) copy-start(f32[768]{0:T(1024)} %param.23) | copy-start | bytes 9220
  68.0 78.0 %copy-start.51 = (s32[128]{0:T(128)}, s32[128]{0:T(128)S(1)}, u32[]{:S(2)}) copy-start(s32[128]{0:T(128)S(1)} %fusion.61) | copy-start | bytes 1540
  68.8 101.7 %all-to-all-start = ((s32[8,1,32]{2,1,0:T(1,128)}), s32[8,1,32]{2,1,0:T(1,128)S(1)}, u32[]{:S(2)}, u32[]{:S(2)}) async-start(s32[8,1,32]{2,1,0:T(1,128)} %all_to_all.17), calls=%async_computation | async-start | bytes 8192 | tf_op jit(solution)/shard_map/all_to_all | solution.py:260
  76.1 163.1 %all-reduce.10.cloned.1.call-start = ((), (), s32[]{:S(2)}) async-start(), calls=%async_computation.5 | async-start | bytes 6291456 | tf_op jit(solution)/shard_map/psum | solution.py:31
  139.1 4.1 copy-start.2
  139.1 4.7 copy-start.8
  146.0 18.8 %copy-start.42 = (f32[2048]{0:T(1024)}, f32[2048]{0:T(1024)S(1)}, u32[]{:S(2)}) copy-start(f32[2048]{0:T(1024)S(1)} %multiply_reduce_fusion) | copy-start | bytes 24580
  146.1 18.7 %copy-start.44 = (f32[2048]{0:T(1024)}, f32[2048]{0:T(1024)S(1)}, u32[]{:S(2)}) copy-start(f32[2048]{0:T(1024)S(1)} %fusion.59) | copy-start | bytes 24580
  146.1 20.4 %copy-start.56 = (bf16[768,768]{1,0:T(8,128)(2,1)S(1)}, bf16[768,768]{1,0:T(8,128)(2,1)}, u32[]{:S(2)}) copy-start(bf16[768,768]{1,0:T(8,128)(2,1)} %param.28) | copy-start | bytes 3538948
  170.4 108.0 %all-gather.4.cloned.1.call-start = ((), (), s32[]{:S(2)}) async-start(), calls=%async_computation.6 | async-start | bytes 1769472 | tf_op jit(solution)/shard_map/all_gather | solution.py:279
  191.7 55.2 %copy-start.64 = (s32[256]{0:T(256)S(1)}, s32[256]{0:T(256)}, u32[]{:S(2)}) copy-start(s32[256]{0:T(256)} %param.31) | copy-start | bytes 3076
  191.7 69.7 %copy-start.52 = (s32[128]{0:T(128)S(1)}, s32[128]{0:T(128)}, u32[]{:S(2)}) copy-start(s32[128]{0:T(128)} %copy-done.51) | copy-start | bytes 1540
  191.7 99.6 %all-gather.6.cloned.1.call-start = ((), (), s32[]{:S(2)}) async-start(), calls=%async_computation.7 | async-start | bytes 1769472 | tf_op jit(solution)/shard_map/all_gather | solution.py:297
  245.4 46.0 %copy-start.22 = (bf16[128,768]{1,0:T(8,128)(2,1)S(1)}, bf16[128,768]{1,0:T(8,128)(2,1)}, u32[]{:S(2)}) copy-start(bf16[128,768]{1,0:T(8,128)(2,1)} %multiply_convert_fusion.6) | copy-start | bytes 589828
  249.4 11.9 %all-to-all-start.2 = ((bf16[8,1,32]{2,1,0:T(2,128)(2,1)}), bf16[8,1,32]{2,1,0:T(2,128)(2,1)S(1)}, u32[]{:S(2)}, u32[]{:S(2)}) async-start(bf16[8,1,32]{2,1,0:T(2,128)(2,1)} %all_to_all.23), calls=%async_computation.2 | async-start | bytes 8192 | tf_op jit(solution)/shard_map/all_to_all | solution.py:268
  254.9 113.9 %reduce-scatter.2.cloned.1.call-start = ((), (), s32[]{:S(2)}) async-start(), calls=%async_computation.8 | async-start | bytes 3538944 | tf_op jit(solution)/shard_map/reduce_scatter | solution.py:309
  294.1 77.0 %copy-start.54 = (f32[128]{0:T(128)S(1)}, f32[128]{0:T(128)}, u32[]{:S(2)}) copy-start(f32[128]{0:T(128)} %get-tuple-element.56) | copy-start | bytes 1540
  296.3 156.9 %all-reduce.12.cloned.1.call-start = ((), (), s32[]{:S(2)}) async-start(), calls=%async_computation.9 | async-start | bytes 6291456 | tf_op jit(solution)/shard_map/psum | solution.py:35
  371.5 8.4 copy-start.24
  381.6 4.1 copy-start.61
  385.6 207.8 %all-reduce.14.cloned.1.call-start = ((), (), s32[]{:S(2)}) async-start(), calls=%async_computation.10 | async-start | bytes 6291456 | tf_op jit(solution)/shard_map/psum | solution.py:39
  394.2 65.8 %copy-start.43 = (f32[2048]{0:T(1024)S(1)}, f32[2048]{0:T(1024)}, u32[]{:S(2)}) copy-start(f32[2048]{0:T(1024)} %copy-done.42) | copy-start | bytes 24580
  394.2 65.8 %copy-start.50 = (f32[768]{0:T(1024)S(1)}, f32[768]{0:T(1024)}, u32[]{:S(2)}) copy-start(f32[768]{0:T(1024)} %param.29) | copy-start | bytes 9220
  453.2 6.8 copy-start.3
  453.2 6.8 copy-start.9
  453.2 6.8 copy-start.17
  466.6 4.4 copy-start.34
  471.0 9.3 %copy-start.20 = (f32[128,3,16]{2,1,0:T(4,128)S(1)}, f32[128,3,16]{2,1,0:T(4,128)}, u32[]{:S(2)}) copy-start(f32[128,3,16]{2,1,0:T(4,128)} %copy-done.19) | copy-start | bytes 73732
  513.2 5.4 copy-start.25
  524.6 7.1 copy-start.18
  524.7 310.7 %all-reduce.16.cloned.1.call-start = ((), (), s32[]{:S(2)}) async-start(), calls=%async_computation.11 | async-start | bytes 14155776 | tf_op jit(solution)/shard_map/psum | solution.py:318
  524.7 7.1 copy-start.30
  538.0 60.0 %copy-start.41 = (f32[2048]{0:T(1024)S(1)}, f32[2048]{0:T(1024)}, u32[]{:S(2)}) copy-start(f32[2048]{0:T(1024)} %copy-done.40) | copy-start | bytes 24580
  593.3 4.7 copy-start.5
  593.3 4.7 copy-start.11
  835.3 4.9 copy-start.32
  835.3 6.3 copy-start.31
  (30 other events, 73.4 us)
Sparse Core Ops, SparseCore 0:
  67.9 71.1 all-reduce.7
  170.6 68.5 all-reduce.9
  385.7 67.4 all-reduce.11
  524.8 68.5 all-reduce.13
  598.8 236.5 all-reduce.15
Sparse Core Ops, SparseCore 1:
  191.8 42.4 all-gather.3
  246.9 44.4 all-gather.5
  296.4 72.3 reduce-scatter.1
where the time goes:
time: 856 us; the launch traced here: 851 us
  waiting for transfers between devices  497 us (58%)
  local copies, waits for them, and re-layouts  101 us (12%)
  matrix products  93.3 us (11%)
  blocking collectives  74.3 us (9%)
  other arithmetic  55.5 us (6%)
  between operations  16.8 us (2%)
  starting transfers between devices  13.1 us (2%)
    psum x1, waiting for transfers between devices, body(): lax.psum((grads[0], grads[1], grads[2], grads[3], grads[4], grads[5], gra...  187 us
    reduce_scatter x1, waiting for transfers between devices, body(): lax.psum_scatter(spread_terms, 'dp', scatter_dimension=0, tiled=True)  72.4 us
    psum x1, waiting for transfers between devices, heads_attn(): return lax.psum(values.astype(jnp.bfloat16), 'mp').astype(jnp.float32)  62.9 us
    psum x1, waiting for transfers between devices, heads_mlp_back(): return lax.psum(values.astype(jnp.bfloat16), 'mp').astype(jnp.float32)  59 us
    psum x1, waiting for transfers between devices, heads_attn_back(): return lax.psum(values.astype(jnp.bfloat16), 'mp').astype(jnp.float32)  52.7 us
    psum x1, waiting for transfers between devices, heads_mlp(): return lax.psum(values.astype(jnp.bfloat16), 'mp').astype(jnp.float32)  47.4 us
    psum x1, blocking collectives, body(): lax.psum((grads[0], grads[1], grads[2], grads[3], grads[4], grads[5], gra...  40.2 us
    unnamed x140, local copies, waits for them, and re-layouts  21.7 us
  transfers between devices with their start and end apart: 10, of which 8 were waited for; matrix products, arithmetic and copies ran while one was open for 10% of the time, Pallas kernels for 0%

commit v1 on v0

v1 whole, which is shorter than its diff:
```python
import functools

import jax
import jax.numpy as jnp
from jax import lax
from jax.experimental import pallas as pl
from jax.experimental.pallas import tpu as pltpu
from jax.sharding import PartitionSpec as P

D = 768
HEAD_DIM = 64
SEQ = 16
F32 = jnp.float32
BF16 = jnp.bfloat16
MESH = pl.DeviceIdType.MESH


def nn(a, b):
    return lax.dot_general(a, b, (((1,), (0,)), ((), ())), preferred_element_type=F32)


def nt(a, b):
    return lax.dot_general(a, b, (((1,), (1,)), ((), ())), preferred_element_type=F32)


def tn(a, b):
    return lax.dot_general(a, b, (((0,), (0,)), ((), ())), preferred_element_type=F32)


def flip(index, k):
    return index + k - 2 * k * lax.rem(lax.div(index, k), 2)


def powers(n):
    out = []
    k = 1
    while k < n:
        out.append(k)
        k *= 2
    return out


def remote(src, dst, ssem, rsem, dev):
    return pltpu.make_async_remote_copy(
        src_ref=src, dst_ref=dst, send_sem=ssem, recv_sem=rsem, device_id=dev, device_id_type=MESH
    )


def norm_parts(v):
    mean = jnp.mean(v, axis=-1, keepdims=True)
    cen = v - mean
    rstd = lax.rsqrt(jnp.mean(cen * cen, axis=-1, keepdims=True) + 1e-05)
    return cen * rstd, rstd


def gelu_and_slope(u):
    z = jnp.abs(u) * 0.7071067811865476
    t = 1.0 / (1.0 + 0.3275911 * z)
    ex = jnp.exp(-(z * z))
    poly = t * (
        0.127414796
        + t * (-0.142248368 + t * (0.7107068705 + t * (-0.7265760135 + t * 0.5307027145)))
    )
    tail = poly * ex
    phi_cum = jnp.where(u >= 0, 1.0 - tail, tail)
    return u * phi_cum, phi_cum + u * (ex * 0.3989422804014327)


def head_masks():
    lane = lax.broadcasted_iota(jnp.int32, (128, 128), 1)
    first = lane < HEAD_DIM
    return first


def two_heads(v, first):
    zero = jnp.zeros_like(v)
    return jnp.concatenate([jnp.where(first, v, zero), jnp.where(first, zero, v)], axis=0)


def seq_mask():
    r = lax.broadcasted_iota(jnp.int32, (128, 128), 0) // SEQ
    c = lax.broadcasted_iota(jnp.int32, (128, 128), 1) // SEQ
    return r == c


def block_probs(q, k2, same):
    s = nt(q, k2)
    out = []
    for h in range(2):
        sh = jnp.where(same, s[:, h * 128 : (h + 1) * 128], -1e30)
        e = jnp.exp(sh - jnp.max(sh, axis=-1, keepdims=True))
        out.append(e / jnp.sum(e, axis=-1, keepdims=True))
    return out


def fwd_kernel(
    n_dp,
    rows,
    x_hbm, wq_hbm, wo_hbm, wu_hbm, wd_hbm, bi_hbm, img_hbm, info_hbm, vec_ref,
    wq_out, wo_out, wu_out, wd_out, imgs, info, qkv_out, mix_out, hid_out, gp_out, s_out, text_out, pool_out,
    xv, wq, wo, wu, wd, bi, n1, qkv, mix, hid, n2, gp, act, acc, sv, pool,
    w_ss, w_rs, b_ss, b_rs, i_ss, i_rs, l_sem, o_sem,
):
    dp = lax.axis_index("dp")
    mp = lax.axis_index("mp")
    b = lax.rem(dp, 2)
    core = (dp, flip(mp, 1))
    xdev = (dp, flip(mp, 2))
    diag = (dp, flip(flip(mp, 1), 2))
    ydev = (flip(dp, 1), mp)
    dps = powers(n_dp)

    bar = pltpu.get_barrier_semaphore()
    greet = [core, xdev, diag] + [(flip(dp, k), mp) for k in dps]
    for dev in greet:
        pl.semaphore_signal(bar, inc=1, device_id=dev, device_id_type=MESH)

    local = [
        pltpu.make_async_copy(x_hbm.at[pl.ds(mp * rows, rows)], xv, l_sem.at[0]),
        pltpu.make_async_copy(wq_hbm, wq.at[0, :, 0], l_sem.at[1]),
        pltpu.make_async_copy(wo_hbm, wo.at[0, 0], l_sem.at[2]),
        pltpu.make_async_copy(wu_hbm, wu.at[0], l_sem.at[3]),
        pltpu.make_async_copy(wd_hbm, wd.at[0], l_sem.at[4]),
        pltpu.make_async_copy(bi_hbm, bi.at[0], l_sem.at[5]),
        pltpu.make_async_copy(img_hbm, imgs.at[0], l_sem.at[6]),
        pltpu.make_async_copy(info_hbm, info.at[0], l_sem.at[7]),
    ]
    for c in local:
        c.start()

    pl.semaphore_wait(bar, len(greet))

    q_rows = wq_hbm.shape[1]
    o_rows = wo_hbm.shape[0]
    u_rows = wu_hbm.shape[0]
    d_rows = wd_hbm.shape[0]

    def half(total, parts, part, which):
        size = total // 2 // parts
        return pl.ds(which * (total // 2) + part * size, size)

    def src_q(cut):
        return wq_hbm.at[:, cut]

    def src_o(cut):
        return wo_hbm.at[cut]

    def src_u(cut):
        return wu_hbm.at[cut]

    def src_d(cut):
        return wd_hbm.at[cut]

    def at_q(s, cut):
        return wq.at[s // 2, :, s % 2, cut]

    def at_o(s, cut):
        return wo.at[s // 2, s % 2, cut]

    def at_u(s, cut):
        return wu.at[s, cut]

    def at_d(s, cut):
        return wd.at[s, cut]

    table = []
    for total, parts, src, at in (
        (q_rows, 1, src_q, at_q),
        (o_rows, 1, src_o, at_o),
        (u_rows, 2, src_u, at_u),
        (d_rows, 2, src_d, at_d),
    ):
        whole = pl.ds(0, total)
        pieces = []
        for part in range(parts):
            pieces.append((half(total, parts, part, b), half(total, parts, part, 1 - b)))
        table.append((whole, pieces, src, at))

    sent = []
    number = [0]

    def go(src, dst, dev):
        i = number[0]
        number[0] += 1
        c = remote(src, dst, w_ss.at[i], w_rs.at[i], dev)
        c.start()
        sent.append(c)
        return c

    bias = [
        remote(bi_hbm, bi.at[s], b_ss.at[s - 1], b_rs.at[s - 1], dev)
        for s, dev in ((1, core), (2, xdev), (3, diag))
    ]
    for c in bias:
        c.start()

    step_x, step_core = [], []
    for whole, pieces, src, at in table:
        step_core.append(go(src(whole), at(1, whole), core))
        step_x.append([go(src(mine), at(2, mine), xdev) for mine, _ in pieces])

    i_half = img_hbm.shape[0] // 2
    own_cut = pl.ds(lax.rem(mp, 2) * i_half, i_half)
    img_copies = []

    def image_step(j):
        k = dps[j]
        dev = (flip(dp, k), mp)
        if j == 0:
            pair = [
                remote(img_hbm.at[own_cut], imgs.at[1, own_cut], i_ss.at[0], i_rs.at[0], dev),
                remote(info_hbm, info.at[1], i_ss.at[1], i_rs.at[1], dev),
            ]
        else:
            if j == 1:
                local[6].wait()
                local[7].wait()
            for c in img_copies[j - 1]:
                c.wait_recv()
            pair = [
                remote(imgs.at[0:k, own_cut], imgs.at[k : 2 * k, own_cut], i_ss.at[2 * j], i_rs.at[2 * j], dev),
                remote(info.at[0:k], info.at[k : 2 * k], i_ss.at[2 * j + 1], i_rs.at[2 * j + 1], dev),
            ]
        for c in pair:
            c.start()
        img_copies.append(pair)

    def image_last():
        if len(dps) == 1:
            local[6].wait()
            local[7].wait()
        for c in img_copies[len(dps) - 1]:
            c.wait_recv()
        n = 2 * len(dps)
        c = remote(imgs.at[1:n_dp, own_cut], imgs.at[1:n_dp, own_cut], i_ss.at[n], i_rs.at[n], core)
        c.start()
        img_copies.append([c])

    image_step(0)

    step_y = [[None] * len(t[1]) for t in table]
    step_f = [[None] * len(t[1]) for t in table]
    step_g = [[None] * len(t[1]) for t in table]

    def forward_x(w, part):
        _, pieces, _, at = table[w]
        mine = pieces[part][0]
        step_x[w][part].wait_recv()
        step_y[w][part] = go(at(2, mine), at(2, mine), ydev)
        step_f[w][part] = go(at(2, mine), at(3, mine), core)

    def forward_y(w, part):
        _, pieces, _, at = table[w]
        other = pieces[part][1]
        step_y[w][part].wait_recv()
        step_g[w][part] = go(at(2, other), at(3, other), core)

    def arrived(w):
        for part in range(len(table[w][1])):
            step_f[w][part].wait_recv()
            step_g[w][part].wait_recv()

    outs = []

    def put(src, dst):
        c = pltpu.make_async_copy(src, dst, o_sem.at[len(outs)])
        c.start()
        outs.append(c)

    g1, s1, ob = vec_ref[0:1], vec_ref[1:2], vec_ref[2:3]
    g2, s2, db = vec_ref[3:4], vec_ref[4:5], vec_ref[5:6]
    local[0].wait()
    step = 128

    def first_norm(i, carry):
        r = pl.ds(pl.multiple_of(i * step, step), step)
        xhat, _ = norm_parts(xv[r].astype(F32))
        n1[r] = (xhat * g1 + s1).astype(BF16)
        return carry

    lax.fori_loop(0, rows // step, first_norm, 0)
    if len(dps) > 1:
        image_step(1)

    first = head_masks()
    same = seq_mask()
    width = 2 * q_rows
    blocks = width // 128

    def project(p):
        qb = bi[2 * p, 1:2, :width] + bi[2 * p + 1, 2:3, :width]
        vb = bi[2 * p, 3:4, :width] + bi[2 * p + 1, 4:5, :width]
        for n in range(3):
            w = wq[p, n].reshape(width, D)
            r = nt(n1[...], w)
            if n == 0:
                r = (r + qb) * (HEAD_DIM**-0.5)
            if n == 2:
                r = r + vb
            qkv[p, n] = r.astype(BF16)

    def attend(p):
        def chunk(i, carry):
            r = pl.ds(pl.multiple_of(i * 128, 128), 128)
            for j in range(blocks):
                c = slice(j * 128, (j + 1) * 128)
                q, k, v = qkv[p, 0, r, c], qkv[p, 1, r, c], qkv[p, 2, r, c]
                pr = block_probs(q, two_heads(k, first), same)
                pb = jnp.concatenate([t.astype(BF16) for t in pr], axis=1)
                mix[p, r, c] = nn(pb, two_heads(v, first)).astype(BF16)
            return carry

        lax.fori_loop(0, rows // 128, chunk, 0)

    local[1].wait()
    local[5].wait()
    step_core[0].wait_recv()
    bias[0].wait_recv()
    project(0)
    attend(0)
    forward_x(0, 0)
    forward_x(1, 0)
    for j in range(2, len(dps)):
        image_step(j)
    forward_y(0, 0)
    forward_y(1, 0)
    bias[1].wait_recv()
    bias[2].wait_recv()
    arrived(0)
    put(wq, wq_out)
    project(1)
    forward_x(2, 0)
    attend(1)
    put(qkv, qkv_out)
    put(mix, mix_out)
    forward_x(2, 1)
    local[2].wait()
    step_core[1].wait_recv()
    arrived(1)
    put(wo, wo_out)

    w_out = [wo[p].reshape(width, D) for p in range(2)]

    def second_norm(i, carry):
        r = pl.ds(pl.multiple_of(i * 256, 256), 256)
        h = nn(mix[0, r], w_out[0]) + nn(mix[1, r], w_out[1])
        h = xv[r].astype(F32) + h + ob
        hid[r] = h
        xhat, _ = norm_parts(h)
        n2[r] = (xhat * g2 + s2).astype(BF16)
        return carry

    lax.fori_loop(0, rows // 256, second_norm, 0)
    put(hid, hid_out)

    caps = rows // SEQ
    pick = (
        lax.broadcasted_iota(jnp.int32, (caps, rows), 0) == lax.broadcasted_iota(jnp.int32, (caps, rows), 1) // SEQ
    ).astype(BF16)
    tile = 256

    def up(s):
        def one(j, carry):
            c = pl.ds(pl.multiple_of(j * tile, tile), tile)
            u = nn(n2[...], wu[s, :, c]) + bi[s, 0:1, c]
            a, slope = gelu_and_slope(u)
            a = a.astype(BF16)
            act[s, :, c] = a
            gp[s, :, c] = slope.astype(BF16)
            sv[s, :, c] = nn(pick, a).astype(BF16)
            return carry

        lax.fori_loop(0, D // tile, one, 0)

    def down(s):
        def one(j, carry):
            c = pl.ds(pl.multiple_of(j * tile, tile), tile)
            r = nn(act[s], wd[s, :, c])
            if s == 0:
                acc[:, c] = r
            else:
                acc[:, c] += r
            return carry

        lax.fori_loop(0, D // tile, one, 0)

    local[3].wait()
    up(0)
    forward_y(2, 0)
    forward_x(3, 0)
    step_core[2].wait_recv()
    up(1)
    forward_y(2, 1)
    forward_x(3, 1)
    local[4].wait()
    down(0)
    arrived(2)
    up(2)
    forward_y(3, 0)
    up(3)
    put(wu, wu_out)
    put(gp, gp_out)
    put(sv, s_out)
    step_core[3].wait_recv()
    down(1)
    forward_y(3, 1)
    image_last()
    arrived(3)
    put(wd, wd_out)
    down(2)
    down(3)

    def finish(i, carry):
        r = pl.ds(pl.multiple_of(i * step, step), step)
        res = hid[r] + acc[r] + db
        text = res.astype(BF16)
        n1[r] = text
        m = jnp.sum(res.reshape(step // SEQ, SEQ, D), axis=1) * (1.0 / SEQ)
        pool[pl.ds(pl.multiple_of(i * (step // SEQ), step // SEQ), step // SEQ)] = m
        return carry

    lax.fori_loop(0, rows // step, finish, 0)
    put(n1, text_out)
    put(pool, pool_out)

    for c in sent:
        c.wait_send()
    for c in bias:
        c.wait_send()
    for pair in img_copies:
        for c in pair:
            c.wait_send()
    img_copies[-1][0].wait_recv()
    for c in outs:
        c.wait()


def run_forward(n_dp, rows, tokens, wq_t, w_out, w_up, w_down, bi, images, info, vec):
    caps = rows // SEQ
    q_rows = wq_t.shape[1]
    width = 2 * q_rows
    sds = jax.ShapeDtypeStruct
    weights = [
        sds((2, 3, 2, q_rows, D), BF16),
        sds((2, 2) + w_out.shape, BF16),
        sds((4,) + w_up.shape, BF16),
        sds((4,) + w_down.shape, BF16),
    ]
    outs = weights + [
        sds((n_dp,) + images.shape, BF16),
        sds((n_dp,) + info.shape, info.dtype),
        sds((2, 3, rows, width), BF16),
        sds((2, rows, width), BF16),
        sds((rows, D), F32),
        sds((4, rows, D), BF16),
        sds((4, caps, D), BF16),
        sds((rows, D), BF16),
        sds((caps, D), F32),
    ]
    any_spec = pl.BlockSpec(memory_space=pl.ANY)
    vm = lambda s: pltpu.VMEM(s.shape, s.dtype)
    n_img = 2 * len(powers(n_dp)) + 1
    return pl.pallas_call(
        functools.partial(fwd_kernel, n_dp, rows),
        out_shape=outs,
        in_specs=[any_spec] * 8 + [pl.BlockSpec(memory_space=pltpu.VMEM)],
        out_specs=[any_spec] * len(outs),
        scratch_shapes=[
            pltpu.VMEM((rows, D), BF16),
            *[vm(s) for s in weights],
            pltpu.VMEM((4,) + bi.shape, F32),
            pltpu.VMEM((rows, D), BF16),
            pltpu.VMEM((2, 3, rows, width), BF16),
            pltpu.VMEM((2, rows, width), BF16),
            pltpu.VMEM((rows, D), F32),
            pltpu.VMEM((rows, D), BF16),
            pltpu.VMEM((4, rows, D), BF16),
            pltpu.VMEM((4, rows, D), BF16),
            pltpu.VMEM((rows, D), F32),
            pltpu.VMEM((4, caps, D), BF16),
            pltpu.VMEM((caps, D), F32),
            pltpu.SemaphoreType.DMA((28,)),
            pltpu.SemaphoreType.DMA((28,)),
            pltpu.SemaphoreType.DMA((3,)),
            pltpu.SemaphoreType.DMA((3,)),
            pltpu.SemaphoreType.DMA((n_img,)),
            pltpu.SemaphoreType.DMA((n_img,)),
            pltpu.SemaphoreType.DMA((8,)),
            pltpu.SemaphoreType.DMA((11,)),
        ],
        compiler_params=pltpu.CompilerParams(
            collective_id=0, has_side_effects=True, vmem_limit_bytes=60 * 2**20
        ),
        name="forward",
    )(tokens, wq_t, w_out, w_up, w_down, bi, images, info, vec)


def pair_kernel(
    n_dp,
    n_mp,
    pool_ref, image_ref, temp_ref,
    grad_ref, loss_ref,
    sums, part, ss, rs, l_ss, l_rs,
):
    dp = lax.axis_index("dp")
    mp = lax.axis_index("mp")
    caps = pool_ref.shape[0]
    total = image_ref.shape[0]
    near = [(dp, flip(mp, 1)), (dp, flip(mp, 2)), (dp, flip(flip(mp, 1), 2))]
    far = [(lax.rem(dp + k, n_dp), mp) for k in range(1, n_dp)]
    bar = pltpu.get_barrier_semaphore()
    for dev in near + far:
        pl.semaphore_signal(bar, inc=1, device_id=dev, device_id_type=MESH)

    pooled = pool_ref[...]
    inv = lax.rsqrt(jnp.sum(pooled * pooled, axis=-1, keepdims=True) + 1e-06)
    text = (pooled * inv).astype(BF16)
    temp = temp_ref[...]
    logits = nt(text, image_ref[...]) * temp
    e = jnp.exp(logits)
    row_sum = jnp.sum(e, axis=-1, keepdims=True)
    part[0] = jnp.sum(e, axis=0, keepdims=True)
    pl.semaphore_wait(bar, len(near) + len(far))

    sent = []
    for i, dev in enumerate(far):
        c = remote(part.at[0], sums.at[i], ss.at[i], rs.at[i], dev)
        c.start()
        sent.append(c)
    own = mp * caps
    base = dp * (caps * n_mp) + own
    eye = (
        lax.broadcasted_iota(jnp.int32, (caps, total), 1)
        == lax.broadcasted_iota(jnp.int32, (caps, total), 0) + base
    ).astype(F32)
    row_grad = ((e / row_sum - eye) * temp).astype(BF16)
    text_grad = nn(row_grad, image_ref[...])
    picked = jnp.sum(logits * eye, axis=-1, keepdims=True)
    for c in sent:
        c.wait_recv()
    part[1] = lax.fori_loop(0, n_dp - 1, lambda i, col: col + sums[i], part[0])
    for i, dev in enumerate(near):
        c = remote(part.at[1], sums.at[n_dp - 1 + i], ss.at[n_dp - 1 + i], rs.at[n_dp - 1 + i], dev)
        c.start()
        sent.append(c)
    for c in sent[n_dp - 1 :]:
        c.wait_recv()
    col = part[1]
    for i in range(3):
        col = col + sums[n_dp - 1 + i]
    col_grad = ((e / col - eye) * temp).astype(BF16)
    text_grad = text_grad + nn(col_grad, image_ref[...])
    col_lse = jnp.sum(jnp.log(col) * eye, axis=-1, keepdims=True)
    loss = jnp.log(row_sum) + col_lse - 2.0 * picked
    mine = pl.ds(own, caps)
    loss_ref[mine] = jnp.broadcast_to(loss, (caps, 128))
    for i, dev in enumerate(near):
        c = remote(loss_ref.at[mine], loss_ref.at[mine], l_ss.at[i], l_rs.at[i], dev)
        c.start()
        sent.append(c)
    dot = jnp.sum(text_grad * pooled, axis=-1, keepdims=True)
    grad = inv * text_grad - pooled * (inv * inv * inv * dot)
    grad_ref[...] = grad * (1.0 / SEQ)
    for c in sent:
        c.wait_send()
    for c in sent[n_dp + 2 :]:
        c.wait_recv()


def run_pairs(n_dp, n_mp, pooled, image_low, temps):
    caps = pooled.shape[0]
    total = image_low.shape[0]
    n = n_dp + 2
    return pl.pallas_call(
        functools.partial(pair_kernel, n_dp, n_mp),
        out_shape=[jax.ShapeDtypeStruct((caps, D), F32), jax.ShapeDtypeStruct((caps * n_mp, 128), F32)],
        in_specs=[pl.BlockSpec(memory_space=pltpu.VMEM)] * 3,
        out_specs=[pl.BlockSpec(memory_space=pltpu.VMEM)] * 2,
        scratch_shapes=[
            pltpu.VMEM((n, 1, total), F32),
            pltpu.VMEM((2, 1, total), F32),
            pltpu.SemaphoreType.DMA((n,)),
            pltpu.SemaphoreType.DMA((n,)),
            pltpu.SemaphoreType.DMA((3,)),
            pltpu.SemaphoreType.DMA((3,)),
        ],
        compiler_params=pltpu.CompilerParams(
            collective_id=1, has_side_effects=True, vmem_limit_bytes=60 * 2**20
        ),
        name="contrast",
    )(pooled, image_low, temps)


def back_plan(rows, n_dp):
    plan = []
    ks = powers(n_dp)
    size = rows
    for k in ks:
        if k != ks[-1] and size % 32 == 0:
            size //= 2
            plan.append((k, True, size))
        else:
            plan.append((k, False, size))
    return plan


def add_rows(dst, left, right, rows):
    step = 48 if rows % 48 == 0 else 16

    def one(i, carry):
        r = pl.ds(pl.multiple_of(i * step, 16), step)
        dst[r] = (left[r].astype(F32) + right[r].astype(F32)).astype(BF16)
        return carry

    lax.fori_loop(0, rows // step, one, 0)


class Sum:
    def __init__(self, view, rows, base, places, bufs, sems, n_dp):
        self.view, self.rows, self.base = view, rows, base
        self.core, self.xdev, self.dpdev, self.bit = places
        self.rc, self.rx, self.rd, result = bufs
        self.res = result.at[pl.ds(base, rows)]
        self.sems = sems
        self.plan = back_plan(rows, n_dp)
        self.cps = {}

    def go(self, key, src, dst, dev):
        ss, rs, number = self.sems
        i = number[0]
        number[0] += 1
        c = remote(src, dst, ss.at[i], rs.at[i], dev)
        c.start()
        self.cps[key] = c

    def cut(self):
        return pl.ds(self.base, self.rows)

    def send_core(self, s):
        self.go(("c", s), self.view(s), self.rc.at[s // 2, self.cut()], self.core)

    def merge_core(self, s):
        self.cps[("c", s + 1)].wait()
        add_rows(self.view(s), self.view(s), self.rc.at[s // 2, self.cut()], self.rows)

    def send_x(self):
        self.go("x", self.view(2), self.rx.at[self.cut()], self.xdev)

    def merge_x(self):
        self.cps["x"].wait()
        add_rows(self.view(0), self.view(0), self.rx.at[self.cut()], self.rows)
        self.off = 0
        self.level = 0
        self.stack = []
        self.start_level()

    def start_level(self):
        k, halve, size = self.plan[self.level]
        land = self.rd[self.level].at[pl.ds(self.base // (self.rows // size), size)]
        if halve:
            keep = self.off + self.bit(k) * size
            give = self.off + (1 - self.bit(k)) * size
            self.off = keep
        else:
            give = self.off
        src = self.view(0).at[pl.ds(pl.multiple_of(give, 16), size)]
        self.land = land
        self.go(("d", self.level), src, land, self.dpdev(k))

    def merge_level(self):
        k, halve, size = self.plan[self.level]
        self.cps[("d", self.level)].wait()
        piece = pl.ds(pl.multiple_of(self.off, 16), size)
        self.level += 1
        more = self.level < len(self.plan)
        kept = self.view(0).at[piece]
        add_rows(kept if more else self.res.at[piece], kept, self.land, size)
        if halve:
            self.stack.append((k, size, self.off))
        if more:
            self.start_level()
        else:
            self.start_back()

    def start_back(self):
        if not self.stack:
            return
        k, size, off = self.stack[-1]
        piece = self.res.at[pl.ds(pl.multiple_of(off, 16), size)]
        self.go(("b", len(self.stack)), piece, piece, self.dpdev(k))

    def merge_back(self):
        self.cps[("b", len(self.stack))].wait()
        self.stack.pop()
        self.start_back()

    def steps(self):
        yield self.merge_x()
        for _ in self.plan:
            yield self.merge_level()
        for _ in [p for p in self.plan if p[1]]:
            yield self.merge_back()


def back_kernel(
    n_dp,
    rows,
    x_hbm, wq_hbm, wo_hbm, wu_hbm, wd_hbm, qkv_hbm, mix_hbm, hid_hbm, gp_hbm, sv_hbm, rg_ref, vec_ref,
    ig_out, g_out, gd_out, sm_out, sa, ra,
    xv, wq, wo, wu, wd, qkv, mix, hid, gp, nv, nt_buf, acc, hl, mg, igv, low, ag,
    gq, go_, gu, rc, rx, rd0, rd1, rd2, result, stage_s, stage_r, gd, pk, pr, pd,
    ss, rs, ig_ss, ig_rs, s_ss, s_rs, r_ss, r_rs, m_ss, m_rs, l_sem, o_sem,
):
    dp = lax.axis_index("dp")
    mp = lax.axis_index("mp")
    core = (dp, flip(mp, 1))
    xdev = (dp, flip(mp, 2))
    diag = (dp, flip(flip(mp, 1), 2))
    dps = powers(n_dp)
    caps = rows // SEQ

    bar = pltpu.get_barrier_semaphore()
    greet = [core, xdev, diag] + [(flip(dp, k), mp) for k in dps]
    for dev in greet:
        pl.semaphore_signal(bar, inc=1, device_id=dev, device_id_type=MESH)

    loads = {}

    def load(key, src, dst):
        c = pltpu.make_async_copy(src, dst, l_sem.at[len(loads)])
        c.start()
        loads[key] = c

    def ready(*keys):
        for key in keys:
            loads[key].wait()

    load("hid", hid_hbm, hid)
    for s in (3, 2, 1, 0):
        load(("wd", s), wd_hbm.at[s], wd.at[s])
        load(("gp", s), gp_hbm.at[s], gp.at[s])
        load(("wu", s), wu_hbm.at[s], wu.at[s])
    load("mix", mix_hbm, mix)
    load("wo", wo_hbm, wo)
    load("qkv", qkv_hbm, qkv)
    load("x", x_hbm.at[pl.ds(mp * rows, rows)], xv)
    load("wq", wq_hbm, wq)
    load("s0", sv_hbm.at[0], sa.at[0, 0, 0])

    low[...] = rg_ref[...].astype(BF16)
    load("r0", low, ra.at[0, 0, 0])
    pl.semaphore_wait(bar, len(greet))

    s_first = [
        remote(sv_hbm.at[k], sa.at[k % 2, 0, k // 2], s_ss.at[k - 1], s_rs.at[k - 1], dev)
        for k, dev in ((1, core), (2, xdev), (3, diag))
    ]
    r_first = remote(low, ra.at[0, 0, 1], r_ss.at[0], r_rs.at[0], xdev)
    for c in s_first + [r_first]:
        c.start()
    s_copies, r_copies = [s_first], [[r_first]]

    def share(j):
        if j == 0:
            ready("s0", "r0")
        for c in s_copies[-1] + r_copies[-1]:
            c.wait_recv()
        if j < len(dps):
            k = dps[j]
            dev = (flip(dp, k), mp)
            s_copies.append([remote(sa.at[:, 0:k], sa.at[:, k : 2 * k], s_ss.at[3 + j], s_rs.at[3 + j], dev)])
            r_copies.append([remote(ra.at[0, 0:k], ra.at[0, k : 2 * k], r_ss.at[1 + j], r_rs.at[1 + j], dev)])
            s_copies[-1][0].start()
            r_copies[-1][0].start()
        elif j == len(dps):
            n = 1 + len(dps)
            r_copies.append([remote(ra.at[0], ra.at[1], r_ss.at[n], r_rs.at[n], core)])
            s_copies.append([])
            r_copies[-1][0].start()

    outs = []

    def put(src, dst):
        c = pltpu.make_async_copy(src, dst, o_sem.at[len(outs)])
        c.start()
        outs.append(c)

    number = [0]
    places = (core, xdev, lambda k: (flip(dp, k), mp), lambda k: lax.rem(lax.div(dp, k), 2))
    rds = (rd0, rd1) + tuple([rd2.at[i] for i in range(rd2.shape[0])])
    make = lambda view, n, base: Sum(view, n, base, places, (rc, rx, rds, result), (ss, rs, number), n_dp)
    u_rows, o_rows, q_rows = gu.shape[1], go_.shape[2], gq.shape[3]
    u_cut = u_rows // 2
    sum_u = [make(lambda s, i=i: gu.at[s, pl.ds(i * u_cut, u_cut)], u_cut, i * u_cut) for i in range(2)]
    sum_o = make(lambda s: go_.at[s // 2, s % 2], o_rows, u_rows)
    sum_q = [
        make(lambda s, n=n: gq.at[s // 2, n, s % 2], q_rows, u_rows + o_rows + n * q_rows) for n in range(3)
    ]

    g1, s1 = vec_ref[0:1], vec_ref[1:2]
    g2, s2 = vec_ref[3:4], vec_ref[4:5]
    step = 128
    pk[...] = jnp.zeros_like(pk)
    pk[0, 5:6] = jnp.sum(rg_ref[...], axis=0, keepdims=True) * float(SEQ)

    ready("hid")

    def norm_again(i, carry):
        r = pl.ds(pl.multiple_of(i * step, step), step)
        xhat, _ = norm_parts(hid[r])
        n = (xhat * g2 + s2).astype(BF16)
        nt_buf[:, r] = n.T
        return carry

    lax.fori_loop(0, rows // step, norm_again, 0)
    tile = 256

    def mlp_grad(s):
        ready(("wd", s), ("gp", s))
        ag[...] = nt(low[...], wd[s])

        def spread(i, total):
            r = pl.ds(pl.multiple_of(i * step, step), step)
            a = ag[pl.ds(pl.multiple_of(i * (step // SEQ), step // SEQ), step // SEQ)]
            a = jnp.broadcast_to(a[:, None, :], (step // SEQ, SEQ, D)).reshape(step, D)
            u = (a * gp[s, r].astype(F32)).astype(BF16)
            gp[s, r] = u
            return total + jnp.sum(u.astype(F32), axis=0, keepdims=True)

        pk[s, 6:7] = lax.fori_loop(0, rows // step, spread, jnp.zeros((1, D), F32))

        def one(j, carry):
            c = pl.ds(pl.multiple_of(j * tile, tile), tile)
            gu[s, :, c] = nn(nt_buf[...], gp[s, :, c]).astype(BF16)
            return carry

        lax.fori_loop(0, D // tile, one, 0)

    def mlp_back(s, begin):
        ready(("wu", s))

        def one(j, carry):
            c = pl.ds(pl.multiple_of(j * tile, tile), tile)
            r = nt(gp[s], wu[s, c, :])
            if begin:
                acc[:, c] = r
            else:
                acc[:, c] += r
            return carry

        lax.fori_loop(0, D // tile, one, 0)

    mlp_grad(3)
    for t in sum_u:
        t.send_core(3)
    mlp_grad(2)
    for t in sum_u:
        t.merge_core(2)
        t.send_x()
    share(0)
    mlp_grad(1)
    for t in sum_u:
        t.send_core(1)
    mlp_grad(0)
    share(1)
    for t in sum_u:
        t.merge_core(0)
    for s in (3, 2, 1, 0):
        mlp_back(s, s == 3)
    share(2)

    def second_back(i, carry):
        r = pl.ds(pl.multiple_of(i * step, step), step)
        g = acc[r]
        xhat, rstd = norm_parts(hid[r])
        t = g * g2
        back = rstd * (
            t - jnp.mean(t, axis=-1, keepdims=True) - xhat * jnp.mean(t * xhat, axis=-1, keepdims=True)
        )
        a = rg_ref[pl.ds(pl.multiple_of(i * (step // SEQ), step // SEQ), step // SEQ)]
        h = jnp.broadcast_to(a[:, None, :], (step // SEQ, SEQ, D)).reshape(step, D) + back
        acc[r] = h
        hl[r] = h.astype(BF16)
        pk[0, 3:4] += jnp.sum(g * xhat, axis=0, keepdims=True)
        pk[0, 4:5] += jnp.sum(g, axis=0, keepdims=True)
        pk[0, 2:3] += jnp.sum(h, axis=0, keepdims=True)
        return carry

    lax.fori_loop(0, rows // step, second_back, 0)

    width = 2 * o_rows
    blocks = width // 128
    ready("mix", "wo")
    for p in (1, 0):
        mt = mix[p].T
        g = nn(mt, hl[...]).astype(BF16)
        go_[p, 0] = g[:o_rows]
        go_[p, 1] = g[o_rows:]
        sum_o.send_core(2 * p + 1)
        mg[p] = nt(hl[...], wo[p].reshape(width, D)).astype(BF16)
    sum_o.merge_core(2)
    sum_o.send_x()
    sum_o.merge_core(0)

    ready("qkv", "x", "wq")

    def first_again(i, carry):
        r = pl.ds(pl.multiple_of(i * step, step), step)
        xhat, _ = norm_parts(xv[r].astype(F32))
        nv[r] = (xhat * g1 + s1).astype(BF16)
        return carry

    lax.fori_loop(0, rows // step, first_again, 0)
    first = head_masks()
    same = seq_mask()

    def attend_back(p):
        def chunk(i, carry):
            r = pl.ds(pl.multiple_of(i * 128, 128), 128)
            for j in range(blocks):
                c = slice(j * 128, (j + 1) * 128)
                q, k, v = qkv[p, 0, r, c], qkv[p, 1, r, c], qkv[p, 2, r, c]
                do = mg[p, r, c]
                k2, v2 = two_heads(k, first), two_heads(v, first)
                probs = block_probs(q, k2, same)
                back = nt(do, v2)
                score = []
                for h in range(2):
                    b = back[:, h * 128 : (h + 1) * 128]
                    score.append(
                        (probs[h] * (b - jnp.sum(probs[h] * b, axis=-1, keepdims=True))).astype(BF16)
                    )
                sb = jnp.concatenate(score, axis=1)
                pb = jnp.concatenate([t.astype(BF16) for t in probs], axis=1)
                qkv[p, 0, r, c] = (nn(sb, k2) * (HEAD_DIM**-0.5)).astype(BF16)
                dk = tn(sb, q)
                dv = tn(pb, do)
                qkv[p, 1, r, c] = jnp.where(first, dk[:128], dk[128:]).astype(BF16)
                qkv[p, 2, r, c] = jnp.where(first, dv[:128], dv[128:]).astype(BF16)
            return carry

        lax.fori_loop(0, rows // 128, chunk, 0)
        for n, at in ((0, 0), (2, width)):
            t = jnp.sum(qkv[p, n].astype(F32), axis=0, keepdims=True)
            for k in (2 * p, 2 * p + 1):
                pk[k, 7:8, at : at + width] = t

    def qkv_grad(p):
        for n in range(3):
            g = nn(qkv[p, n].T, nv[...]).astype(BF16)
            gq[p, n, 0] = g[:q_rows]
            gq[p, n, 1] = g[q_rows:]
            sum_q[n].send_core(2 * p + 1)

    def qkv_back(p, begin):
        def one(j, carry):
            c = pl.ds(pl.multiple_of(j * tile, tile), tile)
            r = nn(qkv[p, 0], wq[p, 0, :, :, c].reshape(width, tile))
            for n in (1, 2):
                r += nn(qkv[p, n], wq[p, n, :, :, c].reshape(width, tile))
            if begin:
                hid[:, c] = r
            else:
                hid[:, c] += r
            return carry

        lax.fori_loop(0, D // tile, one, 0)

    queue = [t.steps() for t in sum_u]
    attend_back(1)
    next(queue[0])
    qkv_grad(1)
    for t in sum_q:
        t.merge_core(2)
        t.send_x()
    next(queue[0])
    qkv_back(1, True)
    next(queue[1])
    next(queue[0])
    attend_back(0)
    next(queue[1])
    qkv_grad(0)
    next(queue[0])
    next(queue[1])
    qkv_back(0, False)
    for t in sum_q:
        t.merge_core(0)

    def first_back(i, carry):
        r = pl.ds(pl.multiple_of(i * step, step), step)
        g = hid[r]
        xhat, rstd = norm_parts(xv[r].astype(F32))
        t = g * g1
        back = rstd * (
            t - jnp.mean(t, axis=-1, keepdims=True) - xhat * jnp.mean(t * xhat, axis=-1, keepdims=True)
        )
        igv[r] = (acc[r] + back).astype(BF16)
        pk[0, 0:1] += jnp.sum(g * xhat, axis=0, keepdims=True)
        pk[0, 1:2] += jnp.sum(g, axis=0, keepdims=True)
        return carry

    lax.fori_loop(0, rows // step, first_back, 0)
    for k in (1, 2, 3):
        pk[k, 0:6] = pk[0, 0:6]
    small = [
        remote(pk.at[k], pr.at[k - 1], m_ss.at[k - 1], m_rs.at[k - 1], dev)
        for k, dev in ((1, core), (2, xdev), (3, diag))
    ]
    for c in small:
        c.start()
    own = pl.ds(mp * rows, rows)
    ig = [
        remote(igv, ig_out.at[own], ig_ss.at[0], ig_rs.at[0], core),
        remote(igv, ig_out.at[own], ig_ss.at[1], ig_rs.at[1], xdev),
    ]
    for c in ig:
        c.start()
    put(igv, ig_out.at[own])

    share(3)
    queue.append(sum_o.steps())
    queue.extend(t.steps() for t in sum_q)

    for j in range(4, len(dps) + 1):
        share(j)
    for c in r_copies[-1]:
        c.wait_recv()
    group = min(n_dp, 8)
    for blk in range(n_dp // group):
        cut = pl.ds(blk * group, group)
        pair = [
            pltpu.make_async_copy(sa.at[:, cut], stage_s, l_sem.at[0]),
            pltpu.make_async_copy(ra.at[:, cut], stage_r, l_sem.at[1]),
        ]
        for c in pair:
            c.start()
        for c in pair:
            c.wait()
        n = 4 * group * caps
        st = stage_s[...].reshape(n, D).T
        for j in range(D // tile):
            c = slice(j * tile, (j + 1) * tile)
            t = nn(st, stage_r[..., c].reshape(n, tile))
            if blk == 0:
                gd[:, c] = t
            else:
                gd[:, c] += t
    put(gd, gd_out)

    def small_steps():
        for c in small:
            c.wait()
        a, b1, b2, b3 = pk[0], pr[0], pr[1], pr[2]
        line = lax.broadcasted_iota(jnp.int32, a.shape, 0)
        total = a + b1 + b2 + b3
        even = a[7:8] + b2[7:8]
        odd = b1[7:8] + b3[7:8]
        total = jnp.where(line == 7, even, jnp.where(line == 8, odd, total))
        pd[0] = total
        m = len(dps)
        for j, k in enumerate(dps):
            c = remote(pd.at[j], pd.at[m + 1 + j], m_ss.at[3 + j], m_rs.at[3 + j], (flip(dp, k), mp))
            c.start()
            yield
            c.wait()
            pd[j + 1] = pd[j] + pd[m + 1 + j]
        put(pd.at[m], sm_out)
        yield

    queue.append(small_steps())
    live = list(queue)
    while live:
        left = []
        for g in live:
            try:
                next(g)
                left.append(g)
            except StopIteration:
                pass
        live = left
    put(result, g_out)

    ig[1].wait()
    far = pl.ds(flip(mp, 2) * rows, rows)
    last = remote(ig_out.at[far], ig_out.at[far], ig_ss.at[2], ig_rs.at[2], core)
    last.start()
    ig[0].wait()
    last.wait()
    for group_ in s_copies + r_copies:
        for c in group_:
            c.wait_send()
    for c in outs:
        c.wait()


def run_backward(n_dp, rows, tokens, wq, wo, wu, wd, qkv, mix, hid, gp, sv, rg, vec):
    caps = rows // SEQ
    sds = jax.ShapeDtypeStruct
    q_rows = wq.shape[3]
    o_rows = wo.shape[2]
    u_rows = wu.shape[1]
    total = u_rows + o_rows + 3 * q_rows
    width = 2 * q_rows
    n_pow = len(powers(n_dp))
    outs = [
        sds(tokens.shape, BF16),
        sds((total, D), BF16),
        sds(wd.shape[1:], F32),
        sds((16, D), F32),
        sds((2, n_dp, 2, caps, D), BF16),
        sds((2, n_dp, 2, caps, D), BF16),
    ]
    group = min(n_dp, 8)
    any_spec = pl.BlockSpec(memory_space=pl.ANY)
    vmem = pl.BlockSpec(memory_space=pltpu.VMEM)
    vm = lambda s: pltpu.VMEM(s.shape, s.dtype)
    sem = lambda n: pltpu.SemaphoreType.DMA((n,))
    n_sum = 6 * (3 + 2 * n_pow)
    return pl.pallas_call(
        functools.partial(back_kernel, n_dp, rows),
        out_shape=outs,
        in_specs=[any_spec] * 10 + [vmem] * 2,
        out_specs=[any_spec] * len(outs),
        scratch_shapes=[
            pltpu.VMEM((rows, D), BF16),
            vm(wq), vm(wo), vm(wu), vm(wd), vm(qkv), vm(mix), vm(hid), vm(gp),
            pltpu.VMEM((rows, D), BF16),
            pltpu.VMEM((D, rows), BF16),
            pltpu.VMEM((rows, D), F32),
            pltpu.VMEM((rows, D), BF16),
            pltpu.VMEM((2, rows, width), BF16),
            pltpu.VMEM((rows, D), BF16),
            pltpu.VMEM((caps, D), BF16),
            pltpu.VMEM((caps, D), F32),
            vm(wq), vm(wo), vm(wu),
            pltpu.VMEM((2, total, D), BF16),
            pltpu.VMEM((total, D), BF16),
            pltpu.VMEM((total // 2, D), BF16),
            pltpu.VMEM((total // 4, D), BF16),
            pltpu.VMEM((max(1, n_pow - 2), total // 4, D), BF16),
            pltpu.VMEM((total, D), BF16),
            pltpu.VMEM((2, group, 2, caps, D), BF16),
            pltpu.VMEM((2, group, 2, caps, D), BF16),
            pltpu.VMEM(wd.shape[1:], F32),
            pltpu.VMEM((4, 16, D), F32),
            pltpu.VMEM((3, 16, D), F32),
            pltpu.VMEM((2 * n_pow + 1, 16, D), F32),
            sem(n_sum), sem(n_sum), sem(3), sem(3), sem(3 + n_pow), sem(3 + n_pow),
            sem(2 + n_pow), sem(2 + n_pow), sem(3 + n_pow), sem(3 + n_pow), sem(20), sem(4),
        ],
        compiler_params=pltpu.CompilerParams(
            collective_id=2, has_side_effects=True, vmem_limit_bytes=62 * 2**20
        ),
        name="backward",
    )(tokens, wq, wo, wu, wd, qkv, mix, hid, gp, sv, rg, vec)


def solution(mesh):
    n_dp, n_mp = mesh.shape["dp"], mesh.shape["mp"]

    def body(
        tokens, ln1_gain, ln1_bias, w_qkv, qv_bias, w_out, out_bias, ln2_gain, ln2_bias,
        w_up, up_bias, w_down, down_bias, images, image_group, pair_shard, pair_row,
    ):
        rows = tokens.shape[0] // n_mp
        per_dp = pair_row.shape[0]
        dp = lax.axis_index("dp")
        mp = lax.axis_index("mp")
        wq_t = jnp.transpose(w_qkv, (0, 2, 1))
        q_rows = wq_t.shape[1]
        zero = jnp.zeros((q_rows,), F32)
        tail = jnp.zeros((D - 2 * q_rows,), F32)
        lines = [up_bias]
        for n in range(2):
            lines.append(jnp.concatenate([qv_bias[n], zero, tail]))
            lines.append(jnp.concatenate([zero, qv_bias[n], tail]))
        bi = jnp.stack(lines + [jnp.zeros((D,), F32)] * 3)
        vec = jnp.stack(
            [ln1_gain, ln1_bias, out_bias, ln2_gain, ln2_bias, down_bias, jnp.zeros((D,), F32), jnp.zeros((D,), F32)]
        )
        n_img = images.shape[0]
        index = pair_shard[:, 0] * n_img + pair_row
        info = jnp.concatenate([index, image_group]).reshape(-1, 128)
        info = jnp.pad(info, ((0, -info.shape[0] % 8), (0, 0)))
        (wq, wo, wu, wd, imgs, infos, qkv, mix, hid, gp, sv, text, pooled) = run_forward(
            n_dp, rows, tokens, wq_t, w_out, w_up, w_down, bi, images, info, vec
        )
        every = lax.bitwise_xor(jnp.arange(n_dp, dtype=jnp.int32), dp)
        flat = infos.reshape(n_dp, -1)[every]
        index = flat[:, :per_dp].reshape(-1)
        group = flat[:, per_dp : per_dp + n_img].reshape(-1)
        place = lax.bitwise_xor(index // n_img, dp) * n_img + index % n_img
        raw = imgs.reshape(n_dp * n_img, D)[place].astype(F32)
        image_low = (raw * lax.rsqrt(jnp.sum(raw * raw, axis=-1, keepdims=True) + 1e-06)).astype(BF16)
        temps = jnp.where(group[index] == 1, 64.0, 40.0).astype(F32)[None, :]
        rg, loss = run_pairs(n_dp, n_mp, pooled, image_low, temps)
        ig, grads, wd_g, small, _, _ = run_backward(
            n_dp, rows, tokens, wq, wo, wu, wd, qkv, mix, hid, gp, sv, rg, vec
        )
        cuts = [w_up.shape[0], w_up.shape[0] + w_out.shape[0]]
        wu_g, wo_g = grads[: cuts[0]], grads[cuts[0] : cuts[1]]
        wq_g = grads[cuts[1] :].reshape(3, q_rows, D)
        text_out = lax.all_gather(text, "mp", axis=0, tiled=True)
        qb = small[7].reshape(2, 2 * q_rows)[:, :q_rows] + small[8].reshape(2, 2 * q_rows)[:, q_rows:]
        return (
            text_out, ig, loss[:, 0],
            small[0], small[1], jnp.transpose(wq_g, (0, 2, 1)).astype(F32), qb, wo_g.astype(F32), small[2],
            small[3], small[4], wu_g.astype(F32), small[6], wd_g, small[5],
        )

    in_specs = (
        P("dp", None), P(), P(), P(None, None, "mp"), P(None, "mp"), P("mp", None), P(), P(), P(),
        P(None, "mp"), P("mp"), P("mp", None), P(), P("dp", None), P("dp"), P("dp", None), P("dp"),
    )
    out_specs = (
        P("dp", None), P("dp", None), P("dp"), P(), P(), P(None, None, "mp"), P(None, "mp"), P("mp", None),
        P(), P(), P(), P(None, "mp"), P("mp"), P("mp", None), P(),
    )
    return jax.shard_map(body, mesh=mesh, in_specs=in_specs, out_specs=out_specs, check_vma=False)
```

time: 856 us -> 308 us (0.36)
  waiting for transfers between devices: 497 us -> 0.02 us
  Pallas kernels: 0 us -> 250 us
  matrix products: 93.3 us -> 0 us
  blocking collectives: 74.3 us -> 0 us
  local copies, waits for them, and re-layouts: 101 us -> 33.6 us
  other arithmetic: 55.5 us -> 9.34 us
  starting transfers between devices: 13.1 us -> 0.04 us
    psum x5 -> x0, waiting for transfers between devices: 409 us -> none  [the longest x1 187 us: body(): lax.psum((grads[0], grads[1], grads[2], grads[3], grads[4], grads[5], gra...]
    pallas_call x0 -> x3, Pallas kernels: none -> 250 us  [the longest x1 166 us: run_backward(): pl.pallas_call(functools.partial(back_kernel, n_dp, rows), out_shape=outs...]
    dot_general x23 -> x0, matrix products: 91 us -> none  [the longest x1 18.7 us: text_forward(): jnp.dot(norm_two_low, w_up, preferred_element_type=jnp.float32) + up_bias]
    reduce_scatter x1 -> x0, waiting for transfers between devices: 72.4 us -> none  [body(): lax.psum_scatter(spread_terms, 'dp', scatter_dimension=0, tiled=True)]
    reduce_sum x18 -> x1, other arithmetic: 42.6 us -> 0.38 us  [body(): jnp.sum(raw * raw, axis=-1, keepdims=True) + 1e-06]
    psum x1 -> x0, blocking collectives: 40.2 us -> none  [body(): lax.psum((grads[0], grads[1], grads[2], grads[3], grads[4], grads[5], gra...]
    convert_element_type x7 -> x0, local copies, waits for them, and re-layouts: 18.9 us -> none  [the longest x2 7.46 us: text_forward(): mixed = mixed.reshape(row_count, local_width).astype(jnp.bfloat16)]
    all_to_all x1 -> x0, blocking collectives: 17.3 us -> none  [body(): lax.all_to_all(sent_rows, 'dp', split_axis=0, concat_axis=0, tiled=True)]
  transfers between devices with their start and end apart: 10 -> 1, of which waited for: 8 -> 0; matrix products, arithmetic and copies ran while one was open for 10% -> 8% of each run, Pallas kernels for 0% -> 59%
where the time goes in v1:
time: 308 us; the launch traced here: 307 us
  Pallas kernels  250 us (81%)
  local copies, waits for them, and re-layouts  33.6 us (11%)
  between operations  14.2 us (5%)
  other arithmetic  9.34 us (3%)
    pallas_call x1, Pallas kernels, run_backward(): pl.pallas_call(functools.partial(back_kernel, n_dp, rows), out_shape=outs...  166 us
    pallas_call x1, Pallas kernels, run_forward(): pl.pallas_call(functools.partial(fwd_kernel, n_dp, rows), out_shape=outs,...  68.2 us
    pallas_call x1, Pallas kernels, run_pairs(): pl.pallas_call(functools.partial(pair_kernel, n_dp, n_mp), out_shape=[jax...  16.1 us
    unnamed x14, local copies, waits for them, and re-layouts  8.9 us
    gather x1, local copies, waits for them, and re-layouts, body(): raw = imgs.reshape(n_dp * n_img, D)[place].astype(F32)  6.77 us
  transfers between devices with their start and end apart: 1, of which 0 were waited for; matrix products, arithmetic and copies ran while one was open for 8% of the time, Pallas kernels for 59%

profile of v1, /device:TPU:0, one launch (start us, length us, event | category | flops | bytes accessed | tf_op | source)
XLA Modules:
  0.0 307.4 jit_solution(5639326152931527391)
XLA Ops:
  7.2 0.0 all-gather.2.cloned.1.call-start
  7.2 0.8 fusion.4
  8.0 0.1 pad_maximum_fusion
  8.1 0.7 stack.39
  8.8 0.7 stack.45
  9.5 0.7 stack.46
  10.2 0.7 stack.47
  10.9 0.7 stack.48
  11.6 0.7 stack.49
  12.2 0.7 stack.50
  12.9 0.7 bitcast_add_fusion
  13.6 0.7 add_bitcast_fusion
  14.3 0.6 pad.4.info_hbm
  14.9 0.6 stack.44.bi_hbm
  15.5 0.6 stack.51.vec_ref
  16.2 68.2 %forward.1 = (bf16[2,3,2,192,768]{4,3,2,1,0:T(8,128)(2,1)}, bf16[2,2,192,768]{3,2,1,0:T(8,128)(2,1)}, bf16[4,768,768]{2,1,0:T(8,128)(2,1)}, bf16[4,768,768]{2,1,...) custom-call(bf16[2048,768]{1,0:T(8,128)(2,1)} %x_hbm.3, ...), custom_call_target="tpu_custom_call" | custom-call | tf_op jit(solution)/shard_map/forward/pallas_call | solution.py:463
  84.4 0.0 all-gather.2.cloned.1.call-update
  84.4 0.8 copy.35
  85.2 0.6 gather_fusion
  85.9 6.8 %gather_fusion.1 = bf16[1024,768]{1,0:T(8,128)(2,1)S(1)} fusion(bf16[2048,768]{1,0:T(8,128)(2,1)} %bitcast.26, s32[1024]{0:T(1024)S(1)} %broadcast_clamp_fusion.1), kind=kCustom, calls=%fused_computation.1 | custom fusion | bytes 3149824 | tf_op jit(solution)/shard_map/gather | solution.py:1193
  92.7 6.2 %gather_fusion.2 = s32[1024]{0:T(1024)S(1)} fusion(s32[2048]{0:T(1024)S(1)} %bitcast.25, s32[1024]{0:T(1024)S(1)} %broadcast_clamp_fusion), kind=kCustom, calls=%fused_computation.2 | custom fusion | bytes 12288 | tf_op jit(solution)/shard_map/gather | solution.py:1195
  98.9 0.4 fusion
  99.2 0.6 compare_select_fusion.5
  99.8 1.5 fusion.1.image_ref
  101.3 16.1 %contrast.1 = (f32[32,768]{1,0:T(8,128)}, f32[128,128]{1,0:T(8,128)}) custom-call(f32[32,768]{1,0:T(8,128)} %get-tuple-element.44.pool_ref, bf16[1024,768]{1,0:T(8,128)(2,1)} %fusion.1.image_ref, f32[1,1024]{1,0:T(1,128)} %bitcast.31), custom_call_target="tpu_custom_call" | custom-call | tf_op jit(solution)/shard_map/contrast/pallas_call | solution.py:574
  117.4 0.0 copy-start.3
  117.5 165.8 %backward.1 = (bf16[2048,768]{1,0:T(8,128)(2,1)}, bf16[1536,768]{1,0:T(8,128)(2,1)}, f32[768,768]{1,0:T(8,128)}, f32[16,768]{1,0:T(8,128)}, bf16[2,8,2,32,768]{4...) custom-call(bf16[2048,768]{1,0:T(8,128)(2,1)} %x_hbm.3, bf16[2,3,2,192,768]{4,3,2,1,0:T(8,128)(2,1)} %get-tuple-element.35.wq_hbm, ...), custom_call_target="tpu_custom_call" | custom-call | tf_op jit(solution)/shard_map/backward/pallas_call | solution.py:1119
  283.2 1.7 slice_reduce_fusion.1
  285.0 0.0 copy-start.1
  285.0 1.4 slice.66
  286.4 0.0 copy-done.3
  286.4 0.6 slice_reduce_fusion
  287.0 0.7 slice_add_fusion
  287.6 1.8 slice_convert_fusion.1
  289.5 1.3 convert_bitcast_fusion
  290.8 0.0 copy-done.1
  290.8 1.6 slice_convert_fusion
  292.4 0.0 all-gather.2.cloned.1.call-done
  292.4 0.0 copy-start
  292.4 3.9 %copy.39 = bf16[2048,768]{1,0:T(8,128)(2,1)} copy(bf16[2048,768]{1,0:T(8,128)(2,1)} %all-gather.2.cloned.1.call-done) | data formatting | bytes 6291456
  296.3 0.0 copy-done
  296.3 0.0 copy-start.2
  296.3 1.7 copy.40
  298.0 1.1 copy-done.2
  299.1 1.4 copy.41
  (19 shorter events, 0.1 us)
Async XLA Ops:
  7.2 285.2 %all-gather.2.cloned.1.call-start = ((), (), s32[]{:S(2)}) async-start(), calls=%async_computation | async-start | bytes 3932160 | tf_op jit(solution)/shard_map/all_gather | solution.py:1203
  117.4 168.9 %copy-start.3 = (f32[128,128]{1,0:T(8,128)S(1)}, f32[128,128]{1,0:T(8,128)}, u32[]{:S(2)}) copy-start(f32[128,128]{1,0:T(8,128)} %get-tuple-element.49) | copy-start | bytes 196612
  285.0 5.8 %copy-start.1 = (bf16[1536,768]{1,0:T(8,128)(2,1)S(1)}, bf16[1536,768]{1,0:T(8,128)(2,1)}, u32[]{:S(2)}) copy-start(bf16[1536,768]{1,0:T(8,128)(2,1)} %get-tuple-element.51) | copy-start | bytes 7077892
  292.4 3.9 %copy-start = (bf16[2048,768]{1,0:T(8,128)(2,1)S(1)}, bf16[2048,768]{1,0:T(8,128)(2,1)}, u32[]{:S(2)}) copy-start(bf16[2048,768]{1,0:T(8,128)(2,1)} %get-tuple-element.88) | copy-start | bytes 9437188
  296.3 2.8 copy-start.2
Sparse Core Ops, SparseCore 0:
  84.6 30.1 all-gather.1

commit v2 on v1

--- a/solution.py
+++ b/solution.py
@@ -96,10 +96,13 @@
 def fwd_kernel(
     n_dp,
     rows,
-    x_hbm, wq_hbm, wo_hbm, wu_hbm, wd_hbm, bi_hbm, img_hbm, info_hbm, vec_ref,
-    wq_out, wo_out, wu_out, wd_out, imgs, info, qkv_out, mix_out, hid_out, gp_out, s_out, text_out, pool_out,
-    xv, wq, wo, wu, wd, bi, n1, qkv, mix, hid, n2, gp, act, acc, sv, pool,
-    w_ss, w_rs, b_ss, b_rs, i_ss, i_rs, l_sem, o_sem,
+    x_hbm, wq_hbm, wo_hbm, wu_hbm, wd_hbm, ub_hbm, qv_hbm, g1_hbm, s1_hbm, ob_hbm, g2_hbm, s2_hbm, db_hbm,
+    img_hbm, group_hbm, shard_hbm, row_hbm,
+    wq_out, wo_out, wu_out, wd_out, imgs, low_out, temp_out, qkv_out, mix_out, hid_out, gp_out, s_out, text_out,
+    pool_out,
+    xv, wq, wo, wu, wd, bi, qv, vec_ref, ints, shard, info, stage, hot, unit, temp, n1, qkv, mix, hid, n2, gp, act,
+    acc, sv, pool,
+    w_ss, w_rs, b_ss, b_rs, i_ss, i_rs, l_sem, p_sem, o_sem, u_sem,
 ):
     dp = lax.axis_index("dp")
     mp = lax.axis_index("mp")
@@ -121,16 +124,35 @@
         pltpu.make_async_copy(wo_hbm, wo.at[0, 0], l_sem.at[2]),
         pltpu.make_async_copy(wu_hbm, wu.at[0], l_sem.at[3]),
         pltpu.make_async_copy(wd_hbm, wd.at[0], l_sem.at[4]),
-        pltpu.make_async_copy(bi_hbm, bi.at[0], l_sem.at[5]),
-        pltpu.make_async_copy(img_hbm, imgs.at[0], l_sem.at[6]),
-        pltpu.make_async_copy(info_hbm, info.at[0], l_sem.at[7]),
+        pltpu.make_async_copy(img_hbm, imgs.at[0], l_sem.at[5]),
     ]
-    for c in local:
+    n_img = img_hbm.shape[0]
+    parts = n_img // 128
+    lines = [(ub_hbm, bi.at[0, 0]), (qv_hbm, qv), (row_hbm, ints.at[0]), (shard_hbm, shard)]
+    lines += [(group_hbm.at[pl.ds(i * 128, 128)], ints.at[1 + i]) for i in range(parts)]
+    early = len(lines)
+    lines += [(v, vec_ref.at[i]) for i, v in enumerate((g1_hbm, s1_hbm, ob_hbm, g2_hbm, s2_hbm, db_hbm))]
+    lines = [pltpu.make_async_copy(a, b_, p_sem.at[i]) for i, (a, b_) in enumerate(lines)]
+    for c in lines[:early] + local + lines[early:]:
         c.start()
+    for c in lines[:early]:
+        c.wait()
+    q_rows = wq_hbm.shape[1]
+    width = 2 * q_rows
+    wide = jnp.concatenate([qv[...], qv[...]], axis=1) if q_rows % 128 == 0 else None
+    if wide is None:
+        bi[0, 8:16, :width] = jnp.zeros((8, width), F32)
+        bi[0, 8:10, :q_rows] = qv[...]
+        wide = bi[0, 8:16, :width]
+    turned = pltpu.roll(wide, q_rows, 1)
+    bi[0, 1:2, :width], bi[0, 2:3, :width] = wide[0:1], turned[0:1]
+    bi[0, 3:4, :width], bi[0, 4:5, :width] = wide[1:2], turned[1:2]
+    tall = jnp.broadcast_to(shard[...], (128, 128)).T
+    info[0, 0:1] = tall[0:1] * n_img + ints[0:1]
+    info[0, 1 : 1 + parts] = ints[1 : 1 + parts]
 
     pl.semaphore_wait(bar, len(greet))
 
-    q_rows = wq_hbm.shape[1]
     o_rows = wo_hbm.shape[0]
     u_rows = wu_hbm.shape[0]
     d_rows = wd_hbm.shape[0]
@@ -188,7 +210,7 @@
         return c
 
     bias = [
-        remote(bi_hbm, bi.at[s], b_ss.at[s - 1], b_rs.at[s - 1], dev)
+        remote(bi.at[0, 0:8], bi.at[s, 0:8], b_ss.at[s - 1], b_rs.at[s - 1], dev)
         for s, dev in ((1, core), (2, xdev), (3, diag))
     ]
     for c in bias:
@@ -209,12 +231,11 @@
         if j == 0:
             pair = [
                 remote(img_hbm.at[own_cut], imgs.at[1, own_cut], i_ss.at[0], i_rs.at[0], dev),
-                remote(info_hbm, info.at[1], i_ss.at[1], i_rs.at[1], dev),
+                remote(info.at[0], info.at[1], i_ss.at[1], i_rs.at[1], dev),
             ]
         else:
             if j == 1:
-                local[6].wait()
-                local[7].wait()
+                local[5].wait()
             for c in img_copies[j - 1]:
                 c.wait_recv()
             pair = [
@@ -227,8 +248,7 @@
 
     def image_last():
         if len(dps) == 1:
-            local[6].wait()
-            local[7].wait()
+            local[5].wait()
         for c in img_copies[len(dps) - 1]:
             c.wait_recv()
         n = 2 * len(dps)
@@ -267,9 +287,11 @@
         c.start()
         outs.append(c)
 
+    for c in lines[early:]:
+        c.wait()
+    local[0].wait()
     g1, s1, ob = vec_ref[0:1], vec_ref[1:2], vec_ref[2:3]
     g2, s2, db = vec_ref[3:4], vec_ref[4:5], vec_ref[5:6]
-    local[0].wait()
     step = 128
 
     def first_norm(i, carry):
@@ -284,7 +306,6 @@
 
     first = head_masks()
     same = seq_mask()
-    width = 2 * q_rows
     blocks = width // 128
 
     def project(p):
@@ -313,7 +334,6 @@
         lax.fori_loop(0, rows // 128, chunk, 0)
 
     local[1].wait()
-    local[5].wait()
     step_core[0].wait_recv()
     bias[0].wait_recv()
     project(0)
@@ -384,6 +404,61 @@
 
         lax.fori_loop(0, D // tile, one, 0)
 
+    near = min(n_dp, 8)
+    table_rows = near * n_img
+    lane = lax.broadcasted_iota(jnp.int32, (128, 128), 1)
+    shift = n_img.bit_length() - 1
+    rests = []
+
+    def fetch(block):
+        return pltpu.make_async_copy(imgs.at[pl.ds(block * near, near)], stage, u_sem.at[0])
+
+    def pick_images():
+        if n_dp == near:
+            fetch(0).start()
+            fetch(0).wait()
+        for q in range(n_dp // 4):
+            raw = None
+            heat = [None] * 4
+            for block in range(n_dp // near):
+                if n_dp != near:
+                    fetch(block).start()
+                    fetch(block).wait()
+                for i in range(4):
+                    line = info[4 * q + i, 0:1]
+                    line = jnp.bitwise_xor(line >> shift, dp) * n_img + (line & (n_img - 1)) - block * table_rows
+                    col = jnp.broadcast_to(line, (128, 128)).T
+                    total = jnp.zeros((128, 128), F32)
+                    for c in range(table_rows // 128):
+                        hit = (col == lane + c * 128).astype(F32)
+                        hot[i * 128 : (i + 1) * 128, c * 128 : (c + 1) * 128] = hit.astype(BF16)
+                        of = block * near + c // parts
+                        group = info[of, 1 + c % parts : 2 + c % parts].astype(F32)
+                        total += hit * group
+                    total = jnp.broadcast_to(jnp.sum(total, axis=1, keepdims=True), (128, 128)).T[0:1]
+                    heat[i] = total if heat[i] is None else heat[i] + total
+                part = nn(hot[...], stage[...].reshape(table_rows, D))
+                raw = part if raw is None else raw + part
+            if q >= 2:
+                for c in rests[2 * 4 * (q - 2) : 2 * 4 * (q - 1)]:
+                    c.wait()
+            low = raw * lax.rsqrt(jnp.sum(raw * raw, axis=-1, keepdims=True) + 1e-06)
+            unit[q % 2] = low.astype(BF16)
+            for i in range(4):
+                r = 4 * q + i
+                place = dp
+                for k in dps:
+                    if r & k:
+                        place = flip(place, k)
+                at = pl.ds(pl.multiple_of(place * 128, 128), 128)
+                temp[r] = jnp.where(heat[i] > 0.5, 64.0, 40.0)
+                rests.append(
+                    pltpu.make_async_copy(unit.at[q % 2, pl.ds(i * 128, 128)], low_out.at[at], u_sem.at[2 * r + 1])
+                )
+                rests.append(pltpu.make_async_copy(temp.at[r], temp_out.at[:, at], u_sem.at[2 * r + 2]))
+            for c in rests[-8:]:
+                c.start()
+
     local[3].wait()
     up(0)
     forward_y(2, 0)
@@ -403,8 +478,10 @@
     put(sv, s_out)
     step_core[3].wait_recv()
     down(1)
+    image_last()
     forward_y(3, 1)
-    image_last()
+    img_copies[-1][0].wait_recv()
+    pick_images()
     arrived(3)
     put(wd, wd_out)
     down(2)
@@ -430,15 +507,21 @@
     for pair in img_copies:
         for c in pair:
             c.wait_send()
-    img_copies[-1][0].wait_recv()
+    for c in rests[-16:]:
+        c.wait()
     for c in outs:
         c.wait()
 
 
-def run_forward(n_dp, rows, tokens, wq_t, w_out, w_up, w_down, bi, images, info, vec):
+def run_forward(n_dp, rows, args):
+    tokens, wq_t, w_out, w_up, w_down = args[:5]
+    images, pair_row = args[13], args[16]
     caps = rows // SEQ
     q_rows = wq_t.shape[1]
     width = 2 * q_rows
+    n_img = images.shape[0]
+    per_dp = pair_row.shape[0]
+    near = min(n_dp, 8)
     sds = jax.ShapeDtypeStruct
     weights = [
         sds((2, 3, 2, q_rows, D), BF16),
@@ -448,7 +531,8 @@
     ]
     outs = weights + [
         sds((n_dp,) + images.shape, BF16),
-        sds((n_dp,) + info.shape, info.dtype),
+        sds((n_dp * per_dp, D), BF16),
+        sds((1, n_dp * per_dp), F32),
         sds((2, 3, rows, width), BF16),
         sds((2, rows, width), BF16),
         sds((rows, D), F32),
@@ -459,16 +543,25 @@
     ]
     any_spec = pl.BlockSpec(memory_space=pl.ANY)
     vm = lambda s: pltpu.VMEM(s.shape, s.dtype)
-    n_img = 2 * len(powers(n_dp)) + 1
+    n_img_sem = 2 * len(powers(n_dp)) + 1
     return pl.pallas_call(
         functools.partial(fwd_kernel, n_dp, rows),
         out_shape=outs,
-        in_specs=[any_spec] * 8 + [pl.BlockSpec(memory_space=pltpu.VMEM)],
+        in_specs=[any_spec] * len(args),
         out_specs=[any_spec] * len(outs),
         scratch_shapes=[
             pltpu.VMEM((rows, D), BF16),
             *[vm(s) for s in weights],
-            pltpu.VMEM((4,) + bi.shape, F32),
+            pltpu.VMEM((4, 16, D), F32),
+            pltpu.VMEM(args[6].shape, F32),
+            pltpu.VMEM((8, D), F32),
+            pltpu.VMEM((8, 128), jnp.int32),
+            pltpu.VMEM((per_dp, 1), jnp.int32),
+            pltpu.VMEM((n_dp, 8, 128), jnp.int32),
+            pltpu.VMEM((near,) + images.shape, BF16),
+            pltpu.VMEM((512, near * n_img), BF16),
+            pltpu.VMEM((2, 512, D), BF16),
+            pltpu.VMEM((n_dp, 1, 128), F32),
             pltpu.VMEM((rows, D), BF16),
             pltpu.VMEM((2, 3, rows, width), BF16),
             pltpu.VMEM((2, rows, width), BF16),
@@ -483,16 +576,18 @@
             pltpu.SemaphoreType.DMA((28,)),
             pltpu.SemaphoreType.DMA((3,)),
             pltpu.SemaphoreType.DMA((3,)),
-            pltpu.SemaphoreType.DMA((n_img,)),
-            pltpu.SemaphoreType.DMA((n_img,)),
-            pltpu.SemaphoreType.DMA((8,)),
+            pltpu.SemaphoreType.DMA((n_img_sem,)),
+            pltpu.SemaphoreType.DMA((n_img_sem,)),
+            pltpu.SemaphoreType.DMA((6,)),
+            pltpu.SemaphoreType.DMA((16,)),
             pltpu.SemaphoreType.DMA((11,)),
+            pltpu.SemaphoreType.DMA((2 * n_dp + 1,)),
         ],
         compiler_params=pltpu.CompilerParams(
             collective_id=0, has_side_effects=True, vmem_limit_bytes=60 * 2**20
         ),
         name="forward",
-    )(tokens, wq_t, w_out, w_up, w_down, bi, images, info, vec)
+    )(*args)
 
 
 def pair_kernel(
@@ -591,9 +686,20 @@
     )(pooled, image_low, temps)
 
 
-def back_plan(rows, n_dp):
+SEQUENCE = (
+    ("p0", "g3", "g2", "g1", "g0", "dn", "m3", "m2", "m1", "m0", "u0", "sb", "d", "go", "n1", "a10", "a11"),
+    ("u0", "u1", "qg1", "d", "u0", "o", "qb1", "o", "u1", "d", "a00", "a01", "o", "u0", "qg0", "u1", "qb0"),
+    ("u0", "q2", "q0", "fb", "q1", "u1", "q2", "q0", "s", "q1", "q2", "u1", "s", "q1", "o", "q0", "q2", "q1"),
+    ("o", "u0", "s", "q2", "q0", "q1", "q0", "q2", "d", "u1", "o", "ig", "s", "q1", "q0"),
+)
+SWAPPED = ("q0", "q2")
+
+
+def back_plan(rows, n_dp, swapped):
     plan = []
     ks = powers(n_dp)
+    if swapped and len(ks) > 2:
+        ks = [ks[1], ks[0]] + ks[2:]
     size = rows
     for k in ks:
         if k != ks[-1] and size % 32 == 0:
@@ -616,13 +722,13 @@
 
 
 class Sum:
-    def __init__(self, view, rows, base, places, bufs, sems, n_dp):
+    def __init__(self, view, rows, base, places, bufs, sems, n_dp, swapped):
         self.view, self.rows, self.base = view, rows, base
         self.core, self.xdev, self.dpdev, self.bit = places
         self.rc, self.rx, self.rd, result = bufs
         self.res = result.at[pl.ds(base, rows)]
         self.sems = sems
-        self.plan = back_plan(rows, n_dp)
+        self.plan = back_plan(rows, n_dp, swapped)
         self.cps = {}
 
     def go(self, key, src, dst, dev):
@@ -652,6 +758,13 @@
         self.off = 0
         self.level = 0
         self.stack = []
+        self.start_level()
+
+    def begin_halved(self):
+        k, _, size = self.plan[0]
+        self.off = self.bit(k) * size
+        self.stack = [(k, size, self.off)]
+        self.level = 1
         self.start_level()
 
     def start_level(self):
@@ -694,9 +807,10 @@
         self.stack.pop()
         self.start_back()
 
-    def steps(self):
-        yield self.merge_x()
-        for _ in self.plan:
+    def steps(self, halved=False):
+        if not halved:
+            yield self.merge_x()
+        for _ in self.plan[1 if halved else 0 :]:
             yield self.merge_level()
         for _ in [p for p in self.plan if p[1]]:
             yield self.merge_back()
@@ -705,10 +819,10 @@
 def back_kernel(
     n_dp,
     rows,
-    x_hbm, wq_hbm, wo_hbm, wu_hbm, wd_hbm, qkv_hbm, mix_hbm, hid_hbm, gp_hbm, sv_hbm, rg_ref, vec_ref,
-    ig_out, g_out, gd_out, sm_out, sa, ra,
-    xv, wq, wo, wu, wd, qkv, mix, hid, gp, nv, nt_buf, acc, hl, mg, igv, low, ag,
-    gq, go_, gu, rc, rx, rd0, rd1, rd2, result, stage_s, stage_r, gd, pk, pr, pd,
+    x_hbm, wq_hbm, wo_hbm, wu_hbm, wd_hbm, qkv_hbm, mix_hbm, hid_hbm, gp_hbm, sv_hbm, g1_hbm, s1_hbm, g2_hbm, s2_hbm, rg_ref,
+    ig_out, g_out, sm_out,
+    xv, vec_ref, wq, wo, wu, wd, qkv, mix, hid, gp, nv, nt_buf, acc, hl, mg, igv, low, ag,
+    gq, go_, gu, rc, rx, rd0, rd1, rd2, result, sa, ra, gd, pk, pr, pd,
     ss, rs, ig_ss, ig_rs, s_ss, s_rs, r_ss, r_rs, m_ss, m_rs, l_sem, o_sem,
 ):
     dp = lax.axis_index("dp")
@@ -735,6 +849,8 @@
         for key in keys:
             loads[key].wait()
 
+    for i, v in enumerate((g1_hbm, s1_hbm, g2_hbm, s2_hbm)):
+        load(("vec", i), v, vec_ref.at[i])
     load("hid", hid_hbm, hid)
     for s in (3, 2, 1, 0):
         load(("wd", s), wd_hbm.at[s], wd.at[s])
@@ -751,32 +867,41 @@
     load("r0", low, ra.at[0, 0, 0])
     pl.semaphore_wait(bar, len(greet))
 
+    bit0 = lax.rem(dp, 2)
+    f_cut = gd.shape[0] // 2
+    other = pl.ds(pl.multiple_of((1 - bit0) * f_cut, 128), f_cut)
+    ydev = (flip(dp, 1), mp)
     s_first = [
         remote(sv_hbm.at[k], sa.at[k % 2, 0, k // 2], s_ss.at[k - 1], s_rs.at[k - 1], dev)
         for k, dev in ((1, core), (2, xdev), (3, diag))
     ]
     r_first = remote(low, ra.at[0, 0, 1], r_ss.at[0], r_rs.at[0], xdev)
+    s_y = remote(sa.at[:, 0, :, :, other], sa.at[:, 1, :, :, other], s_ss.at[3], s_rs.at[3], ydev)
+    r_y = remote(ra.at[0, 0], ra.at[0, 1], r_ss.at[1], r_rs.at[1], ydev)
+    r_core = remote(ra.at[0], ra.at[1], r_ss.at[2], r_rs.at[2], core)
     for c in s_first + [r_first]:
         c.start()
-    s_copies, r_copies = [s_first], [[r_first]]
-
-    def share(j):
-        if j == 0:
-            ready("s0", "r0")
-        for c in s_copies[-1] + r_copies[-1]:
-            c.wait_recv()
-        if j < len(dps):
-            k = dps[j]
-            dev = (flip(dp, k), mp)
-            s_copies.append([remote(sa.at[:, 0:k], sa.at[:, k : 2 * k], s_ss.at[3 + j], s_rs.at[3 + j], dev)])
-            r_copies.append([remote(ra.at[0, 0:k], ra.at[0, k : 2 * k], r_ss.at[1 + j], r_rs.at[1 + j], dev)])
-            s_copies[-1][0].start()
-            r_copies[-1][0].start()
-        elif j == len(dps):
-            n = 1 + len(dps)
-            r_copies.append([remote(ra.at[0], ra.at[1], r_ss.at[n], r_rs.at[n], core)])
-            s_copies.append([])
-            r_copies[-1][0].start()
+
+    def share_y():
+        ready("s0", "r0")
+        for c in s_first + [r_first]:
+            c.wait()
+        s_y.start()
+        r_y.start()
+
+    def share_core():
+        r_y.wait()
+        r_core.start()
+
+    def down_grad():
+        s_y.wait()
+        r_core.wait()
+        n = 8 * caps
+        mine = pl.ds(pl.multiple_of(bit0 * f_cut, 128), f_cut)
+        st = sa[:, :, :, :, mine].reshape(n, f_cut).T
+        rows_at = pl.ds(pl.multiple_of(bit0 * f_cut, 16), f_cut)
+        gd[rows_at] = nn(st, ra[...].reshape(n, D)).astype(BF16)
+        sum_d.begin_halved()
 
     outs = []
 
@@ -788,22 +913,28 @@
     number = [0]
     places = (core, xdev, lambda k: (flip(dp, k), mp), lambda k: lax.rem(lax.div(dp, k), 2))
     rds = (rd0, rd1) + tuple([rd2.at[i] for i in range(rd2.shape[0])])
-    make = lambda view, n, base: Sum(view, n, base, places, (rc, rx, rds, result), (ss, rs, number), n_dp)
     u_rows, o_rows, q_rows = gu.shape[1], go_.shape[2], gq.shape[3]
+
+    def make(name, view, n, base):
+        return Sum(view, n, base, places, (rc, rx, rds, result), (ss, rs, number), n_dp, name in SWAPPED)
+
     u_cut = u_rows // 2
-    sum_u = [make(lambda s, i=i: gu.at[s, pl.ds(i * u_cut, u_cut)], u_cut, i * u_cut) for i in range(2)]
-    sum_o = make(lambda s: go_.at[s // 2, s % 2], o_rows, u_rows)
+    sum_u = [
+        make("u%d" % i, lambda s, i=i: gu.at[s, pl.ds(i * u_cut, u_cut)], u_cut, i * u_cut) for i in range(2)
+    ]
+    sum_o = make("o", lambda s: go_.at[s // 2, s % 2], o_rows, u_rows)
     sum_q = [
-        make(lambda s, n=n: gq.at[s // 2, n, s % 2], q_rows, u_rows + o_rows + n * q_rows) for n in range(3)
+        make("q%d" % n, lambda s, n=n: gq.at[s // 2, n, s % 2], q_rows, u_rows + o_rows + n * q_rows)
+        for n in range(3)
     ]
-
-    g1, s1 = vec_ref[0:1], vec_ref[1:2]
-    g2, s2 = vec_ref[3:4], vec_ref[4:5]
+    sum_d = make("d", lambda s: gd, gd.shape[0], u_rows + o_rows + 3 * q_rows)
+
+    for i in range(4):
+        ready(("vec", i))
+    g1, s1, g2, s2 = vec_ref[0:1], vec_ref[1:2], vec_ref[2:3], vec_ref[3:4]
     step = 128
     pk[...] = jnp.zeros_like(pk)
     pk[0, 5:6] = jnp.sum(rg_ref[...], axis=0, keepdims=True) * float(SEQ)
-
-    ready("hid")
 
     def norm_again(i, carry):
         r = pl.ds(pl.multiple_of(i * step, step), step)
@@ -812,7 +943,6 @@
         nt_buf[:, r] = n.T
         return carry
 
-    lax.fori_loop(0, rows // step, norm_again, 0)
     tile = 256
 
     def mlp_grad(s):
@@ -849,25 +979,6 @@
             return carry
 
         lax.fori_loop(0, D // tile, one, 0)
-
-    mlp_grad(3)
-    for t in sum_u:
-        t.send_core(3)
-    mlp_grad(2)
-    for t in sum_u:
-        t.merge_core(2)
-        t.send_x()
-    share(0)
-    mlp_grad(1)
-    for t in sum_u:
-        t.send_core(1)
-    mlp_grad(0)
-    share(1)
-    for t in sum_u:
-        t.merge_core(0)
-    for s in (3, 2, 1, 0):
-        mlp_back(s, s == 3)
-    share(2)
 
     def second_back(i, carry):
         r = pl.ds(pl.multiple_of(i * step, step), step)
@@ -886,23 +997,21 @@
         pk[0, 2:3] += jnp.sum(h, axis=0, keepdims=True)
         return carry
 
-    lax.fori_loop(0, rows // step, second_back, 0)
-
     width = 2 * o_rows
     blocks = width // 128
-    ready("mix", "wo")
-    for p in (1, 0):
-        mt = mix[p].T
-        g = nn(mt, hl[...]).astype(BF16)
-        go_[p, 0] = g[:o_rows]
-        go_[p, 1] = g[o_rows:]
-        sum_o.send_core(2 * p + 1)
-        mg[p] = nt(hl[...], wo[p].reshape(width, D)).astype(BF16)
-    sum_o.merge_core(2)
-    sum_o.send_x()
-    sum_o.merge_core(0)
-
-    ready("qkv", "x", "wq")
+
+    def out_grad():
+        ready("mix", "wo")
+        for p in (1, 0):
+            mt = mix[p].T
+            g = nn(mt, hl[...]).astype(BF16)
+            go_[p, 0] = g[:o_rows]
+            go_[p, 1] = g[o_rows:]
+            sum_o.send_core(2 * p + 1)
+            mg[p] = nt(hl[...], wo[p].reshape(width, D)).astype(BF16)
+        sum_o.merge_core(2)
+        sum_o.send_x()
+        sum_o.merge_core(0)
 
     def first_again(i, carry):
         r = pl.ds(pl.multiple_of(i * step, step), step)
@@ -910,11 +1019,12 @@
         nv[r] = (xhat * g1 + s1).astype(BF16)
         return carry
 
-    lax.fori_loop(0, rows // step, first_again, 0)
     first = head_masks()
     same = seq_mask()
 
-    def attend_back(p):
+    def attend_back(p, part):
+        turns = rows // 128 // 2
+
         def chunk(i, carry):
             r = pl.ds(pl.multiple_of(i * 128, 128), 128)
             for j in range(blocks):
@@ -939,7 +1049,9 @@
                 qkv[p, 2, r, c] = jnp.where(first, dv[:128], dv[128:]).astype(BF16)
             return carry
 
-        lax.fori_loop(0, rows // 128, chunk, 0)
+        lax.fori_loop(part * turns, (part + 1) * turns, chunk, 0)
+        if part == 0:
+            return
         for n, at in ((0, 0), (2, width)):
             t = jnp.sum(qkv[p, n].astype(F32), axis=0, keepdims=True)
             for k in (2 * p, 2 * p + 1):
@@ -965,26 +1077,6 @@
             return carry
 
         lax.fori_loop(0, D // tile, one, 0)
-
-    queue = [t.steps() for t in sum_u]
-    attend_back(1)
-    next(queue[0])
-    qkv_grad(1)
-    for t in sum_q:
-        t.merge_core(2)
-        t.send_x()
-    next(queue[0])
-    qkv_back(1, True)
-    next(queue[1])
-    next(queue[0])
-    attend_back(0)
-    next(queue[1])
-    qkv_grad(0)
-    next(queue[0])
-    next(queue[1])
-    qkv_back(0, False)
-    for t in sum_q:
-        t.merge_core(0)
 
     def first_back(i, carry):
         r = pl.ds(pl.multiple_of(i * step, step), step)
@@ -999,53 +1091,29 @@
         pk[0, 1:2] += jnp.sum(g, axis=0, keepdims=True)
         return carry
 
-    lax.fori_loop(0, rows // step, first_back, 0)
-    for k in (1, 2, 3):
-        pk[k, 0:6] = pk[0, 0:6]
     small = [
         remote(pk.at[k], pr.at[k - 1], m_ss.at[k - 1], m_rs.at[k - 1], dev)
         for k, dev in ((1, core), (2, xdev), (3, diag))
     ]
-    for c in small:
-        c.start()
     own = pl.ds(mp * rows, rows)
+    far = pl.ds(flip(mp, 2) * rows, rows)
     ig = [
         remote(igv, ig_out.at[own], ig_ss.at[0], ig_rs.at[0], core),
         remote(igv, ig_out.at[own], ig_ss.at[1], ig_rs.at[1], xdev),
+        remote(ig_out.at[far], ig_out.at[far], ig_ss.at[2], ig_rs.at[2], core),
     ]
-    for c in ig:
-        c.start()
-    put(igv, ig_out.at[own])
-
-    share(3)
-    queue.append(sum_o.steps())
-    queue.extend(t.steps() for t in sum_q)
-
-    for j in range(4, len(dps) + 1):
-        share(j)
-    for c in r_copies[-1]:
-        c.wait_recv()
-    group = min(n_dp, 8)
-    for blk in range(n_dp // group):
-        cut = pl.ds(blk * group, group)
-        pair = [
-            pltpu.make_async_copy(sa.at[:, cut], stage_s, l_sem.at[0]),
-            pltpu.make_async_copy(ra.at[:, cut], stage_r, l_sem.at[1]),
-        ]
-        for c in pair:
+
+    def leave():
+        lax.fori_loop(0, rows // step, first_back, 0)
+        for k in (1, 2, 3):
+            pk[k, 0:6] = pk[0, 0:6]
+        for c in small + ig[:2]:
             c.start()
-        for c in pair:
-            c.wait()
-        n = 4 * group * caps
-        st = stage_s[...].reshape(n, D).T
-        for j in range(D // tile):
-            c = slice(j * tile, (j + 1) * tile)
-            t = nn(st, stage_r[..., c].reshape(n, tile))
-            if blk == 0:
-                gd[:, c] = t
-            else:
-                gd[:, c] += t
-    put(gd, gd_out)
+        put(igv, ig_out.at[own])
+
+    def pass_on():
+        ig[1].wait()
+        ig[2].start()
 
     def small_steps():
         for c in small:
@@ -1067,62 +1135,117 @@
         put(pd.at[m], sm_out)
         yield
 
-    queue.append(small_steps())
-    live = list(queue)
+    def piece_g3():
+        mlp_grad(3)
+        for t in sum_u:
+            t.send_core(3)
+
+    def piece_g2():
+        mlp_grad(2)
+        for t in sum_u:
+            t.merge_core(2)
+            t.send_x()
+        share_y()
+
+    def piece_g1():
+        mlp_grad(1)
+        for t in sum_u:
+            t.send_core(1)
+        share_core()
+
+    def piece_g0():
+        mlp_grad(0)
+        for t in sum_u:
+            t.merge_core(0)
+
+    def piece_qg1():
+        qkv_grad(1)
+        for t in sum_q:
+            t.merge_core(2)
+            t.send_x()
+
+    def piece_qb0():
+        qkv_back(0, False)
+        for t in sum_q:
+            t.merge_core(0)
+
+    def loop(body, *need):
+        ready(*need)
+        lax.fori_loop(0, rows // step, body, 0)
+
+    pieces = {
+        "p0": lambda: loop(norm_again, "hid"),
+        "g3": piece_g3,
+        "g2": piece_g2,
+        "g1": piece_g1,
+        "g0": piece_g0,
+        "dn": down_grad,
+        "m3": lambda: mlp_back(3, True),
+        "m2": lambda: mlp_back(2, False),
+        "m1": lambda: mlp_back(1, False),
+        "m0": lambda: mlp_back(0, False),
+        "sb": lambda: loop(second_back),
+        "go": out_grad,
+        "n1": lambda: loop(first_again, "qkv", "x", "wq"),
+        "a10": lambda: attend_back(1, 0),
+        "a11": lambda: attend_back(1, 1),
+        "qg1": piece_qg1,
+        "qb1": lambda: qkv_back(1, True),
+        "a00": lambda: attend_back(0, 0),
+        "a01": lambda: attend_back(0, 1),
+        "qg0": lambda: qkv_grad(0),
+        "qb0": piece_qb0,
+        "fb": leave,
+        "ig": pass_on,
+    }
+    sums = {"u0": sum_u[0].steps(), "u1": sum_u[1].steps(), "o": sum_o.steps(), "d": sum_d.steps(True)}
+    for n in range(3):
+        sums["q%d" % n] = sum_q[n].steps()
+    sums["s"] = small_steps()
+    for line in SEQUENCE:
+        for token in line:
+            if token in pieces:
+                pieces[token]()
+            else:
+                next(sums[token], None)
+    live = list(sums.values())
     while live:
-        left = []
-        for g in live:
-            try:
-                next(g)
-                left.append(g)
-            except StopIteration:
-                pass
-        live = left
+        live = [g for g in live if next(g, live) is not live]
     put(result, g_out)
 
-    ig[1].wait()
-    far = pl.ds(flip(mp, 2) * rows, rows)
-    last = remote(ig_out.at[far], ig_out.at[far], ig_ss.at[2], ig_rs.at[2], core)
-    last.start()
     ig[0].wait()
-    last.wait()
-    for group_ in s_copies + r_copies:
-        for c in group_:
-            c.wait_send()
+    ig[2].wait()
     for c in outs:
         c.wait()
 
 
-def run_backward(n_dp, rows, tokens, wq, wo, wu, wd, qkv, mix, hid, gp, sv, rg, vec):
+def run_backward(n_dp, rows, tokens, wq, wo, wu, wd, qkv, mix, hid, gp, sv, gains, rg):
     caps = rows // SEQ
     sds = jax.ShapeDtypeStruct
     q_rows = wq.shape[3]
     o_rows = wo.shape[2]
     u_rows = wu.shape[1]
-    total = u_rows + o_rows + 3 * q_rows
+    total = u_rows + o_rows + 3 * q_rows + wd.shape[1]
     width = 2 * q_rows
     n_pow = len(powers(n_dp))
     outs = [
         sds(tokens.shape, BF16),
         sds((total, D), BF16),
-        sds(wd.shape[1:], F32),
         sds((16, D), F32),
-        sds((2, n_dp, 2, caps, D), BF16),
-        sds((2, n_dp, 2, caps, D), BF16),
     ]
-    group = min(n_dp, 8)
     any_spec = pl.BlockSpec(memory_space=pl.ANY)
     vmem = pl.BlockSpec(memory_space=pltpu.VMEM)
     vm = lambda s: pltpu.VMEM(s.shape, s.dtype)
     sem = lambda n: pltpu.SemaphoreType.DMA((n,))
-    n_sum = 6 * (3 + 2 * n_pow)
+    n_sum = 7 * (3 + 2 * n_pow)
     return pl.pallas_call(
         functools.partial(back_kernel, n_dp, rows),
         out_shape=outs,
-        in_specs=[any_spec] * 10 + [vmem] * 2,
+        in_specs=[any_spec] * 14 + [vmem],
         out_specs=[any_spec] * len(outs),
         scratch_shapes=[
             pltpu.VMEM((rows, D), BF16),
+            pltpu.VMEM((8, D), F32),
             vm(wq), vm(wo), vm(wu), vm(wd), vm(qkv), vm(mix), vm(hid), vm(gp),
             pltpu.VMEM((rows, D), BF16),
             pltpu.VMEM((D, rows), BF16),
@@ -1139,20 +1262,20 @@
             pltpu.VMEM((total // 4, D), BF16),
             pltpu.VMEM((max(1, n_pow - 2), total // 4, D), BF16),
             pltpu.VMEM((total, D), BF16),
-            pltpu.VMEM((2, group, 2, caps, D), BF16),
-            pltpu.VMEM((2, group, 2, caps, D), BF16),
-            pltpu.VMEM(wd.shape[1:], F32),
+            pltpu.VMEM((2, 2, 2, caps, D), BF16),
+            pltpu.VMEM((2, 2, 2, caps, D), BF16),
+            pltpu.VMEM(wd.shape[1:], BF16),
             pltpu.VMEM((4, 16, D), F32),
             pltpu.VMEM((3, 16, D), F32),
             pltpu.VMEM((2 * n_pow + 1, 16, D), F32),
-            sem(n_sum), sem(n_sum), sem(3), sem(3), sem(3 + n_pow), sem(3 + n_pow),
-            sem(2 + n_pow), sem(2 + n_pow), sem(3 + n_pow), sem(3 + n_pow), sem(20), sem(4),
+            sem(n_sum), sem(n_sum), sem(3), sem(3), sem(4), sem(4),
+            sem(3), sem(3), sem(3 + n_pow), sem(3 + n_pow), sem(24), sem(3),
         ],
         compiler_params=pltpu.CompilerParams(
             collective_id=2, has_side_effects=True, vmem_limit_bytes=62 * 2**20
         ),
         name="backward",
-    )(tokens, wq, wo, wu, wd, qkv, mix, hid, gp, sv, rg, vec)
+    )(tokens, wq, wo, wu, wd, qkv, mix, hid, gp, sv, *gains, rg)
 
 
 def solution(mesh):
@@ -1163,49 +1286,30 @@
         w_up, up_bias, w_down, down_bias, images, image_group, pair_shard, pair_row,
     ):
         rows = tokens.shape[0] // n_mp
-        per_dp = pair_row.shape[0]
-        dp = lax.axis_index("dp")
-        mp = lax.axis_index("mp")
         wq_t = jnp.transpose(w_qkv, (0, 2, 1))
         q_rows = wq_t.shape[1]
-        zero = jnp.zeros((q_rows,), F32)
-        tail = jnp.zeros((D - 2 * q_rows,), F32)
-        lines = [up_bias]
-        for n in range(2):
-            lines.append(jnp.concatenate([qv_bias[n], zero, tail]))
-            lines.append(jnp.concatenate([zero, qv_bias[n], tail]))
-        bi = jnp.stack(lines + [jnp.zeros((D,), F32)] * 3)
-        vec = jnp.stack(
-            [ln1_gain, ln1_bias, out_bias, ln2_gain, ln2_bias, down_bias, jnp.zeros((D,), F32), jnp.zeros((D,), F32)]
+        (wq, wo, wu, wd, _, image_low, temps, qkv, mix, hid, gp, sv, text, pooled) = run_forward(
+            n_dp,
+            rows,
+            (
+                tokens, wq_t, w_out, w_up, w_down, up_bias, qv_bias, ln1_gain, ln1_bias, out_bias, ln2_gain,
+                ln2_bias, down_bias, images, image_group, pair_shard, pair_row,
+            ),
         )
-        n_img = images.shape[0]
-        index = pair_shard[:, 0] * n_img + pair_row
-        info = jnp.concatenate([index, image_group]).reshape(-1, 128)
-        info = jnp.pad(info, ((0, -info.shape[0] % 8), (0, 0)))
-        (wq, wo, wu, wd, imgs, infos, qkv, mix, hid, gp, sv, text, pooled) = run_forward(
-            n_dp, rows, tokens, wq_t, w_out, w_up, w_down, bi, images, info, vec
-        )
-        every = lax.bitwise_xor(jnp.arange(n_dp, dtype=jnp.int32), dp)
-        flat = infos.reshape(n_dp, -1)[every]
-        index = flat[:, :per_dp].reshape(-1)
-        group = flat[:, per_dp : per_dp + n_img].reshape(-1)
-        place = lax.bitwise_xor(index // n_img, dp) * n_img + index % n_img
-        raw = imgs.reshape(n_dp * n_img, D)[place].astype(F32)
-        image_low = (raw * lax.rsqrt(jnp.sum(raw * raw, axis=-1, keepdims=True) + 1e-06)).astype(BF16)
-        temps = jnp.where(group[index] == 1, 64.0, 40.0).astype(F32)[None, :]
         rg, loss = run_pairs(n_dp, n_mp, pooled, image_low, temps)
-        ig, grads, wd_g, small, _, _ = run_backward(
-            n_dp, rows, tokens, wq, wo, wu, wd, qkv, mix, hid, gp, sv, rg, vec
+        ig, grads, small = run_backward(
+            n_dp, rows, tokens, wq, wo, wu, wd, qkv, mix, hid, gp, sv, (ln1_gain, ln1_bias, ln2_gain, ln2_bias), rg
         )
         cuts = [w_up.shape[0], w_up.shape[0] + w_out.shape[0]]
         wu_g, wo_g = grads[: cuts[0]], grads[cuts[0] : cuts[1]]
-        wq_g = grads[cuts[1] :].reshape(3, q_rows, D)
+        cuts.append(cuts[1] + 3 * q_rows)
+        wq_g, wd_g = grads[cuts[1] : cuts[2]].reshape(3, q_rows, D), grads[cuts[2] :]
         text_out = lax.all_gather(text, "mp", axis=0, tiled=True)
         qb = small[7].reshape(2, 2 * q_rows)[:, :q_rows] + small[8].reshape(2, 2 * q_rows)[:, q_rows:]
         return (
             text_out, ig, loss[:, 0],
             small[0], small[1], jnp.transpose(wq_g, (0, 2, 1)).astype(F32), qb, wo_g.astype(F32), small[2],
-            small[3], small[4], wu_g.astype(F32), small[6], wd_g, small[5],
+            small[3], small[4], wu_g.astype(F32), small[6], wd_g.astype(F32), small[5],
         )
 
     in_specs = (

time: 308 us -> 233 us (0.76)
  Pallas kernels: 250 us -> 202 us
  local copies, waits for them, and re-layouts: 33.6 us -> 10.7 us
    pallas_call x1, Pallas kernels: 166 us -> 108 us  [run_backward(): pl.pallas_call(functools.partial(back_kernel, n_dp, rows), out_shape=outs...]
    gather x3 -> x0, local copies, waits for them, and re-layouts: 13.5 us -> none  [the longest x1 6.77 us: body(): raw = imgs.reshape(n_dp * n_img, D)[place].astype(F32)]
    pallas_call x1, Pallas kernels: 68.2 us -> 78.2 us  [run_forward(): pl.pallas_call(functools.partial(fwd_kernel, n_dp, rows), out_shape=outs,...]
    another operation x15 -> x0, local copies, waits for them, and re-layouts: 6.14 us -> none  [the longest x7 4.78 us: body(): jnp.stack([ln1_gain, ln1_bias, out_bias, ln2_gain, ln2_bias, down_bias, j...]
    unnamed x14 -> x9, local copies, waits for them, and re-layouts: 8.9 us -> 6.97 us
  transfers between devices with their start and end apart: 1 -> 1, of which waited for: 0 -> 0; matrix products, arithmetic and copies ran while one was open for 8% -> 4% of each run, Pallas kernels for 59% -> 53%
where the time goes in v2:
time: 233 us
  Pallas kernels  202 us (87%)
  between operations  14.1 us (6%)
  local copies, waits for them, and re-layouts  10.7 us (5%)
  other arithmetic  6.36 us (3%)
    pallas_call x1, Pallas kernels, run_backward(): pl.pallas_call(functools.partial(back_kernel, n_dp, rows), out_shape=outs...  108 us
    pallas_call x1, Pallas kernels, run_forward(): pl.pallas_call(functools.partial(fwd_kernel, n_dp, rows), out_shape=outs,...  78.2 us
    pallas_call x1, Pallas kernels, run_pairs(): pl.pallas_call(functools.partial(pair_kernel, n_dp, n_mp), out_shape=[jax...  15.5 us
    unnamed x9, local copies, waits for them, and re-layouts  6.97 us
  transfers between devices with their start and end apart: 1, of which 0 were waited for; matrix products, arithmetic and copies ran while one was open for 4% of the time, Pallas kernels for 53%

profile of v2, /device:TPU:0, one launch (start us, length us, event | category | flops | bytes accessed | tf_op | source)
XLA Modules:
  0.0 233.1 jit_solution(12397567828291269747)
XLA Ops:
  7.2 0.0 all-gather.2.cloned.1.call-start
  7.2 1.4 copy.33.shard_hbm
  8.6 78.2 %forward.1 = (bf16[2,3,2,192,768]{4,3,2,1,0:T(8,128)(2,1)}, bf16[2,2,192,768]{3,2,1,0:T(8,128)(2,1)}, bf16[4,768,768]{2,1,0:T(8,128)(2,1)}, bf16[4,768,768]{2,1,...) custom-call(bf16[2048,768]{1,0:T(8,128)(2,1)} %x_hbm.3, ...), custom_call_target="tpu_custom_call" | custom-call | tf_op jit(solution)/shard_map/forward/pallas_call | solution.py:547
  86.8 0.0 all-gather.2.cloned.1.call-update
  86.9 15.5 %contrast.1 = (f32[32,768]{1,0:T(8,128)}, f32[128,128]{1,0:T(8,128)}) custom-call(f32[32,768]{1,0:T(8,128)} %get-tuple-element.43.pool_ref, bf16[1024,768]{1,0:T(8,128)(2,1)} %get-tuple-element.44.image_ref, f32[1,1024]{1,0:T(1,128)} %get-tuple-element.45.temp_ref), custom_call_target="tpu_custom_call" | custom-call | tf_op jit(solution)/shard_map/contrast/pallas_call | solution.py:669
  102.4 0.0 copy-start.2
  102.4 108.1 %backward.1 = (bf16[2048,768]{1,0:T(8,128)(2,1)}, bf16[2304,768]{1,0:T(8,128)(2,1)}, f32[16,768]{1,0:T(8,128)}) custom-call(bf16[2048,768]{1,0:T(8,128)(2,1)} %x_hbm.3, bf16[2,3,2,192,768]{4,3,2,1,0:T(8,128)(2,1)} %get-tuple-element.34.wq_hbm, bf16[2,2,192,768]{3,2,1,0:T(8,128)(2,1)} %get-tuple-element.35.wo_hbm, ...), custom_call_target="tpu_custom_call" | custom-call | tf_op jit(solution)/shard_map/backward/pallas_call | solution.py:1241
  210.5 1.7 slice_reduce_fusion.1
  212.3 0.0 copy-start
  212.3 1.4 slice.51
  213.7 0.0 copy-done.2
  213.7 0.6 slice_reduce_fusion
  214.3 0.7 slice_add_fusion
  214.9 1.8 slice_convert_fusion.2
  216.8 1.3 convert_bitcast_fusion
  218.1 0.0 copy-done
  218.1 2.5 %slice_convert_fusion = (f32[768,768]{1,0:T(8,128)}, f32[768,768]{1,0:T(8,128)}) fusion(bf16[2304,768]{1,0:T(8,128)(2,1)S(1)} %copy-done), kind=kLoop, calls=%fused_computation.1 | loop fusion | flops 1179648 | bytes 7077888 | tf_op jit(solution)/shard_map/convert_element_type | solution.py:1312
  220.7 0.0 all-gather.2.cloned.1.call-done
  220.7 0.0 copy-start.1
  220.7 3.9 %copy.36 = bf16[2048,768]{1,0:T(8,128)(2,1)} copy(bf16[2048,768]{1,0:T(8,128)(2,1)} %all-gather.2.cloned.1.call-done) | data formatting | bytes 6291456
  224.6 0.0 copy-done.1
  224.6 1.7 copy.37
  (2 shorter events, 0.0 us)
Async XLA Ops:
  7.2 213.5 %all-gather.2.cloned.1.call-start = ((), (), s32[]{:S(2)}) async-start(), calls=%async_computation | async-start | bytes 3932160 | tf_op jit(solution)/shard_map/all_gather | solution.py:1307
  102.4 111.3 %copy-start.2 = (f32[128,128]{1,0:T(8,128)S(1)}, f32[128,128]{1,0:T(8,128)}, u32[]{:S(2)}) copy-start(f32[128,128]{1,0:T(8,128)} %get-tuple-element.48) | copy-start | bytes 196612
  212.3 5.8 %copy-start = (bf16[2304,768]{1,0:T(8,128)(2,1)S(1)}, bf16[2304,768]{1,0:T(8,128)(2,1)}, u32[]{:S(2)}) copy-start(bf16[2304,768]{1,0:T(8,128)(2,1)} %get-tuple-element.50) | copy-start | bytes 10616836
  220.7 3.9 %copy-start.1 = (bf16[2048,768]{1,0:T(8,128)(2,1)S(1)}, bf16[2048,768]{1,0:T(8,128)(2,1)}, u32[]{:S(2)}) copy-start(bf16[2048,768]{1,0:T(8,128)(2,1)} %get-tuple-element.78) | copy-start | bytes 9437188
Sparse Core Ops, SparseCore 0:
  87.0 33.5 all-gather.1

commit v3 on v2

--- a/solution.py
+++ b/solution.py
@@ -29,6 +29,13 @@
 
 def flip(index, k):
     return index + k - 2 * k * lax.rem(lax.div(index, k), 2)
+
+
+def both(a, b, n):
+    out = a + b
+    for k in powers(n):
+        out = out - 2 * k * lax.rem(lax.div(a, k), 2) * ((b // k) % 2)
+    return out
 
 
 def powers(n):
@@ -98,9 +105,9 @@
     rows,
     x_hbm, wq_hbm, wo_hbm, wu_hbm, wd_hbm, ub_hbm, qv_hbm, g1_hbm, s1_hbm, ob_hbm, g2_hbm, s2_hbm, db_hbm,
     img_hbm, group_hbm, shard_hbm, row_hbm,
-    wq_out, wo_out, wu_out, wd_out, imgs, low_out, temp_out, qkv_out, mix_out, hid_out, gp_out, s_out, text_out,
+    wq_out, wo_out, wu_out, wd_out, imgs_out, low_out, temp_out, qkv_out, mix_out, hid_out, gp_out, s_out, text_out,
     pool_out,
-    xv, wq, wo, wu, wd, bi, qv, vec_ref, ints, shard, info, stage, hot, unit, temp, n1, qkv, mix, hid, n2, gp, act,
+    xv, wq, wo, wu, wd, bi, qv, vec_ref, ints, shard, info, stage, hot, unit, temp, total_rows, n1, qkv, mix, hid, n2, gp, act,
     acc, sv, pool,
     w_ss, w_rs, b_ss, b_rs, i_ss, i_rs, l_sem, p_sem, o_sem, u_sem,
 ):
@@ -112,12 +119,18 @@
     diag = (dp, flip(flip(mp, 1), 2))
     ydev = (flip(dp, 1), mp)
     dps = powers(n_dp)
+    imgs = stage if n_dp == stage.shape[0] else imgs_out
+
+    relay = n_dp == 8
+    bit1, bit2 = lax.rem(lax.div(dp, 2), 2), lax.rem(lax.div(dp, 4), 2)
+    inner = bit1 + bit2 == 1
+    across = (flip(flip(dp, 2), 4), mp)
+    outward = (dp - 2 + 4 * bit2, mp)
 
     bar = pltpu.get_barrier_semaphore()
-    greet = [core, xdev, diag] + [(flip(dp, k), mp) for k in dps]
+    greet = [core, xdev, diag] + [(flip(dp, k), mp) for k in dps] + ([across] if relay else [])
     for dev in greet:
         pl.semaphore_signal(bar, inc=1, device_id=dev, device_id_type=MESH)
-
     local = [
         pltpu.make_async_copy(x_hbm.at[pl.ds(mp * rows, rows)], xv, l_sem.at[0]),
         pltpu.make_async_copy(wq_hbm, wq.at[0, :, 0], l_sem.at[1]),
@@ -135,10 +148,75 @@
     lines = [pltpu.make_async_copy(a, b_, p_sem.at[i]) for i, (a, b_) in enumerate(lines)]
     for c in lines[:early] + local + lines[early:]:
         c.start()
+    pl.semaphore_wait(bar, len(greet))
+    q_rows = wq_hbm.shape[1]
+    width = 2 * q_rows
+    o_rows = wo_hbm.shape[0]
+    u_rows = wu_hbm.shape[0]
+    d_rows = wd_hbm.shape[0]
+
+    def half(total, cuts, part, which):
+        size = total // 2 // cuts
+        return pl.ds(which * (total // 2) + part * size, size)
+
+    def src_q(cut):
+        return wq_hbm.at[:, cut]
+
+    def src_o(cut):
+        return wo_hbm.at[cut]
+
+    def src_u(cut):
+        return wu_hbm.at[cut]
+
+    def src_d(cut):
+        return wd_hbm.at[cut]
+
+    def at_q(s, cut):
+        return wq.at[s // 2, :, s % 2, cut]
+
+    def at_o(s, cut):
+        return wo.at[s // 2, s % 2, cut]
+
+    def at_u(s, cut):
+        return wu.at[s, cut]
+
+    def at_d(s, cut):
+        return wd.at[s, cut]
+
+    table = []
+    for total, cuts, src, at in (
+        (q_rows, 1, src_q, at_q),
+        (o_rows, 1, src_o, at_o),
+        (u_rows, 2, src_u, at_u),
+        (d_rows, 4, src_d, at_d),
+    ):
+        whole = pl.ds(0, total)
+        pieces = []
+        for part in range(cuts):
+            pieces.append((half(total, cuts, part, b), half(total, cuts, part, 1 - b)))
+        table.append((whole, pieces, src, at))
+
+    sent = []
+    number = [0]
+
+    def go(src, dst, dev):
+        i = number[0]
+        number[0] += 1
+        c = remote(src, dst, w_ss.at[i], w_rs.at[i], dev)
+        c.start()
+        sent.append(c)
+        return c
+
+    step_x, step_core = [], []
+
+    def send_own(w):
+        whole, pieces, src, at = table[w]
+        step_core.append(go(src(whole), at(1, whole), core))
+        step_x.append([go(src(mine), at(2, mine), xdev) for mine, _ in pieces])
+
+    send_own(0)
     for c in lines[:early]:
         c.wait()
-    q_rows = wq_hbm.shape[1]
-    width = 2 * q_rows
     wide = jnp.concatenate([qv[...], qv[...]], axis=1) if q_rows % 128 == 0 else None
     if wide is None:
         bi[0, 8:16, :width] = jnp.zeros((8, width), F32)
@@ -151,75 +229,14 @@
     info[0, 0:1] = tall[0:1] * n_img + ints[0:1]
     info[0, 1 : 1 + parts] = ints[1 : 1 + parts]
 
-    pl.semaphore_wait(bar, len(greet))
-
-    o_rows = wo_hbm.shape[0]
-    u_rows = wu_hbm.shape[0]
-    d_rows = wd_hbm.shape[0]
-
-    def half(total, parts, part, which):
-        size = total // 2 // parts
-        return pl.ds(which * (total // 2) + part * size, size)
-
-    def src_q(cut):
-        return wq_hbm.at[:, cut]
-
-    def src_o(cut):
-        return wo_hbm.at[cut]
-
-    def src_u(cut):
-        return wu_hbm.at[cut]
-
-    def src_d(cut):
-        return wd_hbm.at[cut]
-
-    def at_q(s, cut):
-        return wq.at[s // 2, :, s % 2, cut]
-
-    def at_o(s, cut):
-        return wo.at[s // 2, s % 2, cut]
-
-    def at_u(s, cut):
-        return wu.at[s, cut]
-
-    def at_d(s, cut):
-        return wd.at[s, cut]
-
-    table = []
-    for total, parts, src, at in (
-        (q_rows, 1, src_q, at_q),
-        (o_rows, 1, src_o, at_o),
-        (u_rows, 2, src_u, at_u),
-        (d_rows, 2, src_d, at_d),
-    ):
-        whole = pl.ds(0, total)
-        pieces = []
-        for part in range(parts):
-            pieces.append((half(total, parts, part, b), half(total, parts, part, 1 - b)))
-        table.append((whole, pieces, src, at))
-
-    sent = []
-    number = [0]
-
-    def go(src, dst, dev):
-        i = number[0]
-        number[0] += 1
-        c = remote(src, dst, w_ss.at[i], w_rs.at[i], dev)
-        c.start()
-        sent.append(c)
-        return c
-
     bias = [
         remote(bi.at[0, 0:8], bi.at[s, 0:8], b_ss.at[s - 1], b_rs.at[s - 1], dev)
         for s, dev in ((1, core), (2, xdev), (3, diag))
     ]
     for c in bias:
         c.start()
-
-    step_x, step_core = [], []
-    for whole, pieces, src, at in table:
-        step_core.append(go(src(whole), at(1, whole), core))
-        step_x.append([go(src(mine), at(2, mine), xdev) for mine, _ in pieces])
+    for w in range(1, 4):
+        send_own(w)
 
     i_half = img_hbm.shape[0] // 2
     own_cut = pl.ds(lax.rem(mp, 2) * i_half, i_half)
@@ -246,12 +263,53 @@
             c.start()
         img_copies.append(pair)
 
+    def relay_copies(first, moves, dev):
+        out = []
+        for i, (a, to) in enumerate(moves):
+            k = first + 2 * i
+            out.append(
+                [
+                    remote(imgs.at[a : a + 2, own_cut], imgs.at[to : to + 2, own_cut], i_ss.at[k], i_rs.at[k], dev),
+                    remote(info.at[a : a + 2], info.at[to : to + 2], i_ss.at[k + 1], i_rs.at[k + 1], dev),
+                ]
+            )
+        return out
+
+    crossing = relay_copies(4, ((0, 6), (2, 4)), across)
+    leaving = relay_copies(8, ((6, 4), (4, 6)), outward)
+
+    def image_across():
+        for c in img_copies[1]:
+            c.wait_recv()
+
+        @pl.when(inner)
+        def _():
+            for pair in crossing:
+                for c in pair:
+                    c.start()
+
+    def image_outward(part):
+        @pl.when(inner)
+        def _():
+            for c in crossing[part]:
+                c.wait_recv()
+            for c in leaving[part]:
+                c.start()
+
     def image_last():
-        if len(dps) == 1:
-            local[5].wait()
-        for c in img_copies[len(dps) - 1]:
-            c.wait_recv()
-        n = 2 * len(dps)
+        if relay:
+
+            @pl.when(bit1 + bit2 != 1)
+            def _():
+                for pair in leaving:
+                    for c in pair:
+                        c.wait_recv()
+
+            n = 12
+        else:
+            for c in img_copies[len(dps) - 1]:
+                c.wait_recv()
+            n = 2 * len(dps)
         c = remote(imgs.at[1:n_dp, own_cut], imgs.at[1:n_dp, own_cut], i_ss.at[n], i_rs.at[n], core)
         c.start()
         img_copies.append([c])
@@ -340,20 +398,25 @@
     attend(0)
     forward_x(0, 0)
     forward_x(1, 0)
-    for j in range(2, len(dps)):
-        image_step(j)
+    if relay:
+        image_across()
+    else:
+        for j in range(2, len(dps)):
+            image_step(j)
     forward_y(0, 0)
+    forward_x(2, 0)
     forward_y(1, 0)
+    if relay:
+        image_outward(0)
     bias[1].wait_recv()
     bias[2].wait_recv()
     arrived(0)
     put(wq, wq_out)
     project(1)
-    forward_x(2, 0)
+    forward_x(2, 1)
     attend(1)
     put(qkv, qkv_out)
     put(mix, mix_out)
-    forward_x(2, 1)
     local[2].wait()
     step_core[1].wait_recv()
     arrived(1)
@@ -413,75 +476,97 @@
     def fetch(block):
         return pltpu.make_async_copy(imgs.at[pl.ds(block * near, near)], stage, u_sem.at[0])
 
-    def pick_images():
-        if n_dp == near:
-            fetch(0).start()
-            fetch(0).wait()
-        for q in range(n_dp // 4):
-            raw = None
-            heat = [None] * 4
-            for block in range(n_dp // near):
-                if n_dp != near:
-                    fetch(block).start()
-                    fetch(block).wait()
-                for i in range(4):
-                    line = info[4 * q + i, 0:1]
-                    line = jnp.bitwise_xor(line >> shift, dp) * n_img + (line & (n_img - 1)) - block * table_rows
-                    col = jnp.broadcast_to(line, (128, 128)).T
-                    total = jnp.zeros((128, 128), F32)
-                    for c in range(table_rows // 128):
-                        hit = (col == lane + c * 128).astype(F32)
-                        hot[i * 128 : (i + 1) * 128, c * 128 : (c + 1) * 128] = hit.astype(BF16)
-                        of = block * near + c // parts
-                        group = info[of, 1 + c % parts : 2 + c % parts].astype(F32)
-                        total += hit * group
-                    total = jnp.broadcast_to(jnp.sum(total, axis=1, keepdims=True), (128, 128)).T[0:1]
-                    heat[i] = total if heat[i] is None else heat[i] + total
-                part = nn(hot[...], stage[...].reshape(table_rows, D))
-                raw = part if raw is None else raw + part
-            if q >= 2:
-                for c in rests[2 * 4 * (q - 2) : 2 * 4 * (q - 1)]:
-                    c.wait()
-            low = raw * lax.rsqrt(jnp.sum(raw * raw, axis=-1, keepdims=True) + 1e-06)
-            unit[q % 2] = low.astype(BF16)
+    n_block = n_dp // near
+
+    def pick_four(q):
+        def from_block(block):
             for i in range(4):
-                r = 4 * q + i
-                place = dp
-                for k in dps:
-                    if r & k:
-                        place = flip(place, k)
-                at = pl.ds(pl.multiple_of(place * 128, 128), 128)
-                temp[r] = jnp.where(heat[i] > 0.5, 64.0, 40.0)
-                rests.append(
-                    pltpu.make_async_copy(unit.at[q % 2, pl.ds(i * 128, 128)], low_out.at[at], u_sem.at[2 * r + 1])
-                )
-                rests.append(pltpu.make_async_copy(temp.at[r], temp_out.at[:, at], u_sem.at[2 * r + 2]))
-            for c in rests[-8:]:
-                c.start()
-
+                line = info[4 * q + i, 0:1]
+                line = jnp.bitwise_xor(line >> shift, dp) * n_img + (line & (n_img - 1)) - block * table_rows
+                col = jnp.broadcast_to(line, (128, 128)).T
+                total = jnp.zeros((128, 128), F32)
+                for c in range(table_rows // 128):
+                    hit = (col == lane + c * 128).astype(F32)
+                    hot[i * 128 : (i + 1) * 128, c * 128 : (c + 1) * 128] = hit.astype(BF16)
+                    total += hit * info[block * near + c // parts, 1 + c % parts : 2 + c % parts].astype(F32)
+                total = jnp.broadcast_to(jnp.sum(total, axis=1, keepdims=True), (128, 128)).T[0:1]
+                temp[4 * q + i] = total if n_block == 1 else temp[4 * q + i] + total
+            return nn(hot[...], stage[...].reshape(table_rows, D))
+
+        if n_block == 1:
+            raw = from_block(0)
+        else:
+            for i in range(4):
+                temp[4 * q + i] = jnp.zeros((1, 128), F32)
+            total_rows[...] = jnp.zeros_like(total_rows)
+
+            def more(block, carry):
+                fetch(block).start()
+                fetch(block).wait()
+                total_rows[...] += from_block(block)
+                return carry
+
+            lax.fori_loop(0, n_block, more, 0)
+            raw = total_rows[...]
+        slot = q % unit.shape[0]
+        inv = lax.rsqrt(jnp.sum(raw * raw, axis=-1, keepdims=True) + 1e-06)
+        unit[slot] = (raw * inv).astype(BF16)
+        copies = []
+        for i in range(4):
+            r = 4 * q + i
+            at = pl.ds(pl.multiple_of(both(dp, r, n_dp) * 128, 128), 128)
+            temp[r] = jnp.where(temp[r] > 0.5, 64.0, 40.0)
+            copies.append(
+                pltpu.make_async_copy(unit.at[slot, pl.ds(i * 128, 128)], low_out.at[at], u_sem.at[2 * r + 1])
+            )
+            copies.append(pltpu.make_async_copy(temp.at[r], temp_out.at[:, at], u_sem.at[2 * r + 2]))
+        for c in copies:
+            c.start()
+        return copies
+
+    def pick_many():
+        def each(q, carry):
+            for c in pick_four(q):
+                c.wait()
+            return carry
+
+        lax.fori_loop(0, n_dp // 4, each, 0)
+
+    forward_y(2, 0)
+    if relay:
+        image_outward(1)
     local[3].wait()
     up(0)
-    forward_y(2, 0)
     forward_x(3, 0)
+    forward_x(3, 1)
     step_core[2].wait_recv()
     up(1)
     forward_y(2, 1)
-    forward_x(3, 1)
+    forward_x(3, 2)
     local[4].wait()
     down(0)
     arrived(2)
     up(2)
+    forward_x(3, 3)
+    image_last()
     forward_y(3, 0)
     up(3)
     put(wu, wu_out)
     put(gp, gp_out)
     put(sv, s_out)
+    forward_y(3, 1)
     step_core[3].wait_recv()
     down(1)
-    image_last()
-    forward_y(3, 1)
+    forward_y(3, 2)
     img_copies[-1][0].wait_recv()
-    pick_images()
+    if n_block == 1:
+        rests.extend(pick_four(0))
+        forward_y(3, 3)
+        for q in range(1, n_dp // 4):
+            rests.extend(pick_four(q))
+    else:
+        forward_y(3, 3)
+        pick_many()
     arrived(3)
     put(wd, wd_out)
     down(2)
@@ -507,7 +592,15 @@
     for pair in img_copies:
         for c in pair:
             c.wait_send()
-    for c in rests[-16:]:
+    if relay:
+
+        @pl.when(inner)
+        def _():
+            for pair in crossing + leaving:
+                for c in pair:
+                    c.wait_send()
+
+    for c in rests:
         c.wait()
     for c in outs:
         c.wait()
@@ -530,7 +623,7 @@
         sds((4,) + w_down.shape, BF16),
     ]
     outs = weights + [
-        sds((n_dp,) + images.shape, BF16),
+        sds((n_dp if n_dp > near else 1,) + images.shape, BF16),
         sds((n_dp * per_dp, D), BF16),
         sds((1, n_dp * per_dp), F32),
         sds((2, 3, rows, width), BF16),
@@ -543,7 +636,7 @@
     ]
     any_spec = pl.BlockSpec(memory_space=pl.ANY)
     vm = lambda s: pltpu.VMEM(s.shape, s.dtype)
-    n_img_sem = 2 * len(powers(n_dp)) + 1
+    n_img_sem = 13 if n_dp == 8 else 2 * len(powers(n_dp)) + 1
     return pl.pallas_call(
         functools.partial(fwd_kernel, n_dp, rows),
         out_shape=outs,
@@ -562,6 +655,7 @@
             pltpu.VMEM((512, near * n_img), BF16),
             pltpu.VMEM((2, 512, D), BF16),
             pltpu.VMEM((n_dp, 1, 128), F32),
+            pltpu.VMEM((512 if n_dp > near else 8, D), F32),
             pltpu.VMEM((rows, D), BF16),
             pltpu.VMEM((2, 3, rows, width), BF16),
             pltpu.VMEM((2, rows, width), BF16),
@@ -572,8 +666,8 @@
             pltpu.VMEM((rows, D), F32),
             pltpu.VMEM((4, caps, D), BF16),
             pltpu.VMEM((caps, D), F32),
-            pltpu.SemaphoreType.DMA((28,)),
-            pltpu.SemaphoreType.DMA((28,)),
+            pltpu.SemaphoreType.DMA((36,)),
+            pltpu.SemaphoreType.DMA((36,)),
             pltpu.SemaphoreType.DMA((3,)),
             pltpu.SemaphoreType.DMA((3,)),
             pltpu.SemaphoreType.DMA((n_img_sem,)),
@@ -590,104 +684,8 @@
     )(*args)
 
 
-def pair_kernel(
-    n_dp,
-    n_mp,
-    pool_ref, image_ref, temp_ref,
-    grad_ref, loss_ref,
-    sums, part, ss, rs, l_ss, l_rs,
-):
-    dp = lax.axis_index("dp")
-    mp = lax.axis_index("mp")
-    caps = pool_ref.shape[0]
-    total = image_ref.shape[0]
-    near = [(dp, flip(mp, 1)), (dp, flip(mp, 2)), (dp, flip(flip(mp, 1), 2))]
-    far = [(lax.rem(dp + k, n_dp), mp) for k in range(1, n_dp)]
-    bar = pltpu.get_barrier_semaphore()
-    for dev in near + far:
-        pl.semaphore_signal(bar, inc=1, device_id=dev, device_id_type=MESH)
-
-    pooled = pool_ref[...]
-    inv = lax.rsqrt(jnp.sum(pooled * pooled, axis=-1, keepdims=True) + 1e-06)
-    text = (pooled * inv).astype(BF16)
-    temp = temp_ref[...]
-    logits = nt(text, image_ref[...]) * temp
-    e = jnp.exp(logits)
-    row_sum = jnp.sum(e, axis=-1, keepdims=True)
-    part[0] = jnp.sum(e, axis=0, keepdims=True)
-    pl.semaphore_wait(bar, len(near) + len(far))
-
-    sent = []
-    for i, dev in enumerate(far):
-        c = remote(part.at[0], sums.at[i], ss.at[i], rs.at[i], dev)
-        c.start()
-        sent.append(c)
-    own = mp * caps
-    base = dp * (caps * n_mp) + own
-    eye = (
-        lax.broadcasted_iota(jnp.int32, (caps, total), 1)
-        == lax.broadcasted_iota(jnp.int32, (caps, total), 0) + base
-    ).astype(F32)
-    row_grad = ((e / row_sum - eye) * temp).astype(BF16)
-    text_grad = nn(row_grad, image_ref[...])
-    picked = jnp.sum(logits * eye, axis=-1, keepdims=True)
-    for c in sent:
-        c.wait_recv()
-    part[1] = lax.fori_loop(0, n_dp - 1, lambda i, col: col + sums[i], part[0])
-    for i, dev in enumerate(near):
-        c = remote(part.at[1], sums.at[n_dp - 1 + i], ss.at[n_dp - 1 + i], rs.at[n_dp - 1 + i], dev)
-        c.start()
-        sent.append(c)
-    for c in sent[n_dp - 1 :]:
-        c.wait_recv()
-    col = part[1]
-    for i in range(3):
-        col = col + sums[n_dp - 1 + i]
-    col_grad = ((e / col - eye) * temp).astype(BF16)
-    text_grad = text_grad + nn(col_grad, image_ref[...])
-    col_lse = jnp.sum(jnp.log(col) * eye, axis=-1, keepdims=True)
-    loss = jnp.log(row_sum) + col_lse - 2.0 * picked
-    mine = pl.ds(own, caps)
-    loss_ref[mine] = jnp.broadcast_to(loss, (caps, 128))
-    for i, dev in enumerate(near):
-        c = remote(loss_ref.at[mine], loss_ref.at[mine], l_ss.at[i], l_rs.at[i], dev)
-        c.start()
-        sent.append(c)
-    dot = jnp.sum(text_grad * pooled, axis=-1, keepdims=True)
-    grad = inv * text_grad - pooled * (inv * inv * inv * dot)
-    grad_ref[...] = grad * (1.0 / SEQ)
-    for c in sent:
-        c.wait_send()
-    for c in sent[n_dp + 2 :]:
-        c.wait_recv()
-
-
-def run_pairs(n_dp, n_mp, pooled, image_low, temps):
-    caps = pooled.shape[0]
-    total = image_low.shape[0]
-    n = n_dp + 2
-    return pl.pallas_call(
-        functools.partial(pair_kernel, n_dp, n_mp),
-        out_shape=[jax.ShapeDtypeStruct((caps, D), F32), jax.ShapeDtypeStruct((caps * n_mp, 128), F32)],
-        in_specs=[pl.BlockSpec(memory_space=pltpu.VMEM)] * 3,
-        out_specs=[pl.BlockSpec(memory_space=pltpu.VMEM)] * 2,
-        scratch_shapes=[
-            pltpu.VMEM((n, 1, total), F32),
-            pltpu.VMEM((2, 1, total), F32),
-            pltpu.SemaphoreType.DMA((n,)),
-            pltpu.SemaphoreType.DMA((n,)),
-            pltpu.SemaphoreType.DMA((3,)),
-            pltpu.SemaphoreType.DMA((3,)),
-        ],
-        compiler_params=pltpu.CompilerParams(
-            collective_id=1, has_side_effects=True, vmem_limit_bytes=60 * 2**20
-        ),
-        name="contrast",
-    )(pooled, image_low, temps)
-
-
 SEQUENCE = (
-    ("p0", "g3", "g2", "g1", "g0", "dn", "m3", "m2", "m1", "m0", "u0", "sb", "d", "go", "n1", "a10", "a11"),
+    ("p0", "ct", "g3", "tx", "g2", "sy", "g1", "sc", "g0", "te", "dn", "m3", "m2", "m1", "m0", "u0", "sb", "d", "go", "n1", "a10", "a11"),
     ("u0", "u1", "qg1", "d", "u0", "o", "qb1", "o", "u1", "d", "a00", "a01", "o", "u0", "qg0", "u1", "qb0"),
     ("u0", "q2", "q0", "fb", "q1", "u1", "q2", "q0", "s", "q1", "q2", "u1", "s", "q1", "o", "q0", "q2", "q1"),
     ("o", "u0", "s", "q2", "q0", "q1", "q0", "q2", "d", "u1", "o", "ig", "s", "q1", "q0"),
@@ -818,12 +816,14 @@
 
 def back_kernel(
     n_dp,
+    n_mp,
     rows,
-    x_hbm, wq_hbm, wo_hbm, wu_hbm, wd_hbm, qkv_hbm, mix_hbm, hid_hbm, gp_hbm, sv_hbm, g1_hbm, s1_hbm, g2_hbm, s2_hbm, rg_ref,
-    ig_out, g_out, sm_out,
-    xv, vec_ref, wq, wo, wu, wd, qkv, mix, hid, gp, nv, nt_buf, acc, hl, mg, igv, low, ag,
-    gq, go_, gu, rc, rx, rd0, rd1, rd2, result, sa, ra, gd, pk, pr, pd,
-    ss, rs, ig_ss, ig_rs, s_ss, s_rs, r_ss, r_rs, m_ss, m_rs, l_sem, o_sem,
+    x_hbm, wq_hbm, wo_hbm, wu_hbm, wd_hbm, qkv_hbm, mix_hbm, hid_hbm, gp_hbm, sv_hbm, g1_hbm, s1_hbm, g2_hbm, s2_hbm, low_hbm,
+    text_hbm, pool_ref, temp_ref,
+    text_out, ig_out, g_out, sm_out, loss_ref,
+    xv, vec_ref, rg_ref, image, e_ref, cols, part, wq, wo, wu, wd, qkv, mix, hid, gp, nv, nt_buf, acc, hl, mg, text, igv, low, ag,
+    gu, rc, rx, rd0, rd1, rd2, result, sa, ra, gd, pk, pr, pd,
+    ss, rs, t_ss, t_rs, ig_ss, ig_rs, s_ss, s_rs, r_ss, r_rs, m_ss, m_rs, c_ss, c_rs, l_sem, o_sem,
 ):
     dp = lax.axis_index("dp")
     mp = lax.axis_index("mp")
@@ -834,8 +834,9 @@
     caps = rows // SEQ
 
     bar = pltpu.get_barrier_semaphore()
-    greet = [core, xdev, diag] + [(flip(dp, k), mp) for k in dps]
-    for dev in greet:
+    near = [core, xdev, diag]
+    around = [(lax.rem(dp + k, n_dp), mp) for k in range(1, n_dp)]
+    for dev in near + around:
         pl.semaphore_signal(bar, inc=1, device_id=dev, device_id_type=MESH)
 
     loads = {}
@@ -849,6 +850,10 @@
         for key in keys:
             loads[key].wait()
 
+    total = low_hbm.shape[0]
+    block = image.shape[0]
+    load("text", text_hbm, text.at[0])
+    load("image", low_hbm.at[pl.ds(0, block)], image)
     for i, v in enumerate((g1_hbm, s1_hbm, g2_hbm, s2_hbm)):
         load(("vec", i), v, vec_ref.at[i])
     load("hid", hid_hbm, hid)
@@ -863,10 +868,65 @@
     load("wq", wq_hbm, wq)
     load("s0", sv_hbm.at[0], sa.at[0, 0, 0])
 
-    low[...] = rg_ref[...].astype(BF16)
-    load("r0", low, ra.at[0, 0, 0])
-    pl.semaphore_wait(bar, len(greet))
-
+    def image_block(j):
+        if total > block:
+            c = pltpu.make_async_copy(low_hbm.at[pl.ds(j * block, block)], image, l_sem.at[0])
+            c.start()
+            c.wait()
+        return image[...]
+
+    pooled = pool_ref[...]
+    inv = lax.rsqrt(jnp.sum(pooled * pooled, axis=-1, keepdims=True) + 1e-06)
+    unit_text = (pooled * inv).astype(BF16)
+    own_caps = mp * caps
+    base = dp * (caps * n_mp) + own_caps
+
+    def own_columns(j):
+        shape = (caps, block)
+        column = lax.broadcasted_iota(jnp.int32, shape, 1) + j * block
+        return (column == lax.broadcasted_iota(jnp.int32, shape, 0) + base).astype(F32)
+
+    ready("image")
+    row_sum, picked = 0.0, 0.0
+    for j in range(total // block):
+        c = slice(j * block, (j + 1) * block)
+        logits = nt(unit_text, image_block(j)) * temp_ref[:, c]
+        e = jnp.exp(logits)
+        e_ref[:, c] = e
+        row_sum = row_sum + jnp.sum(e, axis=-1, keepdims=True)
+        picked = picked + jnp.sum(logits * own_columns(j), axis=-1, keepdims=True)
+        part[0, :, c] = jnp.sum(e, axis=0, keepdims=True)
+    pl.semaphore_wait(bar, len(near) + len(around))
+    col_copies = []
+
+    def row_block(s):
+        place = mp
+        for k in (1, 2):
+            if s & k:
+                place = flip(place, k)
+        return pl.ds(place * rows, rows)
+
+    def row_copies(buf, send, recv):
+        return [
+            remote(buf.at[0], buf.at[1], send.at[0], recv.at[0], core),
+            remote(buf.at[0], buf.at[2], send.at[1], recv.at[1], xdev),
+            remote(buf.at[2], buf.at[3], send.at[2], recv.at[2], core),
+        ]
+
+    tx = row_copies(text, t_ss, t_rs)
+    ready("text")
+    for c in tx[:2]:
+        c.start()
+
+    def spread_columns(src, first_slot, devs):
+        for i, dev in enumerate(devs):
+            k = first_slot + i
+            c = remote(part.at[src], cols.at[k], c_ss.at[k], c_rs.at[k], dev)
+            c.start()
+            col_copies.append(c)
+        return col_copies[-len(devs) :]
+
+    first_copies = spread_columns(0, 0, around)
     bit0 = lax.rem(dp, 2)
     f_cut = gd.shape[0] // 2
     other = pl.ds(pl.multiple_of((1 - bit0) * f_cut, 128), f_cut)
@@ -879,7 +939,7 @@
     s_y = remote(sa.at[:, 0, :, :, other], sa.at[:, 1, :, :, other], s_ss.at[3], s_rs.at[3], ydev)
     r_y = remote(ra.at[0, 0], ra.at[0, 1], r_ss.at[1], r_rs.at[1], ydev)
     r_core = remote(ra.at[0], ra.at[1], r_ss.at[2], r_rs.at[2], core)
-    for c in s_first + [r_first]:
+    for c in s_first:
         c.start()
 
     def share_y():
@@ -913,7 +973,17 @@
     number = [0]
     places = (core, xdev, lambda k: (flip(dp, k), mp), lambda k: lax.rem(lax.div(dp, k), 2))
     rds = (rd0, rd1) + tuple([rd2.at[i] for i in range(rd2.shape[0])])
-    u_rows, o_rows, q_rows = gu.shape[1], go_.shape[2], gq.shape[3]
+    u_rows, o_rows, q_rows = gu.shape[1], wo.shape[2], wq.shape[3]
+
+    def slot_at(k):
+        per = u_rows // q_rows
+        return wd.at[k // per, pl.ds((k % per) * q_rows, q_rows)]
+
+    def gq_at(p, n, i):
+        return slot_at((p * 3 + n) * 2 + i)
+
+    def go_at(p, i):
+        return slot_at(12 + 2 * p + i)
 
     def make(name, view, n, base):
         return Sum(view, n, base, places, (rc, rx, rds, result), (ss, rs, number), n_dp, name in SWAPPED)
@@ -922,9 +992,9 @@
     sum_u = [
         make("u%d" % i, lambda s, i=i: gu.at[s, pl.ds(i * u_cut, u_cut)], u_cut, i * u_cut) for i in range(2)
     ]
-    sum_o = make("o", lambda s: go_.at[s // 2, s % 2], o_rows, u_rows)
+    sum_o = make("o", lambda s: go_at(s // 2, s % 2), o_rows, u_rows)
     sum_q = [
-        make("q%d" % n, lambda s, n=n: gq.at[s // 2, n, s % 2], q_rows, u_rows + o_rows + n * q_rows)
+        make("q%d" % n, lambda s, n=n: gq_at(s // 2, n, s % 2), q_rows, u_rows + o_rows + n * q_rows)
         for n in range(3)
     ]
     sum_d = make("d", lambda s: gd, gd.shape[0], u_rows + o_rows + 3 * q_rows)
@@ -934,7 +1004,53 @@
     g1, s1, g2, s2 = vec_ref[0:1], vec_ref[1:2], vec_ref[2:3], vec_ref[3:4]
     step = 128
     pk[...] = jnp.zeros_like(pk)
-    pk[0, 5:6] = jnp.sum(rg_ref[...], axis=0, keepdims=True) * float(SEQ)
+
+    def text_on():
+        put(text.at[0], text_out.at[row_block(0)])
+        tx[1].wait()
+        tx[2].start()
+        put(text.at[2], text_out.at[row_block(2)])
+        tx[0].wait()
+        put(text.at[1], text_out.at[row_block(1)])
+
+    def text_end():
+        tx[2].wait()
+        put(text.at[3], text_out.at[row_block(3)])
+
+    def contrast():
+        text_grad = jnp.zeros((caps, D), F32)
+        for j in range(total // block):
+            c = slice(j * block, (j + 1) * block)
+            grad = ((e_ref[:, c] / row_sum - own_columns(j)) * temp_ref[:, c]).astype(BF16)
+            text_grad = text_grad + nn(grad, image_block(j))
+        for c in first_copies:
+            c.wait_recv()
+        part[1] = lax.fori_loop(0, n_dp - 1, lambda i, col: col + cols[i], part[0])
+        for c in spread_columns(1, n_dp - 1, near):
+            c.wait_recv()
+        part[2] = part[1] + cols[n_dp - 1] + cols[n_dp] + cols[n_dp + 1]
+        col_lse = 0.0
+        for j in range(total // block):
+            c = slice(j * block, (j + 1) * block)
+            col = part[2, :, c]
+            grad = ((e_ref[:, c] / col - own_columns(j)) * temp_ref[:, c]).astype(BF16)
+            text_grad = text_grad + nn(grad, image_block(j))
+            col_lse = col_lse + jnp.sum(jnp.log(col) * own_columns(j), axis=-1, keepdims=True)
+        dot = jnp.sum(text_grad * pooled, axis=-1, keepdims=True)
+        grad = (inv * text_grad - pooled * (inv * inv * inv * dot)) * (1.0 / SEQ)
+        rg_ref[...] = grad
+        low[...] = grad.astype(BF16)
+        r_first.start()
+        load("r0", low, ra.at[0, 0, 0])
+        pk[0, 5:6] = jnp.sum(grad, axis=0, keepdims=True) * float(SEQ)
+        loss = jnp.log(row_sum) + col_lse - 2.0 * picked
+        loss_ref[pl.ds(own_caps, caps)] = jnp.broadcast_to(loss, (caps, 128))
+        for i, dev in enumerate(near):
+            at = loss_ref.at[pl.ds(own_caps, caps)]
+            k = n_dp + 2 + i
+            c = remote(at, at, c_ss.at[k], c_rs.at[k], dev)
+            c.start()
+            col_copies.append(c)
 
     def norm_again(i, carry):
         r = pl.ds(pl.multiple_of(i * step, step), step)
@@ -1005,8 +1121,8 @@
         for p in (1, 0):
             mt = mix[p].T
             g = nn(mt, hl[...]).astype(BF16)
-            go_[p, 0] = g[:o_rows]
-            go_[p, 1] = g[o_rows:]
+            go_at(p, 0)[...] = g[:o_rows]
+            go_at(p, 1)[...] = g[o_rows:]
             sum_o.send_core(2 * p + 1)
             mg[p] = nt(hl[...], wo[p].reshape(width, D)).astype(BF16)
         sum_o.merge_core(2)
@@ -1060,8 +1176,8 @@
     def qkv_grad(p):
         for n in range(3):
             g = nn(qkv[p, n].T, nv[...]).astype(BF16)
-            gq[p, n, 0] = g[:q_rows]
-            gq[p, n, 1] = g[q_rows:]
+            gq_at(p, n, 0)[...] = g[:q_rows]
+            gq_at(p, n, 1)[...] = g[q_rows:]
             sum_q[n].send_core(2 * p + 1)
 
     def qkv_back(p, begin):
@@ -1086,7 +1202,7 @@
         back = rstd * (
             t - jnp.mean(t, axis=-1, keepdims=True) - xhat * jnp.mean(t * xhat, axis=-1, keepdims=True)
         )
-        igv[r] = (acc[r] + back).astype(BF16)
+        igv[0, r] = (acc[r] + back).astype(BF16)
         pk[0, 0:1] += jnp.sum(g * xhat, axis=0, keepdims=True)
         pk[0, 1:2] += jnp.sum(g, axis=0, keepdims=True)
         return carry
@@ -1095,13 +1211,7 @@
         remote(pk.at[k], pr.at[k - 1], m_ss.at[k - 1], m_rs.at[k - 1], dev)
         for k, dev in ((1, core), (2, xdev), (3, diag))
     ]
-    own = pl.ds(mp * rows, rows)
-    far = pl.ds(flip(mp, 2) * rows, rows)
-    ig = [
-        remote(igv, ig_out.at[own], ig_ss.at[0], ig_rs.at[0], core),
-        remote(igv, ig_out.at[own], ig_ss.at[1], ig_rs.at[1], xdev),
-        remote(ig_out.at[far], ig_out.at[far], ig_ss.at[2], ig_rs.at[2], core),
-    ]
+    ig = row_copies(igv, ig_ss, ig_rs)
 
     def leave():
         lax.fori_loop(0, rows // step, first_back, 0)
@@ -1109,11 +1219,14 @@
             pk[k, 0:6] = pk[0, 0:6]
         for c in small + ig[:2]:
             c.start()
-        put(igv, ig_out.at[own])
+        put(igv.at[0], ig_out.at[row_block(0)])
 
     def pass_on():
         ig[1].wait()
         ig[2].start()
+        put(igv.at[2], ig_out.at[row_block(2)])
+        ig[0].wait()
+        put(igv.at[1], ig_out.at[row_block(1)])
 
     def small_steps():
         for c in small:
@@ -1145,13 +1258,11 @@
         for t in sum_u:
             t.merge_core(2)
             t.send_x()
-        share_y()
 
     def piece_g1():
         mlp_grad(1)
         for t in sum_u:
             t.send_core(1)
-        share_core()
 
     def piece_g0():
         mlp_grad(0)
@@ -1175,6 +1286,11 @@
 
     pieces = {
         "p0": lambda: loop(norm_again, "hid"),
+        "ct": contrast,
+        "tx": text_on,
+        "te": text_end,
+        "sy": share_y,
+        "sc": share_core,
         "g3": piece_g3,
         "g2": piece_g2,
         "g1": piece_g1,
@@ -1213,52 +1329,67 @@
         live = [g for g in live if next(g, live) is not live]
     put(result, g_out)
 
-    ig[0].wait()
     ig[2].wait()
+    put(igv.at[3], ig_out.at[row_block(3)])
+    for c in col_copies:
+        c.wait_send()
+    for c in col_copies[-len(near) :]:
+        c.wait_recv()
     for c in outs:
         c.wait()
 
 
-def run_backward(n_dp, rows, tokens, wq, wo, wu, wd, qkv, mix, hid, gp, sv, gains, rg):
+def run_backward(n_dp, n_mp, rows, tokens, wq, wo, wu, wd, qkv, mix, hid, gp, sv, gains, low, text, pooled, temps):
     caps = rows // SEQ
     sds = jax.ShapeDtypeStruct
     q_rows = wq.shape[3]
     o_rows = wo.shape[2]
     u_rows = wu.shape[1]
     total = u_rows + o_rows + 3 * q_rows + wd.shape[1]
+    over_x = total - wd.shape[1]
     width = 2 * q_rows
     n_pow = len(powers(n_dp))
     outs = [
         sds(tokens.shape, BF16),
+        sds(tokens.shape, BF16),
         sds((total, D), BF16),
         sds((16, D), F32),
+        sds((caps * n_mp, 128), F32),
     ]
+    captions = low.shape[0]
+    n_col = n_dp + 5
     any_spec = pl.BlockSpec(memory_space=pl.ANY)
     vmem = pl.BlockSpec(memory_space=pltpu.VMEM)
     vm = lambda s: pltpu.VMEM(s.shape, s.dtype)
     sem = lambda n: pltpu.SemaphoreType.DMA((n,))
     n_sum = 7 * (3 + 2 * n_pow)
     return pl.pallas_call(
-        functools.partial(back_kernel, n_dp, rows),
+        functools.partial(back_kernel, n_dp, n_mp, rows),
         out_shape=outs,
-        in_specs=[any_spec] * 14 + [vmem],
-        out_specs=[any_spec] * len(outs),
+        in_specs=[any_spec] * 16 + [vmem] * 2,
+        out_specs=[any_spec] * 4 + [vmem],
         scratch_shapes=[
             pltpu.VMEM((rows, D), BF16),
             pltpu.VMEM((8, D), F32),
+            pltpu.VMEM((caps, D), F32),
+            pltpu.VMEM((captions if captions <= 1024 else 512, D), BF16),
+            pltpu.VMEM((caps, captions), F32),
+            pltpu.VMEM((n_dp + 2, 1, captions), F32),
+            pltpu.VMEM((3, 1, captions), F32),
             vm(wq), vm(wo), vm(wu), vm(wd), vm(qkv), vm(mix), vm(hid), vm(gp),
             pltpu.VMEM((rows, D), BF16),
             pltpu.VMEM((D, rows), BF16),
             pltpu.VMEM((rows, D), F32),
             pltpu.VMEM((rows, D), BF16),
             pltpu.VMEM((2, rows, width), BF16),
-            pltpu.VMEM((rows, D), BF16),
+            pltpu.VMEM((4, rows, D), BF16),
+            pltpu.VMEM((4, rows, D), BF16),
             pltpu.VMEM((caps, D), BF16),
             pltpu.VMEM((caps, D), F32),
-            vm(wq), vm(wo), vm(wu),
-            pltpu.VMEM((2, total, D), BF16),
-            pltpu.VMEM((total, D), BF16),
-            pltpu.VMEM((total // 2, D), BF16),
+            vm(wu),
+            pltpu.VMEM((2, over_x, D), BF16),
+            pltpu.VMEM((over_x, D), BF16),
+            pltpu.VMEM((over_x // 2, D), BF16),
             pltpu.VMEM((total // 4, D), BF16),
             pltpu.VMEM((max(1, n_pow - 2), total // 4, D), BF16),
             pltpu.VMEM((total, D), BF16),
@@ -1268,14 +1399,111 @@
             pltpu.VMEM((4, 16, D), F32),
             pltpu.VMEM((3, 16, D), F32),
             pltpu.VMEM((2 * n_pow + 1, 16, D), F32),
-            sem(n_sum), sem(n_sum), sem(3), sem(3), sem(4), sem(4),
-            sem(3), sem(3), sem(3 + n_pow), sem(3 + n_pow), sem(24), sem(3),
+            sem(n_sum), sem(n_sum), sem(3), sem(3), sem(3), sem(3), sem(4), sem(4),
+            sem(3), sem(3), sem(3 + n_pow), sem(3 + n_pow), sem(n_col), sem(n_col), sem(26), sem(10),
         ],
         compiler_params=pltpu.CompilerParams(
-            collective_id=2, has_side_effects=True, vmem_limit_bytes=62 * 2**20
+            collective_id=1, has_side_effects=True, vmem_limit_bytes=63 * 2**20
         ),
         name="backward",
-    )(tokens, wq, wo, wu, wd, qkv, mix, hid, gp, sv, *gains, rg)
+    )(tokens, wq, wo, wu, wd, qkv, mix, hid, gp, sv, *gains, low, text, pooled, temps)
+
+
+def finish_kernel(
+    q_rows, o_rows, u_rows, width_q,
+    g_hbm, small_ref, loss_ref, ig_hbm, text_hbm,
+    ig_out, text_out, loss_out, wq_out, qv_out, wo_out, wu_out, wd_out,
+    g1_out, s1_out, ob_out, g2_out, s2_out, ub_out, db_out,
+    low, wide, flat, total, line,
+    in_sem, out_sem, big_sem,
+):
+    rows = g_hbm.shape[0]
+    step = q_rows
+    count = rows // step
+    part = ig_hbm.shape[0] // 4
+    cuts = [pl.ds(i * part, part) for i in range(4)]
+    big, away = [], []
+    for n, (src, dst) in enumerate(((ig_hbm, ig_out), (text_hbm, text_out))):
+        for i, c in enumerate(cuts):
+            k = 4 * n + i
+            big.append(pltpu.make_async_copy(src.at[c], wide.at[n, c], big_sem.at[k]))
+            away.append(pltpu.make_async_copy(wide.at[n, c], dst.at[c], big_sem.at[8 + k]))
+    first = [
+        pltpu.make_async_copy(g_hbm.at[pl.ds(i * step, step)], low.at[pl.ds(i * step, step)], in_sem.at[i])
+        for i in range(count)
+    ]
+    q_at = (u_rows + o_rows) // step
+    order = [q_at + n for n in range(3)] + [i for i in range(count) if not q_at <= i < q_at + 3]
+    for i in order:
+        first[i].start()
+    for c in big:
+        c.start()
+    outs = []
+
+    def put(src, dst):
+        c = pltpu.make_async_copy(src, dst, out_sem.at[len(outs)])
+        c.start()
+        outs.append(c)
+
+    total[0:8] = small_ref[0:8]
+    total[8:16] = pltpu.roll(small_ref[8:16], D - q_rows, 1)
+    both_rows = total[7:8] + total[8:9]
+    line[0:1] = both_rows[:, :q_rows]
+    line[1:2] = both_rows[:, width_q : width_q + q_rows]
+    put(line, qv_out)
+    for i, dst in ((0, g1_out), (1, s1_out), (2, ob_out), (3, g2_out), (4, s2_out), (6, ub_out), (5, db_out)):
+        put(total.at[i], dst)
+    total[16:24, :128] = loss_ref[...].T[0:8]
+    put(total.at[16, pl.ds(0, 128)], loss_out)
+    for n, i in enumerate(order):
+        if n >= count - len(big):
+            big[n - count + len(big)].wait()
+            away[n - count + len(big)].start()
+        first[i].wait()
+        r = slice(i * step, (i + 1) * step)
+        v = low[r].astype(F32)
+        if q_at <= i < q_at + 3:
+            flat[r] = v
+            put(flat.at[r], wq_out.at[i - q_at])
+            continue
+        flat[r] = v
+        at = i * step
+        last = rows - wd_out.shape[0]
+        for dst, lo, hi in ((wu_out, 0, u_rows), (wo_out, u_rows, u_rows + o_rows), (wd_out, last, rows)):
+            if lo <= at < hi:
+                put(flat.at[r], dst.at[pl.ds(at - lo, step)])
+    for c in outs + away:
+        c.wait()
+
+
+def run_finish(grads, small, loss, ig, text, q_rows, o_rows, u_rows, d_rows):
+    sds = jax.ShapeDtypeStruct
+    rows = grads.shape[0]
+    outs = [
+        sds(ig.shape, BF16), sds(ig.shape, BF16), sds((loss.shape[0],), F32), sds((3, q_rows, D), F32), sds((2, q_rows), F32),
+        sds((o_rows, D), F32), sds((u_rows, D), F32), sds((d_rows, D), F32),
+    ] + [sds((D,), F32)] * 7
+    any_spec = pl.BlockSpec(memory_space=pl.ANY)
+    vmem = pl.BlockSpec(memory_space=pltpu.VMEM)
+    count = rows // q_rows
+    return pl.pallas_call(
+        functools.partial(finish_kernel, q_rows, o_rows, u_rows, 2 * q_rows),
+        out_shape=outs,
+        in_specs=[any_spec, vmem, vmem, any_spec, any_spec],
+        out_specs=[any_spec] * len(outs),
+        scratch_shapes=[
+            pltpu.VMEM((rows, D), BF16),
+            pltpu.VMEM((2,) + ig.shape, BF16),
+            pltpu.VMEM((rows, D), F32),
+            pltpu.VMEM((24, D), F32),
+            pltpu.VMEM((2, q_rows), F32),
+            pltpu.SemaphoreType.DMA((count,)),
+            pltpu.SemaphoreType.DMA((count + 9,)),
+            pltpu.SemaphoreType.DMA((16,)),
+        ],
+        compiler_params=pltpu.CompilerParams(vmem_limit_bytes=62 * 2**20),
+        name="outputs",
+    )(grads, small, loss, ig, text)
 
 
 def solution(mesh):
@@ -1296,20 +1524,15 @@
                 ln2_bias, down_bias, images, image_group, pair_shard, pair_row,
             ),
         )
-        rg, loss = run_pairs(n_dp, n_mp, pooled, image_low, temps)
-        ig, grads, small = run_backward(
-            n_dp, rows, tokens, wq, wo, wu, wd, qkv, mix, hid, gp, sv, (ln1_gain, ln1_bias, ln2_gain, ln2_bias), rg
+        text_rows, ig, grads, small, loss = run_backward(
+            n_dp, n_mp, rows, tokens, wq, wo, wu, wd, qkv, mix, hid, gp, sv, (ln1_gain, ln1_bias, ln2_gain, ln2_bias),
+            image_low, text, pooled, temps,
         )
-        cuts = [w_up.shape[0], w_up.shape[0] + w_out.shape[0]]
-        wu_g, wo_g = grads[: cuts[0]], grads[cuts[0] : cuts[1]]
-        cuts.append(cuts[1] + 3 * q_rows)
-        wq_g, wd_g = grads[cuts[1] : cuts[2]].reshape(3, q_rows, D), grads[cuts[2] :]
-        text_out = lax.all_gather(text, "mp", axis=0, tiled=True)
-        qb = small[7].reshape(2, 2 * q_rows)[:, :q_rows] + small[8].reshape(2, 2 * q_rows)[:, q_rows:]
+        (input_grad, text_out, caption_loss, wq_g, qv_g, wo_g, wu_g, wd_g, g1, s1, ob, g2, s2, ub, db) = run_finish(
+            grads, small, loss, ig, text_rows, q_rows, w_out.shape[0], w_up.shape[0], w_down.shape[0]
+        )
         return (
-            text_out, ig, loss[:, 0],
-            small[0], small[1], jnp.transpose(wq_g, (0, 2, 1)).astype(F32), qb, wo_g.astype(F32), small[2],
-            small[3], small[4], wu_g.astype(F32), small[6], wd_g.astype(F32), small[5],
+            text_out, input_grad, caption_loss, g1, s1, jnp.transpose(wq_g, (0, 2, 1)), qv_g, wo_g, ob, g2, s2, wu_g, ub, wd_g, db,
         )
 
     in_specs = (

time: 233 us -> 202 us (0.87)
  between operations: 14.1 us -> 0.84 us
  local copies, waits for them, and re-layouts: 10.7 us -> 1.39 us
  other arithmetic: 6.36 us -> 0 us
    pallas_call x1, Pallas kernels: 78.2 us -> 65.1 us  [run_forward(): pl.pallas_call(functools.partial(fwd_kernel, n_dp, rows), out_shape=outs,...]
    pallas_call x2, Pallas kernels: 124 us -> 135 us  [the longest x1 125 us: run_backward(): pl.pallas_call(functools.partial(back_kernel, n_dp, n_mp, rows), out_shap...]
    convert_element_type x3 -> x0, other arithmetic: 5.71 us -> none  [the longest x1 2.54 us: body(): wd_g.astype(F32)]
    unnamed x9 -> x1, local copies, waits for them, and re-layouts: 6.97 us -> 1.39 us
    slice x3 -> x0, local copies, waits for them, and re-layouts: 3.72 us -> none  [the longest x1 1.72 us: body(): small[5]]
  transfers between devices with their start and end apart: 1 -> 0, of which waited for: 0 -> 0; matrix products, arithmetic and copies ran while one was open for 4% -> 0% of each run, Pallas kernels for 53% -> 0%
where the time goes in v3:
time: 202 us
  Pallas kernels  200 us (99%)
    pallas_call x1, Pallas kernels, run_backward(): pl.pallas_call(functools.partial(back_kernel, n_dp, n_mp, rows), out_shap...  125 us
    pallas_call x1, Pallas kernels, run_forward(): pl.pallas_call(functools.partial(fwd_kernel, n_dp, rows), out_shape=outs,...  65.1 us
    pallas_call x1, Pallas kernels, run_finish(): pl.pallas_call(functools.partial(finish_kernel, q_rows, o_rows, u_rows, 2...  9.89 us

profile of v3, /device:TPU:0, one launch (start us, length us, event | category | flops | bytes accessed | tf_op | source)
XLA Modules:
  0.0 202.3 jit_solution(12600783120122926139)
XLA Ops:
  0.6 1.4 copy.32.shard_hbm
  2.0 65.1 %forward.1 = (bf16[2,3,2,192,768]{4,3,2,1,0:T(8,128)(2,1)}, bf16[2,2,192,768]{3,2,1,0:T(8,128)(2,1)}, bf16[4,768,768]{2,1,0:T(8,128)(2,1)}, bf16[4,768,768]{2,1,...) custom-call(bf16[2048,768]{1,0:T(8,128)(2,1)} %x_hbm.3, ...), custom_call_target="tpu_custom_call" | custom-call | tf_op jit(solution)/shard_map/forward/pallas_call | solution.py:640
  67.2 125.0 %backward.1 = (bf16[2048,768]{1,0:T(8,128)(2,1)}, bf16[2048,768]{1,0:T(8,128)(2,1)}, bf16[2304,768]{1,0:T(8,128)(2,1)}, f32[16,768]{1,0:T(8,128)}, f32[128,128]{1,0:T(8,128)}) custom-call(bf16[2048,768]{1,0:T(8,128)(2,1)} %x_hbm.3, bf16[2,3,2,192,768]{4,3,2,1,0:T(8,128)(2,1)} %get-tuple-element.48.wq_hbm, bf16[2,2,192,768]{3,2,1,0:T(8,128)(2,1)} %get-tuple-element.49.wo_hbm, ...), custom_call_target="tpu_custom_call" | custom-call | tf_op jit(solution)/shard_map/backward/pallas_call | solution.py:1366
  192.2 9.9 %outputs.1 = (bf16[2048,768]{1,0:T(8,128)(2,1)}, bf16[2048,768]{1,0:T(8,128)(2,1)}, f32[128]{0:T(128)}, f32[3,192,768]{2,1,0:T(8,128)}, f32[2,192]{1,0:T(2,128)}...) custom-call(bf16[2304,768]{1,0:T(8,128)(2,1)} %get-tuple-element.61., ...), custom_call_target="tpu_custom_call" | custom-call | tf_op jit(solution)/shard_map/outputs/pallas_call | solution.py:1489

commit v4 on v3

--- a/solution.py
+++ b/solution.py
@@ -185,7 +185,7 @@
 
     table = []
     for total, cuts, src, at in (
-        (q_rows, 1, src_q, at_q),
+        (q_rows, 2, src_q, at_q),
         (o_rows, 1, src_o, at_o),
         (u_rows, 2, src_u, at_u),
         (d_rows, 4, src_d, at_d),
@@ -395,8 +395,9 @@
     step_core[0].wait_recv()
     bias[0].wait_recv()
     project(0)
+    forward_x(0, 0)
     attend(0)
-    forward_x(0, 0)
+    forward_x(0, 1)
     forward_x(1, 0)
     if relay:
         image_across()
@@ -404,17 +405,18 @@
         for j in range(2, len(dps)):
             image_step(j)
     forward_y(0, 0)
-    forward_x(2, 0)
-    forward_y(1, 0)
-    if relay:
-        image_outward(0)
+    forward_y(0, 1)
     bias[1].wait_recv()
     bias[2].wait_recv()
     arrived(0)
     put(wq, wq_out)
     project(1)
+    forward_x(2, 0)
+    attend(1)
+    forward_y(1, 0)
+    if relay:
+        image_outward(0)
     forward_x(2, 1)
-    attend(1)
     put(qkv, qkv_out)
     put(mix, mix_out)
     local[2].wait()
@@ -567,9 +569,9 @@
     else:
         forward_y(3, 3)
         pick_many()
+    down(2)
     arrived(3)
     put(wd, wd_out)
-    down(2)
     down(3)
 
     def finish(i, carry):
@@ -666,8 +668,8 @@
             pltpu.VMEM((rows, D), F32),
             pltpu.VMEM((4, caps, D), BF16),
             pltpu.VMEM((caps, D), F32),
-            pltpu.SemaphoreType.DMA((36,)),
-            pltpu.SemaphoreType.DMA((36,)),
+            pltpu.SemaphoreType.DMA((40,)),
+            pltpu.SemaphoreType.DMA((40,)),
             pltpu.SemaphoreType.DMA((3,)),
             pltpu.SemaphoreType.DMA((3,)),
             pltpu.SemaphoreType.DMA((n_img_sem,)),
@@ -685,12 +687,14 @@
 
 
 SEQUENCE = (
-    ("p0", "ct", "g3", "tx", "g2", "sy", "g1", "sc", "g0", "te", "dn", "m3", "m2", "m1", "m0", "u0", "sb", "d", "go", "n1", "a10", "a11"),
-    ("u0", "u1", "qg1", "d", "u0", "o", "qb1", "o", "u1", "d", "a00", "a01", "o", "u0", "qg0", "u1", "qb0"),
-    ("u0", "q2", "q0", "fb", "q1", "u1", "q2", "q0", "s", "q1", "q2", "u1", "s", "q1", "o", "q0", "q2", "q1"),
-    ("o", "u0", "s", "q2", "q0", "q1", "q0", "q2", "d", "u1", "o", "ig", "s", "q1", "q0"),
+    ("p0", "ct", "g3", "g2", "g1", "sy", "g0", "m3", "m2", "sc", "dn", "m1", "m0", "sb", "go", "u1", "d"),
+    ("n1", "a10", "a11", "u2", "u1", "qg1", "u3", "u2", "u0", "qb1", "u1", "d", "u3", "a00", "o", "a01", "qg0"),
+    ("u2", "d", "o", "u1", "qb0", "u0", "o", "q0", "fb", "q1", "u0", "o", "q1", "q2", "u3", "s", "d"),
+    ("o", "q0", "q1", "q2", "u1", "u0", "s", "q0", "u2", "u0", "q2", "q1", "o", "u1", "q0", "u3", "s"),
+    ("u2", "q2", "ig", "q0", "q1", "q2", "u3", "tx", "u2", "q2", "q1", "u0", "q0", "s", "u3", "te"),
 )
-SWAPPED = ("q0", "q2")
+U_PARTS = 4
+SWAPPED = ("q1", "q2")
 
 
 def back_plan(rows, n_dp, swapped):
@@ -857,15 +861,6 @@
     for i, v in enumerate((g1_hbm, s1_hbm, g2_hbm, s2_hbm)):
         load(("vec", i), v, vec_ref.at[i])
     load("hid", hid_hbm, hid)
-    for s in (3, 2, 1, 0):
-        load(("wd", s), wd_hbm.at[s], wd.at[s])
-        load(("gp", s), gp_hbm.at[s], gp.at[s])
-        load(("wu", s), wu_hbm.at[s], wu.at[s])
-    load("mix", mix_hbm, mix)
-    load("wo", wo_hbm, wo)
-    load("qkv", qkv_hbm, qkv)
-    load("x", x_hbm.at[pl.ds(mp * rows, rows)], xv)
-    load("wq", wq_hbm, wq)
     load("s0", sv_hbm.at[0], sa.at[0, 0, 0])
 
     def image_block(j):
@@ -907,16 +902,18 @@
         return pl.ds(place * rows, rows)
 
     def row_copies(buf, send, recv):
+        low_part, high_part = pl.ds(0, ahead), pl.ds(ahead, rows - ahead)
         return [
             remote(buf.at[0], buf.at[1], send.at[0], recv.at[0], core),
-            remote(buf.at[0], buf.at[2], send.at[1], recv.at[1], xdev),
-            remote(buf.at[2], buf.at[3], send.at[2], recv.at[2], core),
+            remote(buf.at[0, low_part], buf.at[2, low_part], send.at[1], recv.at[1], xdev),
+            remote(buf.at[0, high_part], buf.at[2, high_part], send.at[2], recv.at[2], xdev),
+            remote(buf.at[2, low_part], buf.at[3, low_part], send.at[3], recv.at[3], core),
+            remote(buf.at[2, high_part], buf.at[3, high_part], send.at[4], recv.at[4], core),
         ]
 
+    ahead = rows * 5 // 16 // 16 * 16
     tx = row_copies(text, t_ss, t_rs)
     ready("text")
-    for c in tx[:2]:
-        c.start()
 
     def spread_columns(src, first_slot, devs):
         for i, dev in enumerate(devs):
@@ -926,22 +923,30 @@
             col_copies.append(c)
         return col_copies[-len(devs) :]
 
+    s_first = [
+        remote(sv_hbm.at[k], sa.at[k % 2, 0, k // 2], s_ss.at[k - 1], s_rs.at[k - 1], dev)
+        for k, dev in ((1, core), (2, xdev), (3, diag))
+    ]
     first_copies = spread_columns(0, 0, around)
+    for c in s_first + tx[:2]:
+        c.start()
+    for s in (3, 2, 1, 0):
+        load(("wd", s), wd_hbm.at[s], wd.at[s])
+        load(("gp", s), gp_hbm.at[s], gp.at[s])
+        load(("wu", s), wu_hbm.at[s], wu.at[s])
+    load("mix", mix_hbm, mix)
+    load("wo", wo_hbm, wo)
+    load("qkv", qkv_hbm, qkv)
+    load("x", x_hbm.at[pl.ds(mp * rows, rows)], xv)
+    load("wq", wq_hbm, wq)
     bit0 = lax.rem(dp, 2)
     f_cut = gd.shape[0] // 2
     other = pl.ds(pl.multiple_of((1 - bit0) * f_cut, 128), f_cut)
     ydev = (flip(dp, 1), mp)
-    s_first = [
-        remote(sv_hbm.at[k], sa.at[k % 2, 0, k // 2], s_ss.at[k - 1], s_rs.at[k - 1], dev)
-        for k, dev in ((1, core), (2, xdev), (3, diag))
-    ]
     r_first = remote(low, ra.at[0, 0, 1], r_ss.at[0], r_rs.at[0], xdev)
     s_y = remote(sa.at[:, 0, :, :, other], sa.at[:, 1, :, :, other], s_ss.at[3], s_rs.at[3], ydev)
     r_y = remote(ra.at[0, 0], ra.at[0, 1], r_ss.at[1], r_rs.at[1], ydev)
     r_core = remote(ra.at[0], ra.at[1], r_ss.at[2], r_rs.at[2], core)
-    for c in s_first:
-        c.start()
-
     def share_y():
         ready("s0", "r0")
         for c in s_first + [r_first]:
@@ -988,9 +993,9 @@
     def make(name, view, n, base):
         return Sum(view, n, base, places, (rc, rx, rds, result), (ss, rs, number), n_dp, name in SWAPPED)
 
-    u_cut = u_rows // 2
+    u_cut = u_rows // U_PARTS
     sum_u = [
-        make("u%d" % i, lambda s, i=i: gu.at[s, pl.ds(i * u_cut, u_cut)], u_cut, i * u_cut) for i in range(2)
+        make("u%d" % i, lambda s, i=i: gu.at[s, pl.ds(i * u_cut, u_cut)], u_cut, i * u_cut) for i in range(U_PARTS)
     ]
     sum_o = make("o", lambda s: go_at(s // 2, s % 2), o_rows, u_rows)
     sum_q = [
@@ -1008,13 +1013,16 @@
     def text_on():
         put(text.at[0], text_out.at[row_block(0)])
         tx[1].wait()
-        tx[2].start()
+        tx[3].start()
+        tx[2].wait()
+        tx[4].start()
         put(text.at[2], text_out.at[row_block(2)])
         tx[0].wait()
         put(text.at[1], text_out.at[row_block(1)])
 
     def text_end():
-        tx[2].wait()
+        tx[3].wait()
+        tx[4].wait()
         put(text.at[3], text_out.at[row_block(3)])
 
     def contrast():
@@ -1026,7 +1034,9 @@
         for c in first_copies:
             c.wait_recv()
         part[1] = lax.fori_loop(0, n_dp - 1, lambda i, col: col + cols[i], part[0])
-        for c in spread_columns(1, n_dp - 1, near):
+        second_copies = spread_columns(1, n_dp - 1, near)
+        tx[2].start()
+        for c in second_copies:
             c.wait_recv()
         part[2] = part[1] + cols[n_dp - 1] + cols[n_dp] + cols[n_dp + 1]
         col_lse = 0.0
@@ -1217,13 +1227,15 @@
         lax.fori_loop(0, rows // step, first_back, 0)
         for k in (1, 2, 3):
             pk[k, 0:6] = pk[0, 0:6]
-        for c in small + ig[:2]:
+        for c in small + ig[:3]:
             c.start()
         put(igv.at[0], ig_out.at[row_block(0)])
 
     def pass_on():
         ig[1].wait()
-        ig[2].start()
+        ig[3].start()
+        ig[2].wait()
+        ig[4].start()
         put(igv.at[2], ig_out.at[row_block(2)])
         ig[0].wait()
         put(igv.at[1], ig_out.at[row_block(1)])
@@ -1314,7 +1326,9 @@
         "fb": leave,
         "ig": pass_on,
     }
-    sums = {"u0": sum_u[0].steps(), "u1": sum_u[1].steps(), "o": sum_o.steps(), "d": sum_d.steps(True)}
+    sums = {"o": sum_o.steps(), "d": sum_d.steps(True)}
+    for i in range(U_PARTS):
+        sums["u%d" % i] = sum_u[i].steps()
     for n in range(3):
         sums["q%d" % n] = sum_q[n].steps()
     sums["s"] = small_steps()
@@ -1329,7 +1343,8 @@
         live = [g for g in live if next(g, live) is not live]
     put(result, g_out)
 
-    ig[2].wait()
+    ig[3].wait()
+    ig[4].wait()
     put(igv.at[3], ig_out.at[row_block(3)])
     for c in col_copies:
         c.wait_send()
@@ -1362,7 +1377,7 @@
     vmem = pl.BlockSpec(memory_space=pltpu.VMEM)
     vm = lambda s: pltpu.VMEM(s.shape, s.dtype)
     sem = lambda n: pltpu.SemaphoreType.DMA((n,))
-    n_sum = 7 * (3 + 2 * n_pow)
+    n_sum = (5 + U_PARTS) * (3 + 2 * n_pow)
     return pl.pallas_call(
         functools.partial(back_kernel, n_dp, n_mp, rows),
         out_shape=outs,
@@ -1399,7 +1414,7 @@
             pltpu.VMEM((4, 16, D), F32),
             pltpu.VMEM((3, 16, D), F32),
             pltpu.VMEM((2 * n_pow + 1, 16, D), F32),
-            sem(n_sum), sem(n_sum), sem(3), sem(3), sem(3), sem(3), sem(4), sem(4),
+            sem(n_sum), sem(n_sum), sem(5), sem(5), sem(5), sem(5), sem(4), sem(4),
             sem(3), sem(3), sem(3 + n_pow), sem(3 + n_pow), sem(n_col), sem(n_col), sem(26), sem(10),
         ],
         compiler_params=pltpu.CompilerParams(
@@ -1434,10 +1449,10 @@
     ]
     q_at = (u_rows + o_rows) // step
     order = [q_at + n for n in range(3)] + [i for i in range(count) if not q_at <= i < q_at + 3]
+    for c in big:
+        c.start()
     for i in order:
         first[i].start()
-    for c in big:
-        c.start()
     outs = []
 
     def put(src, dst):
@@ -1455,10 +1470,10 @@
         put(total.at[i], dst)
     total[16:24, :128] = loss_ref[...].T[0:8]
     put(total.at[16, pl.ds(0, 128)], loss_out)
-    for n, i in enumerate(order):
-        if n >= count - len(big):
-            big[n - count + len(big)].wait()
-            away[n - count + len(big)].start()
+    for a, b in zip(big, away):
+        a.wait()
+        b.start()
+    for i in order:
         first[i].wait()
         r = slice(i * step, (i + 1) * step)
         v = low[r].astype(F32)

time: 202 us -> 194 us (0.960)
  Pallas kernels: 200 us -> 192 us
    pallas_call x1, Pallas kernels: 125 us -> 117 us  [run_backward(): pl.pallas_call(functools.partial(back_kernel, n_dp, n_mp, rows), out_shap...]
where the time goes in v4:
time: 194 us
  Pallas kernels  192 us (99%)
    pallas_call x1, Pallas kernels, run_backward(): pl.pallas_call(functools.partial(back_kernel, n_dp, n_mp, rows), out_shap...  117 us
    pallas_call x1, Pallas kernels, run_forward(): pl.pallas_call(functools.partial(fwd_kernel, n_dp, rows), out_shape=outs,...  64.6 us
    pallas_call x1, Pallas kernels, run_finish(): pl.pallas_call(functools.partial(finish_kernel, q_rows, o_rows, u_rows, 2...  9.54 us

profile of v4, /device:TPU:0, one launch (start us, length us, event | category | flops | bytes accessed | tf_op | source)
XLA Modules:
  0.0 193.8 jit_solution(16801238478164451171)
XLA Ops:
  0.6 1.4 copy.32.shard_hbm
  2.0 64.6 %forward.1 = (bf16[2,3,2,192,768]{4,3,2,1,0:T(8,128)(2,1)}, bf16[2,2,192,768]{3,2,1,0:T(8,128)(2,1)}, bf16[4,768,768]{2,1,0:T(8,128)(2,1)}, bf16[4,768,768]{2,1,...) custom-call(bf16[2048,768]{1,0:T(8,128)(2,1)} %x_hbm.3, ...), custom_call_target="tpu_custom_call" | custom-call | tf_op jit(solution)/shard_map/forward/pallas_call | solution.py:642
  66.6 117.4 %backward.1 = (bf16[2048,768]{1,0:T(8,128)(2,1)}, bf16[2048,768]{1,0:T(8,128)(2,1)}, bf16[2304,768]{1,0:T(8,128)(2,1)}, f32[16,768]{1,0:T(8,128)}, f32[128,128]{1,0:T(8,128)}) custom-call(bf16[2048,768]{1,0:T(8,128)(2,1)} %x_hbm.3, bf16[2,3,2,192,768]{4,3,2,1,0:T(8,128)(2,1)} %get-tuple-element.48.wq_hbm, bf16[2,2,192,768]{3,2,1,0:T(8,128)(2,1)} %get-tuple-element.49.wo_hbm, ...), custom_call_target="tpu_custom_call" | custom-call | tf_op jit(solution)/shard_map/backward/pallas_call | solution.py:1381
  184.1 9.5 %outputs.1 = (bf16[2048,768]{1,0:T(8,128)(2,1)}, bf16[2048,768]{1,0:T(8,128)(2,1)}, f32[128]{0:T(128)}, f32[3,192,768]{2,1,0:T(8,128)}, f32[2,192]{1,0:T(2,128)}...) custom-call(bf16[2304,768]{1,0:T(8,128)(2,1)} %get-tuple-element.61., ...), custom_call_target="tpu_custom_call" | custom-call | tf_op jit(solution)/shard_map/outputs/pallas_call | solution.py:1504

commit v5 on v4

--- a/solution.py
+++ b/solution.py
@@ -107,7 +107,7 @@
     img_hbm, group_hbm, shard_hbm, row_hbm,
     wq_out, wo_out, wu_out, wd_out, imgs_out, low_out, temp_out, qkv_out, mix_out, hid_out, gp_out, s_out, text_out,
     pool_out,
-    xv, wq, wo, wu, wd, bi, qv, vec_ref, ints, shard, info, stage, hot, unit, temp, total_rows, n1, qkv, mix, hid, n2, gp, act,
+    xv, wq, wo, wu, wd, bi, qv, vec_ref, ints, info, stage, hot, unit, temp, total_rows, n1, qkv, mix, hid, n2, gp, act,
     acc, sv, pool,
     w_ss, w_rs, b_ss, b_rs, i_ss, i_rs, l_sem, p_sem, o_sem, u_sem,
 ):
@@ -141,7 +141,7 @@
     ]
     n_img = img_hbm.shape[0]
     parts = n_img // 128
-    lines = [(ub_hbm, bi.at[0, 0]), (qv_hbm, qv), (row_hbm, ints.at[0]), (shard_hbm, shard)]
+    lines = [(ub_hbm, bi.at[0, 0]), (qv_hbm, qv), (row_hbm, ints.at[0]), (shard_hbm, ints.at[1 + parts])]
     lines += [(group_hbm.at[pl.ds(i * 128, 128)], ints.at[1 + i]) for i in range(parts)]
     early = len(lines)
     lines += [(v, vec_ref.at[i]) for i, v in enumerate((g1_hbm, s1_hbm, ob_hbm, g2_hbm, s2_hbm, db_hbm))]
@@ -188,7 +188,7 @@
         (q_rows, 2, src_q, at_q),
         (o_rows, 1, src_o, at_o),
         (u_rows, 2, src_u, at_u),
-        (d_rows, 4, src_d, at_d),
+        (d_rows, 8, src_d, at_d),
     ):
         whole = pl.ds(0, total)
         pieces = []
@@ -225,8 +225,7 @@
     turned = pltpu.roll(wide, q_rows, 1)
     bi[0, 1:2, :width], bi[0, 2:3, :width] = wide[0:1], turned[0:1]
     bi[0, 3:4, :width], bi[0, 4:5, :width] = wide[1:2], turned[1:2]
-    tall = jnp.broadcast_to(shard[...], (128, 128)).T
-    info[0, 0:1] = tall[0:1] * n_img + ints[0:1]
+    info[0, 0:1] = ints[1 + parts : 2 + parts] * n_img + ints[0:1]
     info[0, 1 : 1 + parts] = ints[1 : 1 + parts]
 
     bias = [
@@ -479,6 +478,7 @@
         return pltpu.make_async_copy(imgs.at[pl.ds(block * near, near)], stage, u_sem.at[0])
 
     n_block = n_dp // near
+    shared_pick = relay
 
     def pick_four(q):
         def from_block(block):
@@ -513,11 +513,15 @@
         slot = q % unit.shape[0]
         inv = lax.rsqrt(jnp.sum(raw * raw, axis=-1, keepdims=True) + 1e-06)
         unit[slot] = (raw * inv).astype(BF16)
+        for i in range(4):
+            temp[4 * q + i] = jnp.where(temp[4 * q + i] > 0.5, 64.0, 40.0)
+
+    def store_four(q):
+        slot = q % unit.shape[0]
         copies = []
         for i in range(4):
             r = 4 * q + i
             at = pl.ds(pl.multiple_of(both(dp, r, n_dp) * 128, 128), 128)
-            temp[r] = jnp.where(temp[r] > 0.5, 64.0, 40.0)
             copies.append(
                 pltpu.make_async_copy(unit.at[slot, pl.ds(i * 128, 128)], low_out.at[at], u_sem.at[2 * r + 1])
             )
@@ -528,7 +532,8 @@
 
     def pick_many():
         def each(q, carry):
-            for c in pick_four(q):
+            pick_four(q)
+            for c in store_four(q):
                 c.wait()
             return carry
 
@@ -539,37 +544,56 @@
         image_outward(1)
     local[3].wait()
     up(0)
-    forward_x(3, 0)
-    forward_x(3, 1)
+    for part in range(4):
+        forward_x(3, part)
     step_core[2].wait_recv()
     up(1)
     forward_y(2, 1)
-    forward_x(3, 2)
+    forward_x(3, 4)
+    forward_x(3, 5)
     local[4].wait()
     down(0)
     arrived(2)
     up(2)
-    forward_x(3, 3)
+    forward_x(3, 6)
+    forward_x(3, 7)
     image_last()
     forward_y(3, 0)
+    forward_y(3, 1)
     up(3)
     put(wu, wu_out)
     put(gp, gp_out)
     put(sv, s_out)
-    forward_y(3, 1)
+    forward_y(3, 2)
+    forward_y(3, 3)
     step_core[3].wait_recv()
     down(1)
-    forward_y(3, 2)
+    forward_y(3, 4)
+    forward_y(3, 5)
     img_copies[-1][0].wait_recv()
-    if n_block == 1:
-        rests.extend(pick_four(0))
-        forward_y(3, 3)
-        for q in range(1, n_dp // 4):
-            rests.extend(pick_four(q))
+    picked = []
+    if shared_pick:
+        half_of = lax.rem(mp, 2)
+        pick_four(half_of)
+        four = pl.ds(4 * half_of, 4)
+        picked.append(remote(unit.at[half_of], unit.at[half_of], i_ss.at[13], i_rs.at[13], core))
+        picked.append(remote(temp.at[four], temp.at[four], i_ss.at[14], i_rs.at[14], core))
+        for c in picked:
+            c.start()
+        rests.extend(store_four(half_of))
+    elif n_block > 1:
+        pick_many()
     else:
-        forward_y(3, 3)
-        pick_many()
+        for q in range(n_dp // 4):
+            pick_four(q)
+            rests.extend(store_four(q))
+    forward_y(3, 6)
+    forward_y(3, 7)
     down(2)
+    if shared_pick:
+        for c in picked:
+            c.wait_recv()
+        rests.extend(store_four(1 - half_of))
     arrived(3)
     put(wd, wd_out)
     down(3)
@@ -602,6 +626,8 @@
                 for c in pair:
                     c.wait_send()
 
+    for c in picked:
+        c.wait_send()
     for c in rests:
         c.wait()
     for c in outs:
@@ -638,7 +664,7 @@
     ]
     any_spec = pl.BlockSpec(memory_space=pl.ANY)
     vm = lambda s: pltpu.VMEM(s.shape, s.dtype)
-    n_img_sem = 13 if n_dp == 8 else 2 * len(powers(n_dp)) + 1
+    n_img_sem = 15 if n_dp == 8 else 2 * len(powers(n_dp)) + 1
     return pl.pallas_call(
         functools.partial(fwd_kernel, n_dp, rows),
         out_shape=outs,
@@ -651,7 +677,6 @@
             pltpu.VMEM(args[6].shape, F32),
             pltpu.VMEM((8, D), F32),
             pltpu.VMEM((8, 128), jnp.int32),
-            pltpu.VMEM((per_dp, 1), jnp.int32),
             pltpu.VMEM((n_dp, 8, 128), jnp.int32),
             pltpu.VMEM((near,) + images.shape, BF16),
             pltpu.VMEM((512, near * n_img), BF16),
@@ -668,8 +693,8 @@
             pltpu.VMEM((rows, D), F32),
             pltpu.VMEM((4, caps, D), BF16),
             pltpu.VMEM((caps, D), F32),
-            pltpu.SemaphoreType.DMA((40,)),
-            pltpu.SemaphoreType.DMA((40,)),
+            pltpu.SemaphoreType.DMA((56,)),
+            pltpu.SemaphoreType.DMA((56,)),
             pltpu.SemaphoreType.DMA((3,)),
             pltpu.SemaphoreType.DMA((3,)),
             pltpu.SemaphoreType.DMA((n_img_sem,)),
@@ -1536,7 +1561,7 @@
             rows,
             (
                 tokens, wq_t, w_out, w_up, w_down, up_bias, qv_bias, ln1_gain, ln1_bias, out_bias, ln2_gain,
-                ln2_bias, down_bias, images, image_group, pair_shard, pair_row,
+                ln2_bias, down_bias, images, image_group, pair_shard.reshape(-1), pair_row,
             ),
         )
         text_rows, ig, grads, small, loss = run_backward(

time: 194 us -> 191 us (0.985)
  Pallas kernels: 192 us -> 190 us
    pallas_call x1, Pallas kernels: 64.6 us -> 61.5 us  [run_forward(): pl.pallas_call(functools.partial(fwd_kernel, n_dp, rows), out_shape=outs,...]
where the time goes in v5:
time: 191 us
  Pallas kernels  190 us (99%)
    pallas_call x1, Pallas kernels, run_backward(): pl.pallas_call(functools.partial(back_kernel, n_dp, n_mp, rows), out_shap...  119 us
    pallas_call x1, Pallas kernels, run_forward(): pl.pallas_call(functools.partial(fwd_kernel, n_dp, rows), out_shape=outs,...  61.5 us
    pallas_call x1, Pallas kernels, run_finish(): pl.pallas_call(functools.partial(finish_kernel, q_rows, o_rows, u_rows, 2...  9.54 us

profile of v5, /device:TPU:0, one launch (start us, length us, event | category | flops | bytes accessed | tf_op | source)
XLA Modules:
  0.0 190.9 jit_solution(4326175911960962481)
XLA Ops:
  0.7 61.5 %forward.1 = (bf16[2,3,2,192,768]{4,3,2,1,0:T(8,128)(2,1)}, bf16[2,2,192,768]{3,2,1,0:T(8,128)(2,1)}, bf16[4,768,768]{2,1,0:T(8,128)(2,1)}, bf16[4,768,768]{2,1,...) custom-call(bf16[2048,768]{1,0:T(8,128)(2,1)} %x_hbm.3, ...), custom_call_target="tpu_custom_call" | custom-call | tf_op jit(solution)/shard_map/forward/pallas_call | solution.py:668
  62.2 119.0 %backward.1 = (bf16[2048,768]{1,0:T(8,128)(2,1)}, bf16[2048,768]{1,0:T(8,128)(2,1)}, bf16[2304,768]{1,0:T(8,128)(2,1)}, f32[16,768]{1,0:T(8,128)}, f32[128,128]{1,0:T(8,128)}) custom-call(bf16[2048,768]{1,0:T(8,128)(2,1)} %x_hbm.3, bf16[2,3,2,192,768]{4,3,2,1,0:T(8,128)(2,1)} %get-tuple-element.48.wq_hbm, bf16[2,2,192,768]{3,2,1,0:T(8,128)(2,1)} %get-tuple-element.49.wo_hbm, ...), custom_call_target="tpu_custom_call" | custom-call | tf_op jit(solution)/shard_map/backward/pallas_call | solution.py:1406
  181.2 9.5 %outputs.1 = (bf16[2048,768]{1,0:T(8,128)(2,1)}, bf16[2048,768]{1,0:T(8,128)(2,1)}, f32[128]{0:T(128)}, f32[3,192,768]{2,1,0:T(8,128)}, f32[2,192]{1,0:T(2,128)}...) custom-call(bf16[2304,768]{1,0:T(8,128)(2,1)} %get-tuple-element.61., ...), custom_call_target="tpu_custom_call" | custom-call | tf_op jit(solution)/shard_map/outputs/pallas_call | solution.py:1529

commit v6 on v5

--- a/solution.py
+++ b/solution.py
@@ -881,8 +881,8 @@
 
     total = low_hbm.shape[0]
     block = image.shape[0]
+    load("image", low_hbm.at[pl.ds(0, block)], image)
     load("text", text_hbm, text.at[0])
-    load("image", low_hbm.at[pl.ds(0, block)], image)
     for i, v in enumerate((g1_hbm, s1_hbm, g2_hbm, s2_hbm)):
         load(("vec", i), v, vec_ref.at[i])
     load("hid", hid_hbm, hid)
@@ -958,6 +958,7 @@
     for s in (3, 2, 1, 0):
         load(("wd", s), wd_hbm.at[s], wd.at[s])
         load(("gp", s), gp_hbm.at[s], gp.at[s])
+    for s in (3, 2, 1, 0):
         load(("wu", s), wu_hbm.at[s], wu.at[s])
     load("mix", mix_hbm, mix)
     load("wo", wo_hbm, wo)

time: 191 us -> 191 us (level)
  no operation moved by 1% of the time
where the time goes in v6:
time: 191 us
  Pallas kernels  190 us (99%)
    pallas_call x1, Pallas kernels, run_backward(): pl.pallas_call(functools.partial(back_kernel, n_dp, n_mp, rows), out_shap...  119 us
    pallas_call x1, Pallas kernels, run_forward(): pl.pallas_call(functools.partial(fwd_kernel, n_dp, rows), out_shape=outs,...  61.5 us
    pallas_call x1, Pallas kernels, run_finish(): pl.pallas_call(functools.partial(finish_kernel, q_rows, o_rows, u_rows, 2...  9.54 us

profile of v6, /device:TPU:0, one launch (start us, length us, event | category | flops | bytes accessed | tf_op | source)
XLA Modules:
  0.0 190.9 jit_solution(14692020386132842274)
XLA Ops:
  0.7 61.5 %forward.1 = (bf16[2,3,2,192,768]{4,3,2,1,0:T(8,128)(2,1)}, bf16[2,2,192,768]{3,2,1,0:T(8,128)(2,1)}, bf16[4,768,768]{2,1,0:T(8,128)(2,1)}, bf16[4,768,768]{2,1,...) custom-call(bf16[2048,768]{1,0:T(8,128)(2,1)} %x_hbm.3, ...), custom_call_target="tpu_custom_call" | custom-call | tf_op jit(solution)/shard_map/forward/pallas_call | solution.py:668
  62.2 119.0 %backward.1 = (bf16[2048,768]{1,0:T(8,128)(2,1)}, bf16[2048,768]{1,0:T(8,128)(2,1)}, bf16[2304,768]{1,0:T(8,128)(2,1)}, f32[16,768]{1,0:T(8,128)}, f32[128,128]{1,0:T(8,128)}) custom-call(bf16[2048,768]{1,0:T(8,128)(2,1)} %x_hbm.3, bf16[2,3,2,192,768]{4,3,2,1,0:T(8,128)(2,1)} %get-tuple-element.48.wq_hbm, bf16[2,2,192,768]{3,2,1,0:T(8,128)(2,1)} %get-tuple-element.49.wo_hbm, ...), custom_call_target="tpu_custom_call" | custom-call | tf_op jit(solution)/shard_map/backward/pallas_call | solution.py:1407
  181.2 9.5 %outputs.1 = (bf16[2048,768]{1,0:T(8,128)(2,1)}, bf16[2048,768]{1,0:T(8,128)(2,1)}, f32[128]{0:T(128)}, f32[3,192,768]{2,1,0:T(8,128)}, f32[2,192]{1,0:T(2,128)}...) custom-call(bf16[2304,768]{1,0:T(8,128)(2,1)} %get-tuple-element.61., ...), custom_call_target="tpu_custom_call" | custom-call | tf_op jit(solution)/shard_map/outputs/pallas_call | solution.py:1530
